TPU v7x, 512 devices: a whole 4x8x8 slice. The times are simulated.
512 devices in a mesh: grp: 4 (over z_hi, core), gx: 32 (over x, y), gy: 4 (over z_lo).
Axes of the slice: x: 4, y: 8, z: 8 (z_hi: 2, z_lo: 4; z = z_hi * 4 + z_lo), core: 2. Of those that a mesh axis runs over, the one named last changes fastest.
Arguments:
- slot_field: float32 [4, 2, 1536, 512], P('grp', None, 'gx', 'gy'), may hold values from -6 to 6
- solid: int32 [2, 1536, 512], P(None, 'gx', 'gy'), may hold values 0 or 1
- lift_weight: bfloat16 [3, 64], replicated, may hold values from -3.5 to 3.5
- spectral_weight: bfloat16 [2048, 128], replicated, may hold values from -1.5 to 1.5
- mix_weight: bfloat16 [64, 64], replicated, may hold values from -0.75 to 0.75
- project_weight: bfloat16 [64, 3], replicated, may hold values from -0.75 to 0.75
- mode_index: int32 [32], replicated, may hold values from 0 to 47, as said below
Outputs:
- new_velocity: float32 [3, 2, 1536, 512], P(None, None, 'gx', 'gy')
- spectral_grad: float32 [2048, 128], P(('grp', 'gx', 'gy'))
- mix_grad: float32 [64, 64], replicated
Inputs may be any that keep to these rules, and one draw needn't show every extreme that they name: `mode_index`: 32 distinct values in ascending order; 0 and 47 are always among them.
All inputs are finite; a program needn't handle non-finite values. No bound on the sum of `solid` on one device may be relied on, other than what follows from the above.
Results may differ from a plain program's by a relative error of at most 0.0013.
Values may be sent and summed in bfloat16 or wider, within the bound.
No kernel may reach another device: no remote copies, remote signals or barrier semaphores. Data moves between devices by JAX's collectives and lax.ppermute only.
A program may use at most 64 MiB of HBM per device.

v0:
```python
import math

import jax
import jax.numpy as jnp
from jax import lax
from jax.sharding import PartitionSpec as P

VISCOSITY = 0.05
TIME_STEP = 0.1


def with_halo(block, sides, width):
    for axis, dim in sides:
        count = lax.axis_size(axis)
        forward = [(i, i + 1) for i in range(count - 1)]
        backward = [(target, source) for source, target in forward]
        low = lax.ppermute(
            lax.slice_in_dim(block, block.shape[dim] - width, None, axis=dim), axis, forward
        )
        high = lax.ppermute(lax.slice_in_dim(block, 0, width, axis=dim), axis, backward)
        block = jnp.concatenate([low, block, high], axis=dim)
    return block


def interior(source):
    return source[1:-1, 1:-1, 1:-1]


def along_x(source):
    return 0.5 * (source[1:-1, 2:, 1:-1] - source[1:-1, :-2, 1:-1])


def along_y(source):
    return 0.5 * (source[1:-1, 1:-1, 2:] - source[1:-1, 1:-1, :-2])


def along_z(source):
    return 0.5 * (source[2:, 1:-1, 1:-1] - source[:-2, 1:-1, 1:-1])


def laplace(source):
    total = source[2:, 1:-1, 1:-1] + source[:-2, 1:-1, 1:-1]
    total = total + source[1:-1, 2:, 1:-1] + source[1:-1, :-2, 1:-1]
    total = total + source[1:-1, 1:-1, 2:] + source[1:-1, 1:-1, :-2]
    return total - 6.0 * interior(source)


def section_component(padded, component, solid):
    source = padded[component]
    velocity = [interior(padded[index]) for index in range(3)]
    advect = (
        velocity[0] * along_x(source)
        + velocity[1] * along_y(source)
        + velocity[2] * along_z(source)
    )
    pressure = padded[3]
    press_grad = jnp.stack([along_x(pressure), along_y(pressure), along_z(pressure)])[component]
    update = interior(source) + TIME_STEP * (VISCOSITY * laplace(source) - advect - press_grad)
    return update * (1.0 - solid.astype(jnp.float32))


def spectral_table(mode_index, x_length):
    places = jnp.arange(x_length, dtype=jnp.int32)
    phases = mode_index[:, None] * places[None, :] % x_length
    angles = 2.0 * jnp.pi / x_length * phases.astype(jnp.float32)
    return jnp.concatenate([jnp.cos(angles), -jnp.sin(angles)], axis=0).astype(jnp.bfloat16)


def contract(form, left, right):
    return jnp.einsum(form, left, right, preferred_element_type=jnp.float32)


def student_terms(
    line_data,
    dft_table,
    lift_weight,
    spectral_weight,
    mix_weight,
    project_weight,
    loss_scale,
    x_length,
):
    mode_count = dft_table.shape[0] // 2
    chan_count = mix_weight.shape[0]
    scale_dft = 1.0 / math.sqrt(x_length)
    old_part = line_data[:3]
    target = line_data[3:].astype(jnp.float32)
    lifted = contract("iln,ic->cln", old_part, lift_weight).astype(jnp.bfloat16)
    coeffs = (contract("cln,mn->clm", lifted, dft_table) * scale_dft).astype(jnp.bfloat16)
    real_in = coeffs[..., :mode_count]
    imag_in = coeffs[..., mode_count:]
    weights = spectral_weight.reshape(mode_count, chan_count, 2 * chan_count)
    real_w = weights[..., :chan_count]
    imag_w = weights[..., chan_count:]
    real_out = contract("clm,mco->olm", real_in, real_w) - contract("clm,mco->olm", imag_in, imag_w)
    imag_out = contract("clm,mco->olm", real_in, imag_w) + contract("clm,mco->olm", imag_in, real_w)
    mixed = jnp.concatenate([real_out, imag_out], axis=2).astype(jnp.bfloat16)
    spectral = contract("olm,mn->oln", mixed, dft_table) * (2.0 * scale_dft)
    local_term = contract("cln,co->oln", lifted, mix_weight)
    hidden = spectral + local_term
    active, gelu_back = jax.vjp(jax.nn.gelu, hidden)
    active = active.astype(jnp.bfloat16)
    predicted = contract("oln,oi->iln", active, project_weight)
    misfit = (predicted - target) * loss_scale
    back_active = jnp.einsum(
        "iln,oi->oln", misfit, project_weight.astype(jnp.float32), precision=lax.Precision.HIGHEST
    )
    back_hidden = gelu_back(back_active)[0].astype(jnp.bfloat16)
    mix_part = contract("cln,oln->co", lifted, back_hidden)
    back_mixed = (contract("oln,mn->olm", back_hidden, dft_table) * (2.0 * scale_dft)).astype(
        jnp.bfloat16
    )
    back_real = back_mixed[..., :mode_count]
    back_imag = back_mixed[..., mode_count:]
    grad_real = contract("clm,olm->mco", real_in, back_real) + contract(
        "clm,olm->mco", imag_in, back_imag
    )
    grad_imag = contract("clm,olm->mco", real_in, back_imag) - contract(
        "clm,olm->mco", imag_in, back_real
    )
    spectral_part = jnp.concatenate([grad_real, grad_imag], axis=2).reshape(
        mode_count * chan_count, 2 * chan_count
    )
    return (spectral_part, mix_part)


def local(slot_field, solid, lift_weight, spectral_weight, mix_weight, project_weight, mode_index):
    role_index = lax.axis_index("grp")
    own_tile = slot_field[0]
    planes, x_rows, y_cols = own_tile.shape
    x_length = x_rows * lax.axis_size("gx")
    cell_total = x_length * y_cols * lax.axis_size("gy") * planes
    loss_scale = 16.0 / math.sqrt(cell_total)
    dft_table = spectral_table(mode_index, x_length)
    rimmed = with_halo(own_tile, (("gx", 1), ("gy", 2)), 1)
    gathered = lax.all_gather(rimmed[None], "grp", axis=0, tiled=True)
    padded = jnp.pad(gathered, ((0, 0), (1, 1), (0, 0), (0, 0)))
    old_velocity = gathered[:3, :, 1:-1, 1:-1]
    new_tile = lax.cond(
        role_index < 3,
        lambda: section_component(padded, jnp.minimum(role_index, 2), solid),
        lambda: own_tile,
    )
    new_slots = lax.all_gather(new_tile[None], "grp", axis=0, tiled=True)
    new_velocity = new_slots[:3]
    both_fields = jnp.concatenate([old_velocity, new_velocity], axis=0).astype(jnp.bfloat16)
    pencil_data = lax.all_to_all(
        jnp.transpose(both_fields, (0, 1, 3, 2)), "gx", split_axis=2, concat_axis=3, tiled=True
    )
    line_data = pencil_data.reshape(6, -1, x_length)

    def student(own_lines):
        return student_terms(
            own_lines,
            dft_table,
            lift_weight,
            spectral_weight,
            mix_weight,
            project_weight,
            loss_scale,
            x_length,
        )

    def nothing():
        return (
            jnp.zeros(spectral_weight.shape, jnp.float32),
            jnp.zeros(mix_weight.shape, jnp.float32),
        )

    spectral_part, mix_part = lax.cond(role_index == 3, lambda: student(line_data), nothing)
    spectral_grad = lax.psum_scatter(
        spectral_part, ("grp", "gx", "gy"), scatter_dimension=0, tiled=True
    )
    mix_grad = lax.psum(mix_part, ("grp", "gx", "gy"))
    return (new_velocity, spectral_grad, mix_grad)


def solution(mesh):
    in_specs = (P("grp", None, "gx", "gy"), P(None, "gx", "gy"), P(), P(), P(), P(), P())
    out_specs = (P(None, None, "gx", "gy"), P(("grp", "gx", "gy"), None), P())
    return jax.shard_map(local, mesh=mesh, in_specs=in_specs, out_specs=out_specs, check_vma=False)
```

profile of v0, /device:TPU:1, one launch (start us, length us, event | category | flops | bytes accessed | tf_op | source)
XLA Modules:
  0.0 370.9 jit_solution(1954952146609632961)
XLA Ops:
  7.2 0.8 copy.109
  8.0 4.0 %collective-permute-start = (f32[2,1,128]{2,1,0:T(1,128)S(1)}, f32[2,1,128]{2,1,0:T(1,128)S(1)}, u32[]{:S(2)}, u32[]{:S(2)}) collective-permute-start(f32[2,1,128]{2,1,0:T(1,128)S(1)} %get-tuple-element.99), channel_id=1, source_target_pairs={{0,4},{4,8},{8,12},{12,16},{16,20},{20,24},{24,28},{28,32},{32,36}... | collective-permute-start | bytes 3080 | tf_op jit(solution)/shard_map/ppermute | solution.py:17
  12.0 1.3 collective-permute-start.1
  13.3 0.0 collective-permute-done
  13.3 3.0 collective-permute-done.1
  16.3 0.1 fusion.79
  16.4 4.0 %collective-permute-start.2 = (f32[2,50,1]{2,1,0:T(8,128)S(1)}, f32[2,50,1]{2,1,0:T(8,128)S(1)}, u32[]{:S(2)}, u32[]{:S(2)}) collective-permute-start(f32[2,50,1]{2,1,0:T(8,128)S(1)} %get-tuple-element.97), channel_id=1, source_target_pairs={{0,1},{1,2},{2,3},{4,5},{5,6},{6,7},{8,9},{9,10},{10,11},{12,13},{... | collective-permute-start | bytes 1208 | tf_op jit(solution)/shard_map/ppermute | solution.py:17
  20.4 1.3 collective-permute-start.3
  21.7 0.0 collective-permute-done.2
  21.7 4.2 %collective-permute-done.3 = f32[2,50,1]{2,1,0:T(8,128)S(1)} collective-permute-done((f32[2,50,1]{2,1,0:T(8,128)S(1)}, f32[2,50,1]{2,1,0:T(8,128)S(1)}, u32[]{:S(2)}, u32[]{:S(2)}) %collective-permute-start.3) | collective-permute-done | bytes 432 | tf_op jit(solution)/shard_map/ppermute | solution.py:20
  26.0 0.1 pad_maximum_fusion.4
  26.1 16.3 %all-gather = f32[8,50,130]{2,1,0:T(8,128)S(1)} all-gather(f32[2,50,130]{2,1,0:T(8,128)S(1)} %pad_maximum_fusion.4), channel_id=2, replica_groups=mesh['grp'=4,'gx'=32,'gy'=4] {'grp'}, dimensions={0}, use_global_device_ids=true | all-gather | bytes 260000 | tf_op jit(solution)/shard_map/all_gather | solution.py:136
  42.4 0.0 copy-start.6
  42.4 0.1 slice.233
  42.5 1.3 conditional.2
  42.5 0.1 fusion
  42.6 0.1 fusion.13
  42.7 1.0 fusion.11
  43.7 0.0 copy-start
  43.7 0.0 copy-start.3
  43.8 0.0 copy-start.4
  43.8 0.0 copy-start.5
  43.8 9.6 %all-gather.1 = f32[8,48,128]{2,1,0:T(8,128)S(1)} all-gather(f32[2,48,128]{2,1,0:T(8,128)S(1)} %get-tuple-element.107), channel_id=3, replica_groups=mesh['grp'=4,'gx'=32,'gy'=4] {'grp'}, dimensions={0}, use_global_device_ids=true | all-gather | bytes 245760 | tf_op jit(solution)/shard_map/all_gather | solution.py:144
  53.4 0.0 copy-start.2
  53.5 0.4 copy.68
  53.9 0.3 bitcast_bitcast_fusion
  54.2 1.2 reshape.29
  55.5 9.9 %all-to-all-start = ((bf16[32,2,1152]{2,1,0:T(2,128)(2,1)}), bf16[32,2,1152]{2,1,0:T(2,128)(2,1)S(1)}, u32[]{:S(2)}, u32[]{:S(2)}) async-start(bf16[32,2,1152]{2,1,0:T(2,128)(2,1)} %reshape.29), calls=%async_computation | async-start | bytes 294912 | tf_op jit(solution)/shard_map/all_to_all | solution.py:147
  65.3 0.0 all-reduce.4.cloned.1.call-start
  65.4 0.0 copy-done.6
  65.4 0.9 cosine_convert_fusion
  66.3 8.2 %all-to-all-done = bf16[32,2,1152]{2,1,0:T(2,128)(2,1)S(1)} async-done(((bf16[32,2,1152]{2,1,0:T(2,128)(2,1)}), bf16[32,2,1152]{2,1,0:T(2,128)(2,1)S(1)}, u32[]{:S(2)}, u32[]{:S(2)}) %all-to-all-start) | async-done | bytes 147488 | tf_op jit(solution)/shard_map/all_to_all | solution.py:147
  74.5 0.4 reshape.30
  74.9 0.1 copy.69
  75.0 0.0 copy-done
  75.0 0.0 copy-done.3
  75.0 0.0 copy-done.4
  75.0 0.0 copy-done.5
  75.0 0.0 copy-done.2
  75.0 0.3 conditional.3
  75.1 0.1 broadcast.48
  75.3 0.0 copy-start.1
  75.3 1.0 copy-done.1
  76.3 0.0 all-reduce.4.cloned.1.call-update
  76.3 115.8 %psum.7 = f32[64,64]{1,0:T(8,128)} all-reduce(f32[64,64]{1,0:T(8,128)S(1)} %get-tuple-element.46), channel_id=1, replica_groups=mesh['grp'=4,'gx'=32,'gy'=4] {'grp','gx','gy'}, use_global_device_ids=true, to_apply=%region_5.6 | all-reduce | flops 4096 | bytes 32768 | tf_op jit(solution)/shard_map/psum | solution.py:174
  192.2 170.6 %all-reduce.4.cloned.1.call-done = f32[2048,128]{1,0:T(8,128)} async-done(((f32[2048,128]{1,0:T(8,128)}), f32[2048,128]{1,0:T(8,128)}) %all-reduce.4.cloned.1.call-update) | async-done | bytes 1048592
  362.8 1.2 constant_dynamic-slice_fusion
  (7 shorter events, 0.1 us)
Async XLA Ops:
  8.0 5.3 %collective-permute-start = (f32[2,1,128]{2,1,0:T(1,128)S(1)}, f32[2,1,128]{2,1,0:T(1,128)S(1)}, u32[]{:S(2)}, u32[]{:S(2)}) collective-permute-start(f32[2,1,128]{2,1,0:T(1,128)S(1)} %get-tuple-element.99), channel_id=1, source_target_pairs={{0,4},{4,8},{8,12},{12,16},{16,20},{20,24},{24,28},{28,32},{32,36}... | collective-permute-start | bytes 3080 | tf_op jit(solution)/shard_map/ppermute | solution.py:17
  12.0 4.3 %collective-permute-start.1 = (f32[2,1,128]{2,1,0:T(1,128)S(1)}, f32[2,1,128]{2,1,0:T(1,128)S(1)}, u32[]{:S(2)}, u32[]{:S(2)}) collective-permute-start(f32[2,1,128]{2,1,0:T(1,128)S(1)} %get-tuple-element.100), channel_id=1, source_target_pairs={{4,0},{8,4},{12,8},{16,12},{20,16},{24,20},{28,24},{32,28},{36,32}... | collective-permute-start | bytes 3080 | tf_op jit(solution)/shard_map/ppermute | solution.py:20
  16.4 5.3 %collective-permute-start.2 = (f32[2,50,1]{2,1,0:T(8,128)S(1)}, f32[2,50,1]{2,1,0:T(8,128)S(1)}, u32[]{:S(2)}, u32[]{:S(2)}) collective-permute-start(f32[2,50,1]{2,1,0:T(8,128)S(1)} %get-tuple-element.97), channel_id=1, source_target_pairs={{0,1},{1,2},{2,3},{4,5},{5,6},{6,7},{8,9},{9,10},{10,11},{12,13},{... | collective-permute-start | bytes 1208 | tf_op jit(solution)/shard_map/ppermute | solution.py:17
  20.4 5.6 %collective-permute-start.3 = (f32[2,50,1]{2,1,0:T(8,128)S(1)}, f32[2,50,1]{2,1,0:T(8,128)S(1)}, u32[]{:S(2)}, u32[]{:S(2)}) collective-permute-start(f32[2,50,1]{2,1,0:T(8,128)S(1)} %get-tuple-element.98), channel_id=1, source_target_pairs={{1,0},{2,1},{3,2},{5,4},{6,5},{7,6},{9,8},{10,9},{11,10},{13,12},{... | collective-permute-start | bytes 1208 | tf_op jit(solution)/shard_map/ppermute | solution.py:20
  42.4 23.0 %copy-start.6 = (s32[32]{0:T(128)S(1)}, s32[32]{0:T(128)}, u32[]{:S(2)}) copy-start(s32[32]{0:T(128)} %param.17) | copy-start | bytes 388
  43.7 31.3 %copy-start = (bf16[2048,128]{1,0:T(8,128)(2,1)S(1)}, bf16[2048,128]{1,0:T(8,128)(2,1)}, u32[]{:S(2)}) copy-start(bf16[2048,128]{1,0:T(8,128)(2,1)} %param.14) | copy-start | bytes 1572868
  43.7 31.2 %copy-start.3 = (bf16[64,64]{1,0:T(8,128)(2,1)S(1)}, bf16[64,64]{1,0:T(8,128)(2,1)}, u32[]{:S(2)}) copy-start(bf16[64,64]{1,0:T(8,128)(2,1)} %param.15) | copy-start | bytes 24580
  43.8 31.2 %copy-start.4 = (bf16[64,3]{0,1:T(4,128)(2,1)S(1)}, bf16[64,3]{0,1:T(4,128)(2,1)}, u32[]{:S(2)}) copy-start(bf16[64,3]{0,1:T(4,128)(2,1)} %param.16) | copy-start | bytes 1156
  43.8 31.2 %copy-start.5 = (bf16[3,64]{1,0:T(4,128)(2,1)S(1)}, bf16[3,64]{1,0:T(4,128)(2,1)}, u32[]{:S(2)}) copy-start(bf16[3,64]{1,0:T(4,128)(2,1)} %param.13) | copy-start | bytes 1156
  53.4 21.6 %copy-start.2 = (f32[6,48,128]{2,1,0:T(8,128)}, f32[6,48,128]{2,1,0:T(8,128)S(1)}, u32[]{:S(2)}) copy-start(f32[6,48,128]{2,1,0:T(8,128)S(1)} %slice.169) | copy-start | bytes 442372
  55.5 19.1 %all-to-all-start = ((bf16[32,2,1152]{2,1,0:T(2,128)(2,1)}), bf16[32,2,1152]{2,1,0:T(2,128)(2,1)S(1)}, u32[]{:S(2)}, u32[]{:S(2)}) async-start(bf16[32,2,1152]{2,1,0:T(2,128)(2,1)} %reshape.29), calls=%async_computation | async-start | bytes 294912 | tf_op jit(solution)/shard_map/all_to_all | solution.py:147
  65.3 297.5 %all-reduce.4.cloned.1.call-start = ((), (), s32[]{:S(2)}) async-start(), calls=%async_computation.1 | async-start | bytes 2097152
  75.3 1.0 copy-start.1
Sparse Core Ops, SparseCore 0:
  76.4 286.3 all-reduce.3
where the time goes:
time: 371 us
  waiting for transfers between devices  186 us (50%)
  blocking collectives  142 us (38%)
  starting transfers between devices  20.5 us (6%)
  between operations  14.3 us (4%)
  local copies, waits for them, and re-layouts  5.77 us (2%)
    unnamed x2, waiting for transfers between devices  171 us
    psum x1, blocking collectives, local(): mix_grad = lax.psum(mix_part, ('grp', 'gx', 'gy'))  116 us
    all_gather x1, blocking collectives, local(): gathered = lax.all_gather(rimmed[None], 'grp', axis=0, tiled=True)  16.3 us
    all_to_all x1, starting transfers between devices, local(): lax.all_to_all(jnp.transpose(both_fields, (0, 1, 3, 2)), 'gx', split_axis...  9.87 us
    all_gather x1, blocking collectives, local(): new_slots = lax.all_gather(new_tile[None], 'grp', axis=0, tiled=True)  9.64 us
    all_to_all x1, waiting for transfers between devices, local(): lax.all_to_all(jnp.transpose(both_fields, (0, 1, 3, 2)), 'gx', split_axis...  8.23 us
    ppermute x2, starting transfers between devices, with_halo(): lax.ppermute(lax.slice_in_dim(block, block.shape[dim] - width, None, axis...  8.01 us
  transfers between devices with their start and end apart: 6, of which 4 were waited for; matrix products, arithmetic and copies ran while one was open for 0% of the time, Pallas kernels for 0%

commit v1 on v0

v1 whole, which is shorter than its diff:
```python
import math

import jax
import jax.numpy as jnp
from jax import lax
from jax.experimental import pallas as pl
from jax.experimental.pallas import tpu as pltpu
from jax.sharding import PartitionSpec as P

VISCOSITY = 0.05
TIME_STEP = 0.1
F32 = jnp.float32
BF16 = jnp.bfloat16
GELU_A = math.sqrt(2.0 / math.pi)
GELU_B = 0.044715
VMEM = pl.BlockSpec(memory_space=pltpu.VMEM)
NT = (((1,), (1,)), ((), ()))
NN = (((1,), (0,)), ((), ()))
TN = (((0,), (0,)), ((), ()))


def dot(a, b, dims):
    return lax.dot_general(a, b, dims, preferred_element_type=F32)


def iota(shape, axis):
    return lax.broadcasted_iota(jnp.int32, shape, axis)


def call(kernel, out_shape, *args, scratch=()):
    count = len(out_shape) if isinstance(out_shape, (tuple, list)) else 1
    return pl.pallas_call(
        kernel,
        out_shape=out_shape,
        in_specs=[VMEM] * len(args),
        out_specs=[VMEM] * count if isinstance(out_shape, (tuple, list)) else VMEM,
        scratch_shapes=list(scratch),
        compiler_params=pltpu.CompilerParams(vmem_limit_bytes=40 * 1024 * 1024),
    )(*args)


def edge_kernel(tile_ref, up_ref, down_ref, right_ref, left_ref):
    rows, lanes = tile_ref.shape[1:]
    same = iota((rows, lanes), 0) == iota((rows, lanes), 1)
    for z in range(2):
        tile = tile_ref[z]
        up_ref[z : z + 1, :] = tile[rows - 1 : rows, :]
        down_ref[z : z + 1, :] = tile[0:1, :]
        for ref, lane in ((right_ref, lanes - 1), (left_ref, 0)):
            column = jnp.broadcast_to(tile[:, lane : lane + 1], (rows, lanes))
            ref[z : z + 1, :] = jnp.sum(jnp.where(same, column, 0.0), axis=0, keepdims=True)


def stencil_kernel(rows, fields_ref, solid_ref, new_ref, send_ref):
    lanes = fields_ref.shape[3]
    role = lax.axis_index("grp")
    row = iota((rows, lanes), 0)
    lane = iota((rows, lanes), 1)
    same = row == lane
    centre = [[fields_ref[f, z, 0:rows, :] for z in range(2)] for f in range(4)]

    def near(f, z):
        tile = centre[f][z]
        x_up = fields_ref[f, z, 1 : rows + 1, :]
        below = fields_ref[f, z, rows + 1 : rows + 2, :]
        x_down = jnp.where(row == 0, below, pltpu.roll(tile, 1, 0))
        rims = []
        for k in (2, 3):
            line = jnp.broadcast_to(fields_ref[f, z, rows + k : rows + k + 1, :], (rows, lanes))
            rims.append(jnp.sum(jnp.where(same, line, 0.0), axis=1, keepdims=True))
        y_down = jnp.where(lane == 0, rims[0], pltpu.roll(tile, 1, 1))
        y_up = jnp.where(lane == lanes - 1, rims[1], pltpu.roll(tile, lanes - 1, 1))
        return x_up, x_down, y_up, y_down

    values = []
    for z in range(2):
        fluid = 1.0 - solid_ref[z].astype(F32)
        velocity = [centre[f][z] for f in range(3)]
        sign = 0.5 if z == 0 else -0.5
        px_up, px_down, py_up, py_down = near(3, z)
        press = (0.5 * (px_up - px_down), 0.5 * (py_up - py_down), sign * centre[3][1 - z])
        new = []
        for f in range(3):
            x_up, x_down, y_up, y_down = near(f, z)
            other = centre[f][1 - z]
            advect = (
                velocity[0] * (0.5 * (x_up - x_down))
                + velocity[1] * (0.5 * (y_up - y_down))
                + velocity[2] * (sign * other)
            )
            lap = other + x_up + x_down + y_up + y_down - 6.0 * velocity[f]
            update = velocity[f] + TIME_STEP * (VISCOSITY * lap - advect - press[f])
            new.append(update * fluid)
            new_ref[f, z] = new[f]
        parts = [part.astype(BF16) for part in velocity + new]
        values.append(jnp.concatenate(parts, axis=1))
    pad = jnp.zeros((128 - 2 * rows, 6 * lanes), BF16)
    stacked = jnp.concatenate(values + [pad], axis=0)
    count = send_ref.shape[0]
    out_row = iota((count, 6 * lanes), 0)
    column = iota((count, 6 * lanes), 1)
    wanted = (out_row & 7) * lanes + (out_row >> 3) + role * (count // 8)
    pick = jnp.where(((out_row & 7) < 6) & (column == wanted), 1.0, 0.0).astype(BF16)
    send_ref[...] = dot(pick, stacked, NT).astype(BF16)


def line_kernel(
    scale_dft, loss_scale, recv_ref, table_ref, lift_ref, mix_ref, weight_ref, proj_ref, projt_ref,
    send_ref, back_ref, coef_ref,
):
    blocks = recv_ref.shape[0]
    cells = blocks * 128
    rows = 48
    lines = jnp.concatenate([recv_ref[b] for b in range(blocks)], axis=1)
    plane = iota((64, cells), 1) & 127
    table = table_ref[...]
    zero = jnp.zeros_like(table)
    first = jnp.where(plane < rows, table, zero)
    second = jnp.where((plane >= rows) & (plane < 2 * rows), table, zero)
    both = jnp.concatenate([first, second], axis=0)
    lifted = dot(lift_ref[...], lines, NN).astype(BF16)
    coeffs = dot(both, lifted, NT) * scale_dft
    coeffs16 = coeffs.astype(BF16)
    wide = jnp.concatenate([coeffs16] * 32, axis=1)
    mode_row = iota(wide.shape, 0) & 31
    mode_col = iota(wide.shape, 1) >> 6
    wide = jnp.where(mode_row == mode_col, wide, jnp.zeros_like(wide))
    product = dot(wide, weight_ref[...], NN)
    turned = pltpu.roll(product, 64, 1)
    parts = []
    for line in range(2):
        real = slice(64 * line, 64 * line + 32)
        imag = slice(64 * line + 32, 64 * line + 64)
        parts.append(product[real] - turned[imag])
        parts.append(turned[real] + product[imag])
    mixed = jnp.concatenate(parts, axis=0)
    mixed_t = jnp.transpose(mixed)[0:64].astype(BF16)
    hidden = dot(mixed_t, both, NN) * (2.0 * scale_dft) + dot(mix_ref[...], lifted, NN)
    square = hidden * hidden
    inner = GELU_A * (hidden + GELU_B * (square * hidden))
    tanh = jnp.tanh(inner)
    half = 0.5 * (1.0 + tanh)
    active = (hidden * half).astype(BF16)
    slope = half + (0.5 * GELU_A) * hidden * (1.0 - tanh * tanh) * (1.0 + (3.0 * GELU_B) * square)
    predicted = dot(projt_ref[...], active, NN)
    target = pltpu.roll(lines.astype(F32), 5, 0)
    misfit = (predicted - target) * loss_scale
    misfit = jnp.where(iota(misfit.shape, 0) < 3, misfit, 0.0)
    high = misfit.astype(BF16)
    low = (misfit - high.astype(F32)).astype(BF16)
    proj = proj_ref[...]
    back = slope * (dot(proj, high, NN) + dot(proj, low, NN))
    back16 = back.astype(BF16)
    mix_terms = dot(lines, back16, NT)
    back_mixed = dot(both, back16, NT) * (2.0 * scale_dft)
    back_ref[...] = jnp.concatenate([back_mixed[0:64], back_mixed[64:128]], axis=1)
    coef_ref[...] = jnp.concatenate([coeffs[0:64], coeffs[64:128]], axis=1)
    mix_high = mix_terms.astype(BF16)
    mix_low = (mix_terms - mix_high.astype(F32)).astype(BF16)
    tail = jnp.concatenate([mix_high, mix_low], axis=1)
    for j in range(8):
        chunk = jnp.concatenate(
            [
                back_ref[pl.ds(j, 8, stride=8), :],
                coef_ref[pl.ds(j, 8, stride=8), :],
                tail.astype(F32),
            ],
            axis=0,
        ).astype(BF16)
        for q in range(4):
            send_ref[4 * j + q] = chunk


def grad_kernel(recv_ref, send_ref, wide_ref, grad_ref):
    quarter = lax.rem(lax.axis_index("gx"), 4)
    blocks, height = recv_ref.shape[:2]
    for b in range(blocks):
        wide_ref[b * height : (b + 1) * height, :] = recv_ref[b].astype(F32)

    def rows(k):
        return wide_ref[pl.ds(k, blocks, stride=height), :]

    for g in range(4):
        back_re, back_im, coef_re, coef_im = rows(g), rows(4 + g), rows(8 + g), rows(12 + g)
        outs = []
        for left, right in (
            ([coef_re, coef_im], [back_re, back_im]),
            ([coef_re, -coef_im], [back_im, back_re]),
        ):
            left = jnp.concatenate(left, axis=0).astype(BF16)
            right = jnp.concatenate(right, axis=0).astype(BF16)
            outs.append(dot(left, right, TN))
        real, imag = outs
        lane = iota(real.shape, 1)
        low = jnp.where(lane < 64, real, pltpu.roll(imag, 64, 1))
        high = jnp.where(lane < 64, pltpu.roll(real, 64, 1), imag)
        grad_ref[g] = low[0:64] + high[64:128]
    mix = []
    for i in range(3):
        total = jnp.sum(rows(16 + i), axis=0, keepdims=True)
        mix.append(total + pltpu.roll(total, 64, 1))
    for g in range(4):
        own = grad_ref[g, pl.ds(quarter * 16, 16), :]
        for c in range(4):
            k = 4 * g + c
            send_ref[k, 0:4, :] = own[4 * c : 4 * c + 4]
            for i in range(3):
                send_ref[k, 4 + i : 5 + i, :] = mix[i]
            send_ref[k, 7:8, :] = mix[0]


def final_kernel(recv_ref, lift_ref, grad_ref, mix_ref):
    total = recv_ref[0]
    for k in range(1, recv_ref.shape[0]):
        total = total + recv_ref[k]
    grad_ref[...] = total[0:4]
    lift = lift_ref[...].astype(F32)
    mix = lift[:, 0:1] * total[4:5, 0:64]
    mix = mix + lift[:, 1:2] * total[5:6, 0:64]
    mix_ref[...] = mix + lift[:, 2:3] * total[6:7, 0:64]


def spectral_table(mode_index, blocks, rows):
    place = jnp.arange(blocks * 128, dtype=jnp.int32)
    within = place & 127
    cell = (place >> 7) * rows + jnp.where(within >= rows, within - rows, within)
    x_length = blocks * rows
    phases = mode_index[:, None] * cell[None, :] % x_length
    angles = 2.0 * jnp.pi / x_length * phases.astype(F32)
    return jnp.concatenate([jnp.cos(angles), -jnp.sin(angles)], axis=0).astype(BF16)


def local(slot_field, solid, lift_weight, spectral_weight, mix_weight, project_weight, mode_index):
    tile = slot_field[0]
    planes, rows, lanes = tile.shape
    blocks = lax.axis_size("gx")
    x_length = rows * blocks
    cell_total = x_length * lanes * lax.axis_size("gy") * planes
    loss_scale = 16.0 / math.sqrt(cell_total)
    scale_dft = 1.0 / math.sqrt(x_length)
    table = spectral_table(mode_index, blocks, rows)
    lift_t = jnp.pad(lift_weight.T, ((0, 0), (0, 5)))
    mix_t = mix_weight.T
    proj = jnp.pad(project_weight, ((0, 0), (0, 5)))
    proj_t = proj.T

    edge = jax.ShapeDtypeStruct((planes, lanes), F32)
    up, down, right, left = call(edge_kernel, [edge] * 4, tile)

    def shift(array, axis, step):
        count = lax.axis_size(axis)
        pairs = [(i, i + step) for i in range(count) if 0 <= i + step < count]
        return lax.ppermute(array, axis, pairs)

    rims = [shift(down, "gx", -1), shift(up, "gx", 1), shift(right, "gy", 1), shift(left, "gy", -1)]
    rims = jnp.stack(rims + [jnp.zeros_like(up)] * 4, axis=1)
    payload = jnp.concatenate([tile, rims], axis=1)
    fields = lax.all_gather(payload, "grp", axis=0)

    new_velocity, send = call(
        lambda *refs: stencil_kernel(rows, *refs),
        [
            jax.ShapeDtypeStruct((3, planes, rows, lanes), F32),
            jax.ShapeDtypeStruct((blocks * 8, 128), BF16),
        ],
        fields,
        solid,
    )
    recv = lax.all_to_all(
        send.reshape(blocks, 8, 128), "gx", split_axis=0, concat_axis=0, tiled=True
    )
    send = call(
        lambda *refs: line_kernel(scale_dft, loss_scale, *refs),
        jax.ShapeDtypeStruct((blocks, 24, 128), BF16),
        recv,
        table,
        lift_t,
        mix_t,
        spectral_weight,
        proj,
        proj_t,
        scratch=[pltpu.VMEM((64, 128), F32), pltpu.VMEM((64, 128), F32)],
    )
    recv = lax.all_to_all(send, "gx", split_axis=0, concat_axis=0, tiled=True)
    send = call(
        grad_kernel,
        jax.ShapeDtypeStruct((16, 8, 128), F32),
        recv,
        scratch=[pltpu.VMEM((blocks * 24, 128), F32), pltpu.VMEM((4, 64, 128), F32)],
    )
    recv = lax.all_to_all(send, ("grp", "gy"), split_axis=0, concat_axis=0, tiled=True)
    spectral_grad, mix_grad = call(
        final_kernel,
        [jax.ShapeDtypeStruct((4, 128), F32), jax.ShapeDtypeStruct((64, 64), F32)],
        recv,
        lift_t,
    )
    return new_velocity, spectral_grad, mix_grad


def solution(mesh):
    in_specs = (P("grp", None, "gx", "gy"), P(None, "gx", "gy"), P(), P(), P(), P(), P())
    out_specs = (P(None, None, "gx", "gy"), P(("grp", "gx", "gy"), None), P())
    return jax.shard_map(local, mesh=mesh, in_specs=in_specs, out_specs=out_specs, check_vma=False)
```

time: 371 us -> 85.5 us (0.23)
  waiting for transfers between devices: 186 us -> 7.88 us
  blocking collectives: 142 us -> 44.4 us
  between operations: 14.3 us -> 0.82 us
  Pallas kernels: 0 us -> 5.5 us
    unnamed x2 -> x0, waiting for transfers between devices: 171 us -> none
    psum x1 -> x0, blocking collectives: 116 us -> none  [local(): mix_grad = lax.psum(mix_part, ('grp', 'gx', 'gy'))]
    all_to_all x0 -> x2, blocking collectives: none -> 30.3 us  [the longest x1 17.7 us: local(): lax.all_to_all(send, ('grp', 'gy'), split_axis=0, concat_axis=0, tiled=True)]
    all_gather x2 -> x1, blocking collectives: 25.9 us -> 14.1 us  [local(): fields = lax.all_gather(payload, 'grp', axis=0)]
    ppermute x4, waiting for transfers between devices: 7.25 us -> 1.25 us  [shift(): return lax.ppermute(array, axis, pairs)]
    pallas_call x0 -> x5, Pallas kernels: none -> 5.5 us  [call(): pl.pallas_call(kernel, out_shape=out_shape, in_specs=[VMEM] * len(args),...]
  transfers between devices with their start and end apart: 6 -> 5, of which waited for: 4 -> 2; matrix products, arithmetic and copies ran while one was open for 0% -> 3% of each run, Pallas kernels for 0% -> 0%
where the time goes in v1:
time: 85.5 us; the launch traced here: 85 us
  blocking collectives  44.4 us (52%)
  starting transfers between devices  21.1 us (25%)
  waiting for transfers between devices  7.88 us (9%)
  Pallas kernels  5.5 us (6%)
  local copies, waits for them, and re-layouts  2.99 us (3%)
  other arithmetic  2.38 us (3%)
    all_to_all x1, blocking collectives, local(): lax.all_to_all(send, ('grp', 'gy'), split_axis=0, concat_axis=0, tiled=True)  17.7 us
    all_gather x1, blocking collectives, local(): fields = lax.all_gather(payload, 'grp', axis=0)  14.1 us
    all_to_all x1, blocking collectives, local(): recv = lax.all_to_all(send, 'gx', split_axis=0, concat_axis=0, tiled=True)  12.5 us
    ppermute x4, starting transfers between devices, shift(): return lax.ppermute(array, axis, pairs)  11.4 us
    all_to_all x1, starting transfers between devices, local(): lax.all_to_all(send.reshape(blocks, 8, 128), 'gx', split_axis=0, concat_a...  9.68 us
    all_to_all x1, waiting for transfers between devices, local(): lax.all_to_all(send.reshape(blocks, 8, 128), 'gx', split_axis=0, concat_a...  6.63 us
    pallas_call x5, Pallas kernels, call(): pl.pallas_call(kernel, out_shape=out_shape, in_specs=[VMEM] * len(args),...  5.5 us
    unnamed x19, local copies, waits for them, and re-layouts  2.94 us
  transfers between devices with their start and end apart: 5, of which 2 were waited for; matrix products, arithmetic and copies ran while one was open for 3% of the time, Pallas kernels for 0%

profile of v1, /device:TPU:1, one launch (start us, length us, event | category | flops | bytes accessed | tf_op | source)
XLA Modules:
  0.0 85.0 jit_solution(5797069768072641303)
XLA Ops:
  0.6 0.0 copy-start.1
  0.6 0.8 copy-done.1
  1.4 0.1 shard_map.94
  1.5 1.3 %collective-permute-start = (f32[2,128]{1,0:T(2,128)S(1)}, f32[2,128]{1,0:T(2,128)S(1)}, u32[]{:S(2)}, u32[]{:S(2)}) collective-permute-start(f32[2,128]{1,0:T(2,128)S(1)} %get-tuple-element.11), channel_id=1, source_target_pairs={{4,0},{8,4},{12,8},{16,12},{20,16},{24,20},{28,24},{32,28},{36,32}... | collective-permute-start | bytes 3080 | tf_op jit(solution)/shard_map/ppermute | solution.py:253
  2.8 4.7 %collective-permute-start.1 = (f32[2,128]{1,0:T(2,128)S(1)}, f32[2,128]{1,0:T(2,128)S(1)}, u32[]{:S(2)}, u32[]{:S(2)}) collective-permute-start(f32[2,128]{1,0:T(2,128)S(1)} %get-tuple-element.12), channel_id=1, source_target_pairs={{0,4},{4,8},{8,12},{12,16},{16,20},{20,24},{24,28},{28,32},{32,36}... | collective-permute-start | bytes 3080 | tf_op jit(solution)/shard_map/ppermute | solution.py:253
  7.5 4.2 %collective-permute-start.2 = (f32[2,128]{1,0:T(2,128)S(1)}, f32[2,128]{1,0:T(2,128)S(1)}, u32[]{:S(2)}, u32[]{:S(2)}) collective-permute-start(f32[2,128]{1,0:T(2,128)S(1)} %get-tuple-element.13), channel_id=1, source_target_pairs={{0,1},{1,2},{2,3},{4,5},{5,6},{6,7},{8,9},{9,10},{10,11},{12,13},{... | collective-permute-start | bytes 3080 | tf_op jit(solution)/shard_map/ppermute | solution.py:253
  11.7 0.0 copy-start.7
  11.7 1.3 %collective-permute-start.3 = (f32[2,128]{1,0:T(2,128)S(1)}, f32[2,128]{1,0:T(2,128)S(1)}, u32[]{:S(2)}, u32[]{:S(2)}) collective-permute-start(f32[2,128]{1,0:T(2,128)S(1)} %get-tuple-element.14), channel_id=1, source_target_pairs={{1,0},{2,1},{3,2},{5,4},{6,5},{7,6},{9,8},{10,9},{11,10},{13,12},{... | collective-permute-start | bytes 3080 | tf_op jit(solution)/shard_map/ppermute | solution.py:253
  13.0 0.0 copy-done.7
  13.0 0.0 copy-start.2
  13.0 2.3 %cosine_convert_fusion = (bf16[32,4096]{1,0:T(8,128)(2,1)S(1)}, bf16[32,4096]{1,0:T(8,128)(2,1)S(1)}) fusion(s32[4096]{0:T(1024)S(1)} %fusion.6, s32[32]{0:T(128)S(1)} %copy-done.7), kind=kLoop, calls=%fused_computation.5 | loop fusion | flops 1572864 | bytes 540800 | tf_op jit(solution)/shard_map/convert
  15.4 0.0 collective-permute-done
  15.4 0.0 collective-permute-done.1
  15.4 0.0 collective-permute-done.2
  15.4 1.2 %collective-permute-done.3 = f32[2,128]{1,0:T(2,128)S(1)} collective-permute-done((f32[2,128]{1,0:T(2,128)S(1)}, f32[2,128]{1,0:T(2,128)S(1)}, u32[]{:S(2)}, u32[]{:S(2)}) %collective-permute-start.3) | collective-permute-done | bytes 1056 | tf_op jit(solution)/shard_map/ppermute | solution.py:253
  16.6 0.0 copy-done.2
  16.7 0.0 copy-start.3
  16.7 14.1 %all-gather = f32[8,56,128]{2,1,0:T(8,128)S(1)} all-gather(f32[2,56,128]{2,1,0:T(8,128)S(1)} %concatenate.11), channel_id=2, replica_groups=mesh['grp'=4,'gx'=32,'gy'=4] {'grp'}, dimensions={0}, use_global_device_ids=true | all-gather | bytes 286720 | tf_op jit(solution)/shard_map/all_gather | solution.py:258
  30.8 0.0 copy-done.3
  30.8 1.4 %shard_map.95 = (f32[3,2,48,128]{3,2,1,0:T(8,128)}, bf16[256,128]{1,0:T(8,128)(2,1)}) custom-call(f32[4,2,56,128]{3,2,1,0:T(8,128)S(1)} %bitcast.11, s32[2,48,128]{2,1,0:T(8,128)S(1)} %copy-done.3), custom_call_target="tpu_custom_call" | custom-call | tf_op jit(solution)/shard_map/pallas_call | solution.py:32
  32.2 9.7 %all-to-all-start = ((bf16[32,8,128]{2,1,0:T(8,128)(2,1)}), bf16[32,8,128]{2,1,0:T(8,128)(2,1)S(1)}, u32[]{:S(2)}, u32[]{:S(2)}) async-start(bf16[32,8,128]{2,1,0:T(8,128)(2,1)} %bitcast.6), calls=%async_computation | async-start | bytes 131072 | tf_op jit(solution)/shard_map/all_to_all | solution.py:269
  41.9 0.0 copy-start.6
  41.9 0.0 copy-start
  42.0 0.6 copy-done.6
  42.6 0.0 copy-start.4
  42.6 0.1 copy.13
  42.7 0.6 copy-done.4
  43.3 0.0 copy-start.5
  43.3 0.1 copy.14
  43.4 0.6 copy-done.5
  44.0 0.1 copy.16
  44.1 6.6 %all-to-all-done.refs_0_ = bf16[32,8,128]{2,1,0:T(8,128)(2,1)S(1)} async-done(((bf16[32,8,128]{2,1,0:T(8,128)(2,1)}), bf16[32,8,128]{2,1,0:T(8,128)(2,1)S(1)}, u32[]{:S(2)}, u32[]{:S(2)}) %all-to-all-start) | async-done | bytes 65568 | tf_op jit(solution)/shard_map/all_to_all | solution.py:269
  50.8 0.0 copy-done
  50.8 2.9 %shard_map.96 = bf16[32,24,128]{2,1,0:T(8,128)(2,1)S(1)} custom-call(bf16[32,8,128]{2,1,0:T(8,128)(2,1)S(1)} %all-to-all-done.refs_0_, bf16[64,4096]{1,0:T(8,128)(2,1)S(1)} %pad_maximum_fusion.refs_1_, bf16[64,8]{1,0:T(8,128)(2,1)S(1)} %pad.7.refs_2_.lift_ref, bf16[64,64]{1,0:T(8,128)(2,1)S(1)} %bitcast.14, bf16[2048,128]{1,0:T(8,128)(2,1)S(1)} %copy-done, ...), custom_call_target="tpu_custom_call" | custom-call | tf_op jit(solution)/shard_map/pallas_call | solution.py:32
  53.7 12.5 %all_to_all.15.recv_ref = bf16[32,24,128]{2,1,0:T(8,128)(2,1)S(1)} all-to-all(bf16[32,24,128]{2,1,0:T(8,128)(2,1)S(1)} %shard_map.96), channel_id=1, replica_groups=mesh['grp'=4,'gx'=32,'gy'=4] {'gx'}, dimensions={0} | all-to-all | bytes 393216 | tf_op jit(solution)/shard_map/all_to_all | solution.py:284
  66.2 0.4 shard_map.97
  66.6 17.7 %all_to_all.16.recv_ref = f32[16,8,128]{2,1,0:T(8,128)S(1)} all-to-all(f32[16,8,128]{2,1,0:T(8,128)S(1)} %shard_map.97), channel_id=1, replica_groups=mesh['grp'=4,'gx'=32,'gy'=4] {'grp','gy'}, dimensions={0} | all-to-all | bytes 131072 | tf_op jit(solution)/shard_map/all_to_all | solution.py:291
  84.3 0.7 shard_map.98
  (7 shorter events, 0.1 us)
Async XLA Ops:
  0.6 0.8 copy-start.1
  1.5 13.8 %collective-permute-start = (f32[2,128]{1,0:T(2,128)S(1)}, f32[2,128]{1,0:T(2,128)S(1)}, u32[]{:S(2)}, u32[]{:S(2)}) collective-permute-start(f32[2,128]{1,0:T(2,128)S(1)} %get-tuple-element.11), channel_id=1, source_target_pairs={{4,0},{8,4},{12,8},{16,12},{20,16},{24,20},{28,24},{32,28},{36,32}... | collective-permute-start | bytes 3080 | tf_op jit(solution)/shard_map/ppermute | solution.py:253
  2.8 12.5 %collective-permute-start.1 = (f32[2,128]{1,0:T(2,128)S(1)}, f32[2,128]{1,0:T(2,128)S(1)}, u32[]{:S(2)}, u32[]{:S(2)}) collective-permute-start(f32[2,128]{1,0:T(2,128)S(1)} %get-tuple-element.12), channel_id=1, source_target_pairs={{0,4},{4,8},{8,12},{12,16},{16,20},{20,24},{24,28},{28,32},{32,36}... | collective-permute-start | bytes 3080 | tf_op jit(solution)/shard_map/ppermute | solution.py:253
  7.5 7.9 %collective-permute-start.2 = (f32[2,128]{1,0:T(2,128)S(1)}, f32[2,128]{1,0:T(2,128)S(1)}, u32[]{:S(2)}, u32[]{:S(2)}) collective-permute-start(f32[2,128]{1,0:T(2,128)S(1)} %get-tuple-element.13), channel_id=1, source_target_pairs={{0,1},{1,2},{2,3},{4,5},{5,6},{6,7},{8,9},{9,10},{10,11},{12,13},{... | collective-permute-start | bytes 3080 | tf_op jit(solution)/shard_map/ppermute | solution.py:253
  11.7 1.3 %copy-start.7 = (s32[32]{0:T(128)S(1)}, s32[32]{0:T(128)}, u32[]{:S(2)}) copy-start(s32[32]{0:T(128)} %param.13) | copy-start | bytes 388
  11.7 5.0 %collective-permute-start.3 = (f32[2,128]{1,0:T(2,128)S(1)}, f32[2,128]{1,0:T(2,128)S(1)}, u32[]{:S(2)}, u32[]{:S(2)}) collective-permute-start(f32[2,128]{1,0:T(2,128)S(1)} %get-tuple-element.14), channel_id=1, source_target_pairs={{1,0},{2,1},{3,2},{5,4},{6,5},{7,6},{9,8},{10,9},{11,10},{13,12},{... | collective-permute-start | bytes 3080 | tf_op jit(solution)/shard_map/ppermute | solution.py:253
  13.0 3.6 %copy-start.2 = (f32[1,2,48,128]{3,2,1,0:T(8,128)S(1)}, f32[1,2,48,128]{3,2,1,0:T(8,128)}, u32[]{:S(2)}) copy-start(f32[1,2,48,128]{3,2,1,0:T(8,128)} %param.7) | copy-start | bytes 147460
  16.7 14.2 %copy-start.3 = (s32[2,48,128]{2,1,0:T(8,128)S(1)}, s32[2,48,128]{2,1,0:T(8,128)}, u32[]{:S(2)}) copy-start(s32[2,48,128]{2,1,0:T(8,128)} %refs_1_.1) | copy-start | bytes 147460
  32.2 18.5 %all-to-all-start = ((bf16[32,8,128]{2,1,0:T(8,128)(2,1)}), bf16[32,8,128]{2,1,0:T(8,128)(2,1)S(1)}, u32[]{:S(2)}, u32[]{:S(2)}) async-start(bf16[32,8,128]{2,1,0:T(8,128)(2,1)} %bitcast.6), calls=%async_computation | async-start | bytes 131072 | tf_op jit(solution)/shard_map/all_to_all | solution.py:269
  41.9 0.7 copy-start.6
  41.9 8.8 %copy-start = (bf16[2048,128]{1,0:T(8,128)(2,1)S(1)}, bf16[2048,128]{1,0:T(8,128)(2,1)}, u32[]{:S(2)}) copy-start(bf16[2048,128]{1,0:T(8,128)(2,1)} %refs_4_.1) | copy-start | bytes 1572868
  42.6 0.7 copy-start.4
  43.3 0.7 copy-start.5

commit v2 on v1

--- a/solution.py
+++ b/solution.py
@@ -39,21 +39,18 @@
     )(*args)
 
 
-def edge_kernel(tile_ref, up_ref, down_ref, right_ref, left_ref):
+def edge_kernel(tile_ref, right_ref, left_ref):
     rows, lanes = tile_ref.shape[1:]
     same = iota((rows, lanes), 0) == iota((rows, lanes), 1)
     for z in range(2):
         tile = tile_ref[z]
-        up_ref[z : z + 1, :] = tile[rows - 1 : rows, :]
-        down_ref[z : z + 1, :] = tile[0:1, :]
         for ref, lane in ((right_ref, lanes - 1), (left_ref, 0)):
             column = jnp.broadcast_to(tile[:, lane : lane + 1], (rows, lanes))
             ref[z : z + 1, :] = jnp.sum(jnp.where(same, column, 0.0), axis=0, keepdims=True)
 
 
-def stencil_kernel(rows, fields_ref, solid_ref, new_ref, send_ref):
+def section(rows, fields_ref, solid_ref, rims):
     lanes = fields_ref.shape[3]
-    role = lax.axis_index("grp")
     row = iota((rows, lanes), 0)
     lane = iota((rows, lanes), 1)
     same = row == lane
@@ -61,18 +58,20 @@
 
     def near(f, z):
         tile = centre[f][z]
-        x_up = fields_ref[f, z, 1 : rows + 1, :]
-        below = fields_ref[f, z, rows + 1 : rows + 2, :]
+        below = above = 0.0
+        if rims is not None:
+            below, above = (ref[2 * f + z : 2 * f + z + 1, :] for ref in rims)
         x_down = jnp.where(row == 0, below, pltpu.roll(tile, 1, 0))
-        rims = []
-        for k in (2, 3):
+        x_up = jnp.where(row == rows - 1, above, pltpu.roll(tile, rows - 1, 0))
+        sides = []
+        for k in (0, 1):
             line = jnp.broadcast_to(fields_ref[f, z, rows + k : rows + k + 1, :], (rows, lanes))
-            rims.append(jnp.sum(jnp.where(same, line, 0.0), axis=1, keepdims=True))
-        y_down = jnp.where(lane == 0, rims[0], pltpu.roll(tile, 1, 1))
-        y_up = jnp.where(lane == lanes - 1, rims[1], pltpu.roll(tile, lanes - 1, 1))
+            sides.append(jnp.sum(jnp.where(same, line, 0.0), axis=1, keepdims=True))
+        y_down = jnp.where(lane == 0, sides[0], pltpu.roll(tile, 1, 1))
+        y_up = jnp.where(lane == lanes - 1, sides[1], pltpu.roll(tile, lanes - 1, 1))
         return x_up, x_down, y_up, y_down
 
-    values = []
+    results = []
     for z in range(2):
         fluid = 1.0 - solid_ref[z].astype(F32)
         velocity = [centre[f][z] for f in range(3)]
@@ -91,17 +90,49 @@
             lap = other + x_up + x_down + y_up + y_down - 6.0 * velocity[f]
             update = velocity[f] + TIME_STEP * (VISCOSITY * lap - advect - press[f])
             new.append(update * fluid)
-            new_ref[f, z] = new[f]
-        parts = [part.astype(BF16) for part in velocity + new]
-        values.append(jnp.concatenate(parts, axis=1))
-    pad = jnp.zeros((128 - 2 * rows, 6 * lanes), BF16)
+        results.append(velocity + new + [centre[3][z], fluid])
+    return results
+
+
+def source_kernel(rows, fields_ref, solid_ref, send_ref, low_ref, high_ref):
+    lanes = fields_ref.shape[3]
+    role = lax.axis_index("grp")
+    results = section(rows, fields_ref, solid_ref, None)
+    for f in range(4):
+        for z in range(2):
+            low_ref[2 * f + z : 2 * f + z + 1, :] = fields_ref[f, z, 0:1, :]
+            high_ref[2 * f + z : 2 * f + z + 1, :] = fields_ref[f, z, rows - 1 : rows, :]
+    values = [jnp.concatenate([p.astype(BF16) for p in parts], axis=1) for parts in results]
+    pad = jnp.zeros((128 - 2 * rows, 8 * lanes), BF16)
     stacked = jnp.concatenate(values + [pad], axis=0)
     count = send_ref.shape[0]
-    out_row = iota((count, 6 * lanes), 0)
-    column = iota((count, 6 * lanes), 1)
+    out_row = iota((count, 8 * lanes), 0)
+    column = iota((count, 8 * lanes), 1)
     wanted = (out_row & 7) * lanes + (out_row >> 3) + role * (count // 8)
-    pick = jnp.where(((out_row & 7) < 6) & (column == wanted), 1.0, 0.0).astype(BF16)
+    pick = jnp.where(column == wanted, 1.0, 0.0).astype(BF16)
     send_ref[...] = dot(pick, stacked, NT).astype(BF16)
+
+
+def velocity_kernel(rows, fields_ref, solid_ref, below_ref, above_ref, new_ref):
+    results = section(rows, fields_ref, solid_ref, (below_ref, above_ref))
+    for z in range(2):
+        for f in range(3):
+            new_ref[f, z] = results[z][3 + f]
+
+
+def neighbour_terms(lines, rows):
+    cells = lines.shape[1]
+    lane = iota((8, cells), 1)
+    place = lane & 127
+    starts = ((place == 0) | (place == rows)) & (lane >= 128)
+    stops = ((place == rows - 1) | (place == 2 * rows - 1)) & (lane < cells - 128)
+    hop = 128 - rows + 1
+    below = jnp.where(starts, pltpu.roll(lines, hop, 1), 0.0)
+    above = jnp.where(stops, pltpu.roll(lines, cells - hop, 1), 0.0)
+    slope = 0.5 * (above - below)
+    first = jnp.where(iota((8, cells), 0) == 0, slope[6:7, :], 0.0)
+    terms = VISCOSITY * (above + below) - lines[0:1, :] * slope - first
+    return lines[7:8, :] * (TIME_STEP * terms)
 
 
 def line_kernel(
@@ -143,7 +174,8 @@
     active = (hidden * half).astype(BF16)
     slope = half + (0.5 * GELU_A) * hidden * (1.0 - tanh * tanh) * (1.0 + (3.0 * GELU_B) * square)
     predicted = dot(projt_ref[...], active, NN)
-    target = pltpu.roll(lines.astype(F32), 5, 0)
+    wide_lines = lines.astype(F32)
+    target = pltpu.roll(wide_lines, 5, 0) + neighbour_terms(wide_lines, rows)
     misfit = (predicted - target) * loss_scale
     misfit = jnp.where(iota(misfit.shape, 0) < 3, misfit, 0.0)
     high = misfit.astype(BF16)
@@ -238,36 +270,42 @@
     cell_total = x_length * lanes * lax.axis_size("gy") * planes
     loss_scale = 16.0 / math.sqrt(cell_total)
     scale_dft = 1.0 / math.sqrt(x_length)
-    table = spectral_table(mode_index, blocks, rows)
     lift_t = jnp.pad(lift_weight.T, ((0, 0), (0, 5)))
     mix_t = mix_weight.T
     proj = jnp.pad(project_weight, ((0, 0), (0, 5)))
     proj_t = proj.T
 
-    edge = jax.ShapeDtypeStruct((planes, lanes), F32)
-    up, down, right, left = call(edge_kernel, [edge] * 4, tile)
-
     def shift(array, axis, step):
         count = lax.axis_size(axis)
         pairs = [(i, i + step) for i in range(count) if 0 <= i + step < count]
         return lax.ppermute(array, axis, pairs)
 
-    rims = [shift(down, "gx", -1), shift(up, "gx", 1), shift(right, "gy", 1), shift(left, "gy", -1)]
-    rims = jnp.stack(rims + [jnp.zeros_like(up)] * 4, axis=1)
+    edge = jax.ShapeDtypeStruct((planes, lanes), F32)
+    right, left = call(edge_kernel, [edge] * 2, tile)
+    rims = [shift(right, "gy", 1), shift(left, "gy", -1)]
+    rims = jnp.stack(rims + [jnp.zeros_like(right)] * 6, axis=1)
     payload = jnp.concatenate([tile, rims], axis=1)
     fields = lax.all_gather(payload, "grp", axis=0)
 
-    new_velocity, send = call(
-        lambda *refs: stencil_kernel(rows, *refs),
-        [
-            jax.ShapeDtypeStruct((3, planes, rows, lanes), F32),
-            jax.ShapeDtypeStruct((blocks * 8, 128), BF16),
-        ],
+    rim = jax.ShapeDtypeStruct((8, lanes), F32)
+    send, low, high = call(
+        lambda *refs: source_kernel(rows, *refs),
+        [jax.ShapeDtypeStruct((blocks * 8, 128), BF16), rim, rim],
         fields,
         solid,
     )
+    mode_index, low, high, send = lax.optimization_barrier((mode_index, low, high, send))
     recv = lax.all_to_all(
         send.reshape(blocks, 8, 128), "gx", split_axis=0, concat_axis=0, tiled=True
+    )
+    table = spectral_table(mode_index, blocks, rows)
+    new_velocity = call(
+        lambda *refs: velocity_kernel(rows, *refs),
+        jax.ShapeDtypeStruct((3, planes, rows, lanes), F32),
+        fields,
+        solid,
+        shift(high, "gx", 1),
+        shift(low, "gx", -1),
     )
     send = call(
         lambda *refs: line_kernel(scale_dft, loss_scale, *refs),

time: 85.5 us -> 82.6 us (0.966)
  blocking collectives: 44.4 us -> 26.7 us
  starting transfers between devices: 21.1 us -> 30.5 us
  waiting for transfers between devices: 7.88 us -> 12.3 us
  Pallas kernels: 5.5 us -> 7.25 us
  local copies, waits for them, and re-layouts: 2.99 us -> 1.74 us
    all_to_all x1 -> x0, blocking collectives: 17.7 us -> none  [local(): lax.all_to_all(send, ('grp', 'gy'), split_axis=0, concat_axis=0, tiled=True)]
    all_to_all x0 -> x1, starting transfers between devices: none -> 10.2 us  [local(): lax.all_to_all(send, ('grp', 'gy'), split_axis=0, concat_axis=0, tiled=True)]
    ppermute x4, waiting for transfers between devices: 1.25 us -> 5.82 us  [shift(): return lax.ppermute(array, axis, pairs)]
    pallas_call x5 -> x6, Pallas kernels: 5.5 us -> 7.25 us  [call(): pl.pallas_call(kernel, out_shape=out_shape, in_specs=[VMEM] * len(args),...]
    unnamed x19, local copies, waits for them, and re-layouts: 2.94 us -> 1.69 us
  transfers between devices with their start and end apart: 5 -> 6, of which waited for: 2 -> 3; matrix products, arithmetic and copies ran while one was open for 3% -> 3% of each run, Pallas kernels for 0% -> 1%
where the time goes in v2:
time: 82.6 us; the launch traced here: 81.7 us
  starting transfers between devices  30.5 us (37%)
  blocking collectives  26.7 us (32%)
  waiting for transfers between devices  12.3 us (15%)
  Pallas kernels  7.25 us (9%)
  other arithmetic  2.38 us (3%)
  local copies, waits for them, and re-layouts  1.74 us (2%)
    all_gather x1, blocking collectives, local(): fields = lax.all_gather(payload, 'grp', axis=0)  13.7 us
    all_to_all x1, blocking collectives, local(): recv = lax.all_to_all(send, 'gx', split_axis=0, concat_axis=0, tiled=True)  13 us
    ppermute x4, starting transfers between devices, shift(): return lax.ppermute(array, axis, pairs)  10.5 us
    all_to_all x1, starting transfers between devices, local(): lax.all_to_all(send, ('grp', 'gy'), split_axis=0, concat_axis=0, tiled=True)  10.2 us
    all_to_all x1, starting transfers between devices, local(): lax.all_to_all(send.reshape(blocks, 8, 128), 'gx', split_axis=0, concat_a...  9.8 us
    pallas_call x6, Pallas kernels, call(): pl.pallas_call(kernel, out_shape=out_shape, in_specs=[VMEM] * len(args),...  7.25 us
    all_to_all x1, waiting for transfers between devices, local(): lax.all_to_all(send.reshape(blocks, 8, 128), 'gx', split_axis=0, concat_a...  6.45 us
    ppermute x4, waiting for transfers between devices, shift(): return lax.ppermute(array, axis, pairs)  5.82 us
  transfers between devices with their start and end apart: 6, of which 3 were waited for; matrix products, arithmetic and copies ran while one was open for 3% of the time, Pallas kernels for 1%

profile of v2, /device:TPU:1, one launch (start us, length us, event | category | flops | bytes accessed | tf_op | source)
XLA Modules:
  0.0 81.7 jit_solution(7214182364463667648)
XLA Ops:
  0.6 0.0 copy-start.1
  0.6 0.8 copy-done.1
  1.4 0.1 shard_map.94
  1.5 4.8 %collective-permute-start = (f32[2,128]{1,0:T(2,128)S(1)}, f32[2,128]{1,0:T(2,128)S(1)}, u32[]{:S(2)}, u32[]{:S(2)}) collective-permute-start(f32[2,128]{1,0:T(2,128)S(1)} %get-tuple-element.14), channel_id=1, source_target_pairs={{0,1},{1,2},{2,3},{4,5},{5,6},{6,7},{8,9},{9,10},{10,11},{12,13},{... | collective-permute-start | bytes 3080 | tf_op jit(solution)/shard_map/ppermute | solution.py:281
  6.4 0.0 copy-start.5
  6.4 1.3 %collective-permute-start.1 = (f32[2,128]{1,0:T(2,128)S(1)}, f32[2,128]{1,0:T(2,128)S(1)}, u32[]{:S(2)}, u32[]{:S(2)}) collective-permute-start(f32[2,128]{1,0:T(2,128)S(1)} %get-tuple-element.15), channel_id=1, source_target_pairs={{1,0},{2,1},{3,2},{5,4},{6,5},{7,6},{9,8},{10,9},{11,10},{13,12},{... | collective-permute-start | bytes 3080 | tf_op jit(solution)/shard_map/ppermute | solution.py:281
  7.7 0.0 copy-done.5
  7.7 0.0 copy-start.6
  7.7 0.0 copy-start.4
  7.7 0.1 copy.16
  7.9 0.5 copy-done.6
  8.4 0.1 copy.13
  8.5 0.0 copy-done.4
  8.5 0.0 copy-start.2
  8.5 0.1 copy.14
  8.7 0.0 collective-permute-done
  8.7 2.7 %collective-permute-done.1 = f32[2,128]{1,0:T(2,128)S(1)} collective-permute-done((f32[2,128]{1,0:T(2,128)S(1)}, f32[2,128]{1,0:T(2,128)S(1)}, u32[]{:S(2)}, u32[]{:S(2)}) %collective-permute-start.1) | collective-permute-done | bytes 1056 | tf_op jit(solution)/shard_map/ppermute | solution.py:281
  11.3 0.0 copy-done.2
  11.4 0.0 copy-start.3
  11.4 13.7 %all-gather = f32[8,56,128]{2,1,0:T(8,128)S(1)} all-gather(f32[2,56,128]{2,1,0:T(8,128)S(1)} %concatenate.15), channel_id=2, replica_groups=mesh['grp'=4,'gx'=32,'gy'=4] {'grp'}, dimensions={0}, use_global_device_ids=true | all-gather | bytes 286720 | tf_op jit(solution)/shard_map/all_gather | solution.py:288
  25.1 0.0 copy-done.3
  25.1 1.4 %shard_map.95 = (bf16[256,128]{1,0:T(8,128)(2,1)}, f32[8,128]{1,0:T(8,128)S(1)}, f32[8,128]{1,0:T(8,128)S(1)}) custom-call(f32[4,2,56,128]{3,2,1,0:T(8,128)S(1)} %bitcast.9, s32[2,48,128]{2,1,0:T(8,128)S(1)} %copy-done.3), custom_call_target="tpu_custom_call" | custom-call | tf_op jit(solution)/shard_map/pallas_call | solution.py:32
  26.5 0.0 copy-start.7
  26.5 9.8 %all-to-all-start = ((bf16[32,8,128]{2,1,0:T(8,128)(2,1)}), bf16[32,8,128]{2,1,0:T(8,128)(2,1)S(1)}, u32[]{:S(2)}, u32[]{:S(2)}) async-start(bf16[32,8,128]{2,1,0:T(8,128)(2,1)} %bitcast.4), calls=%async_computation | async-start | bytes 131072 | tf_op jit(solution)/shard_map/all_to_all | solution.py:298
  36.3 0.0 copy-done.7
  36.3 2.3 %cosine_convert_fusion = (bf16[32,4096]{1,0:T(8,128)(2,1)S(1)}, bf16[32,4096]{1,0:T(8,128)(2,1)S(1)}) fusion(s32[4096]{0:T(1024)S(1)} %fusion.6, s32[32]{0:T(128)S(1)} %copy-done.7), kind=kLoop, calls=%fused_computation.5 | loop fusion | flops 1572864 | bytes 540800 | tf_op jit(solution)/shard_map/convert
  38.7 0.0 copy-start
  38.7 6.5 %all-to-all-done.refs_0_ = bf16[32,8,128]{2,1,0:T(8,128)(2,1)S(1)} async-done(((bf16[32,8,128]{2,1,0:T(8,128)(2,1)}), bf16[32,8,128]{2,1,0:T(8,128)(2,1)S(1)}, u32[]{:S(2)}, u32[]{:S(2)}) %all-to-all-start) | async-done | bytes 65568 | tf_op jit(solution)/shard_map/all_to_all | solution.py:298
  45.2 0.0 copy-done
  45.2 2.9 %shard_map.97 = bf16[32,24,128]{2,1,0:T(8,128)(2,1)S(1)} custom-call(bf16[32,8,128]{2,1,0:T(8,128)(2,1)S(1)} %all-to-all-done.refs_0_, bf16[64,4096]{1,0:T(8,128)(2,1)S(1)} %pad_maximum_fusion.refs_1_, bf16[64,8]{1,0:T(8,128)(2,1)S(1)} %pad.7.refs_2_.lift_ref, bf16[64,64]{1,0:T(8,128)(2,1)S(1)} %bitcast.13, bf16[2048,128]{1,0:T(8,128)(2,1)S(1)} %copy-done, ...), custom_call_target="tpu_custom_call" | custom-call | tf_op jit(solution)/shard_map/pallas_call | solution.py:32
  48.1 13.0 %all_to_all.15.recv_ref = bf16[32,24,128]{2,1,0:T(8,128)(2,1)S(1)} all-to-all(bf16[32,24,128]{2,1,0:T(8,128)(2,1)S(1)} %shard_map.97), channel_id=1, replica_groups=mesh['grp'=4,'gx'=32,'gy'=4] {'gx'}, dimensions={0} | all-to-all | bytes 393216 | tf_op jit(solution)/shard_map/all_to_all | solution.py:322
  61.1 1.0 %shard_map.98 = f32[16,8,128]{2,1,0:T(8,128)} custom-call(bf16[32,24,128]{2,1,0:T(8,128)(2,1)S(1)} %all_to_all.15.recv_ref), custom_call_target="tpu_custom_call" | custom-call | tf_op jit(solution)/shard_map/pallas_call | solution.py:32
  62.1 10.2 %all-to-all-start.2 = ((f32[16,8,128]{2,1,0:T(8,128)}), f32[16,8,128]{2,1,0:T(8,128)S(1)}, u32[]{:S(2)}, u32[]{:S(2)}) async-start(f32[16,8,128]{2,1,0:T(8,128)} %shard_map.98), calls=%async_computation.2 | async-start | bytes 131072 | tf_op jit(solution)/shard_map/all_to_all | solution.py:329
  72.3 3.1 %collective-permute-start.2 = (f32[8,128]{1,0:T(8,128)S(1)}, f32[8,128]{1,0:T(8,128)S(1)}, u32[]{:S(2)}, u32[]{:S(2)}) collective-permute-start(f32[8,128]{1,0:T(8,128)S(1)} %get-tuple-element.19), channel_id=1, source_target_pairs={{0,4},{4,8},{8,12},{12,16},{16,20},{20,24},{24,28},{28,32},{32,36}... | collective-permute-start | bytes 12296 | tf_op jit(solution)/shard_map/ppermute | solution.py:281
  75.4 1.3 %collective-permute-start.3 = (f32[8,128]{1,0:T(8,128)S(1)}, f32[8,128]{1,0:T(8,128)S(1)}, u32[]{:S(2)}, u32[]{:S(2)}) collective-permute-start(f32[8,128]{1,0:T(8,128)S(1)} %get-tuple-element.20), channel_id=1, source_target_pairs={{4,0},{8,4},{12,8},{16,12},{20,16},{24,20},{28,24},{32,28},{36,32}... | collective-permute-start | bytes 12296 | tf_op jit(solution)/shard_map/ppermute | solution.py:281
  76.7 0.0 collective-permute-done.2.refs_2_
  76.7 3.1 %collective-permute-done.3.refs_3_ = f32[8,128]{1,0:T(8,128)S(1)} collective-permute-done((f32[8,128]{1,0:T(8,128)S(1)}, f32[8,128]{1,0:T(8,128)S(1)}, u32[]{:S(2)}, u32[]{:S(2)}) %collective-permute-start.3) | collective-permute-done | bytes 4128 | tf_op jit(solution)/shard_map/ppermute | solution.py:281
  79.9 1.1 %shard_map.96 = f32[3,2,48,128]{3,2,1,0:T(8,128)} custom-call(f32[4,2,56,128]{3,2,1,0:T(8,128)S(1)} %bitcast.10, s32[2,48,128]{2,1,0:T(8,128)S(1)} %copy-done.3, f32[8,128]{1,0:T(8,128)S(1)} %collective-permute-done.2.refs_2_, f32[8,128]{1,0:T(8,128)S(1)} %collective-permute-done.3.refs_3_), custom_call_target="tpu_custom_call" | custom-call | tf_op jit(solution)/shard_map/pallas_call | solution.py:32
  81.0 0.0 all-to-all-done.2.recv_ref
  81.0 0.7 shard_map.99
  (8 shorter events, 0.1 us)
Async XLA Ops:
  0.6 0.8 copy-start.1
  1.5 7.1 %collective-permute-start = (f32[2,128]{1,0:T(2,128)S(1)}, f32[2,128]{1,0:T(2,128)S(1)}, u32[]{:S(2)}, u32[]{:S(2)}) collective-permute-start(f32[2,128]{1,0:T(2,128)S(1)} %get-tuple-element.14), channel_id=1, source_target_pairs={{0,1},{1,2},{2,3},{4,5},{5,6},{6,7},{8,9},{9,10},{10,11},{12,13},{... | collective-permute-start | bytes 3080 | tf_op jit(solution)/shard_map/ppermute | solution.py:281
  6.4 1.3 %copy-start.5 = (bf16[64,3]{0,1:T(4,128)(2,1)S(1)}, bf16[64,3]{0,1:T(4,128)(2,1)}, u32[]{:S(2)}) copy-start(bf16[64,3]{0,1:T(4,128)(2,1)} %param.12) | copy-start | bytes 1156
  6.4 5.0 %collective-permute-start.1 = (f32[2,128]{1,0:T(2,128)S(1)}, f32[2,128]{1,0:T(2,128)S(1)}, u32[]{:S(2)}, u32[]{:S(2)}) collective-permute-start(f32[2,128]{1,0:T(2,128)S(1)} %get-tuple-element.15), channel_id=1, source_target_pairs={{1,0},{2,1},{3,2},{5,4},{6,5},{7,6},{9,8},{10,9},{11,10},{13,12},{... | collective-permute-start | bytes 3080 | tf_op jit(solution)/shard_map/ppermute | solution.py:281
  7.7 0.7 copy-start.6
  7.7 0.8 copy-start.4
  8.5 2.8 %copy-start.2 = (f32[1,2,48,128]{3,2,1,0:T(8,128)S(1)}, f32[1,2,48,128]{3,2,1,0:T(8,128)}, u32[]{:S(2)}) copy-start(f32[1,2,48,128]{3,2,1,0:T(8,128)} %param.7) | copy-start | bytes 147460
  11.4 13.7 %copy-start.3 = (s32[2,48,128]{2,1,0:T(8,128)S(1)}, s32[2,48,128]{2,1,0:T(8,128)}, u32[]{:S(2)}) copy-start(s32[2,48,128]{2,1,0:T(8,128)} %refs_1_.3) | copy-start | bytes 147460
  26.5 9.8 %copy-start.7 = (s32[32]{0:T(128)S(1)}, s32[32]{0:T(128)}, u32[]{:S(2)}) copy-start(s32[32]{0:T(128)} %param.13) | copy-start | bytes 388
  26.5 18.7 %all-to-all-start = ((bf16[32,8,128]{2,1,0:T(8,128)(2,1)}), bf16[32,8,128]{2,1,0:T(8,128)(2,1)S(1)}, u32[]{:S(2)}, u32[]{:S(2)}) async-start(bf16[32,8,128]{2,1,0:T(8,128)(2,1)} %bitcast.4), calls=%async_computation | async-start | bytes 131072 | tf_op jit(solution)/shard_map/all_to_all | solution.py:298
  38.7 6.5 %copy-start = (bf16[2048,128]{1,0:T(8,128)(2,1)S(1)}, bf16[2048,128]{1,0:T(8,128)(2,1)}, u32[]{:S(2)}) copy-start(bf16[2048,128]{1,0:T(8,128)(2,1)} %refs_4_.1) | copy-start | bytes 1572868
  62.1 18.9 %all-to-all-start.2 = ((f32[16,8,128]{2,1,0:T(8,128)}), f32[16,8,128]{2,1,0:T(8,128)S(1)}, u32[]{:S(2)}, u32[]{:S(2)}) async-start(f32[16,8,128]{2,1,0:T(8,128)} %shard_map.98), calls=%async_computation.2 | async-start | bytes 131072 | tf_op jit(solution)/shard_map/all_to_all | solution.py:329
  72.3 4.4 %collective-permute-start.2 = (f32[8,128]{1,0:T(8,128)S(1)}, f32[8,128]{1,0:T(8,128)S(1)}, u32[]{:S(2)}, u32[]{:S(2)}) collective-permute-start(f32[8,128]{1,0:T(8,128)S(1)} %get-tuple-element.19), channel_id=1, source_target_pairs={{0,4},{4,8},{8,12},{12,16},{16,20},{20,24},{24,28},{28,32},{32,36}... | collective-permute-start | bytes 12296 | tf_op jit(solution)/shard_map/ppermute | solution.py:281
  75.4 4.5 %collective-permute-start.3 = (f32[8,128]{1,0:T(8,128)S(1)}, f32[8,128]{1,0:T(8,128)S(1)}, u32[]{:S(2)}, u32[]{:S(2)}) collective-permute-start(f32[8,128]{1,0:T(8,128)S(1)} %get-tuple-element.20), channel_id=1, source_target_pairs={{4,0},{8,4},{12,8},{16,12},{20,16},{24,20},{28,24},{32,28},{36,32}... | collective-permute-start | bytes 12296 | tf_op jit(solution)/shard_map/ppermute | solution.py:281

commit v3 on v2

--- a/solution.py
+++ b/solution.py
@@ -143,12 +143,7 @@
     cells = blocks * 128
     rows = 48
     lines = jnp.concatenate([recv_ref[b] for b in range(blocks)], axis=1)
-    plane = iota((64, cells), 1) & 127
-    table = table_ref[...]
-    zero = jnp.zeros_like(table)
-    first = jnp.where(plane < rows, table, zero)
-    second = jnp.where((plane >= rows) & (plane < 2 * rows), table, zero)
-    both = jnp.concatenate([first, second], axis=0)
+    both = table_ref[...]
     lifted = dot(lift_ref[...], lines, NN).astype(BF16)
     coeffs = dot(both, lifted, NT) * scale_dft
     coeffs16 = coeffs.astype(BF16)
@@ -252,14 +247,30 @@
     mix_ref[...] = mix + lift[:, 2:3] * total[6:7, 0:64]
 
 
-def spectral_table(mode_index, blocks, rows):
-    place = jnp.arange(blocks * 128, dtype=jnp.int32)
-    within = place & 127
-    cell = (place >> 7) * rows + jnp.where(within >= rows, within - rows, within)
-    x_length = blocks * rows
-    phases = mode_index[:, None] * cell[None, :] % x_length
-    angles = 2.0 * jnp.pi / x_length * phases.astype(F32)
-    return jnp.concatenate([jnp.cos(angles), -jnp.sin(angles)], axis=0).astype(BF16)
+def table_kernel(blocks, rows, mode_ref, table_ref):
+    modes = mode_ref.shape[1]
+    square = (modes, modes)
+    index = jnp.where(iota(square, 0) == iota(square, 1), mode_ref[...].astype(F32), 0.0)
+    index = jnp.sum(index, axis=1, keepdims=True).astype(jnp.int32)
+    shape = (modes, 128)
+    lane = iota(shape, 1)
+    unit = 2.0 * math.pi / (blocks * rows)
+    outer = unit * (((index * lane) & (blocks - 1)) * rows).astype(F32)
+    cell = jnp.where(lane >= rows, lane - rows, lane)
+    cell = jnp.where(lane < 2 * rows, cell, 0)
+    inner = unit * (index * cell).astype(F32)
+    outer_cos, outer_sin = jnp.cos(outer), jnp.sin(outer)
+    inner_cos, inner_sin = jnp.cos(inner), jnp.sin(inner)
+    planes = [lane < rows, (lane >= rows) & (lane < 2 * rows)]
+    factors = [(jnp.where(p, inner_cos, 0.0), jnp.where(p, inner_sin, 0.0)) for p in planes]
+    for b in range(blocks):
+        cos_b = outer_cos[:, b : b + 1]
+        sin_b = outer_sin[:, b : b + 1]
+        parts = []
+        for cos_c, sin_c in factors:
+            parts.append(cos_b * cos_c - sin_b * sin_c)
+            parts.append(-(sin_b * cos_c) - cos_b * sin_c)
+        table_ref[:, b * 128 : (b + 1) * 128] = jnp.concatenate(parts, axis=0).astype(BF16)
 
 
 def local(slot_field, solid, lift_weight, spectral_weight, mix_weight, project_weight, mode_index):
@@ -298,14 +309,20 @@
     recv = lax.all_to_all(
         send.reshape(blocks, 8, 128), "gx", split_axis=0, concat_axis=0, tiled=True
     )
-    table = spectral_table(mode_index, blocks, rows)
+    table = call(
+        lambda *refs: table_kernel(blocks, rows, *refs),
+        jax.ShapeDtypeStruct((128, blocks * 128), BF16),
+        mode_index.reshape(1, -1),
+    )
+    below, above = shift(high, "gx", 1), shift(low, "gx", -1)
+    recv, below, above = lax.optimization_barrier((recv, below, above))
     new_velocity = call(
         lambda *refs: velocity_kernel(rows, *refs),
         jax.ShapeDtypeStruct((3, planes, rows, lanes), F32),
         fields,
         solid,
-        shift(high, "gx", 1),
-        shift(low, "gx", -1),
+        below,
+        above,
     )
     send = call(
         lambda *refs: line_kernel(scale_dft, loss_scale, *refs),

time: 82.6 us -> 87.1 us (1.054)
  blocking collectives: 26.7 us -> 32.4 us
  other arithmetic: 2.38 us -> 0 us
    all_to_all x1, waiting for transfers between devices: 0.01 us -> 6.48 us  [local(): lax.all_to_all(send, ('grp', 'gy'), split_axis=0, concat_axis=0, tiled=True)]
    all_to_all x1, blocking collectives: 13 us -> 18.7 us  [local(): recv = lax.all_to_all(send, 'gx', split_axis=0, concat_axis=0, tiled=True)]
    all_to_all x1, waiting for transfers between devices: 6.45 us -> 1.07 us  [local(): lax.all_to_all(send.reshape(blocks, 8, 128), 'gx', split_axis=0, concat_a...]
    another operation x1 -> x0, other arithmetic: 2.33 us -> none
    ppermute x4, waiting for transfers between devices: 5.82 us -> 4.81 us  [shift(): return lax.ppermute(array, axis, pairs)]
    pallas_call x6 -> x7, Pallas kernels: 7.25 us -> 7.84 us  [call(): pl.pallas_call(kernel, out_shape=out_shape, in_specs=[VMEM] * len(args),...]
  transfers between devices with their start and end apart: 6 -> 6, of which waited for: 3 -> 4; matrix products, arithmetic and copies ran while one was open for 3% -> 0% of each run, Pallas kernels for 1% -> 2%
where the time goes in v3:
time: 87.1 us; the launch traced here: 86.5 us
  blocking collectives  32.4 us (37%)
  starting transfers between devices  30.7 us (35%)
  waiting for transfers between devices  12.4 us (14%)
  Pallas kernels  7.84 us (9%)
  local copies, waits for them, and re-layouts  2.38 us (3%)
    all_to_all x1, blocking collectives, local(): recv = lax.all_to_all(send, 'gx', split_axis=0, concat_axis=0, tiled=True)  18.7 us
    all_gather x1, blocking collectives, local(): fields = lax.all_gather(payload, 'grp', axis=0)  13.7 us
    ppermute x4, starting transfers between devices, shift(): return lax.ppermute(array, axis, pairs)  10.5 us
    all_to_all x1, starting transfers between devices, local(): lax.all_to_all(send, ('grp', 'gy'), split_axis=0, concat_axis=0, tiled=True)  10.4 us
    all_to_all x1, starting transfers between devices, local(): lax.all_to_all(send.reshape(blocks, 8, 128), 'gx', split_axis=0, concat_a...  9.8 us
    pallas_call x7, Pallas kernels, call(): pl.pallas_call(kernel, out_shape=out_shape, in_specs=[VMEM] * len(args),...  7.84 us
    all_to_all x1, waiting for transfers between devices, local(): lax.all_to_all(send, ('grp', 'gy'), split_axis=0, concat_axis=0, tiled=True)  6.48 us
    ppermute x4, waiting for transfers between devices, shift(): return lax.ppermute(array, axis, pairs)  4.81 us
  transfers between devices with their start and end apart: 6, of which 4 were waited for; matrix products, arithmetic and copies ran while one was open for 0% of the time, Pallas kernels for 2%

profile of v3, /device:TPU:1, one launch (start us, length us, event | category | flops | bytes accessed | tf_op | source)
XLA Modules:
  0.0 86.5 jit_solution(15978834441300752217)
XLA Ops:
  0.6 0.0 copy-start.1
  0.6 0.8 copy-done.1
  1.4 0.0 copy-start.2
  1.4 0.1 shard_map.94
  1.5 4.8 %collective-permute-start = (f32[2,128]{1,0:T(2,128)S(1)}, f32[2,128]{1,0:T(2,128)S(1)}, u32[]{:S(2)}, u32[]{:S(2)}) collective-permute-start(f32[2,128]{1,0:T(2,128)S(1)} %get-tuple-element.17), channel_id=1, source_target_pairs={{0,1},{1,2},{2,3},{4,5},{5,6},{6,7},{8,9},{9,10},{10,11},{12,13},{... | collective-permute-start | bytes 3080 | tf_op jit(solution)/shard_map/ppermute | solution.py:292
  6.4 1.3 %collective-permute-start.1 = (f32[2,128]{1,0:T(2,128)S(1)}, f32[2,128]{1,0:T(2,128)S(1)}, u32[]{:S(2)}, u32[]{:S(2)}) collective-permute-start(f32[2,128]{1,0:T(2,128)S(1)} %get-tuple-element.18), channel_id=1, source_target_pairs={{1,0},{2,1},{3,2},{5,4},{6,5},{7,6},{9,8},{10,9},{11,10},{13,12},{... | collective-permute-start | bytes 3080 | tf_op jit(solution)/shard_map/ppermute | solution.py:292
  7.7 0.0 collective-permute-done
  7.7 3.6 %collective-permute-done.1 = f32[2,128]{1,0:T(2,128)S(1)} collective-permute-done((f32[2,128]{1,0:T(2,128)S(1)}, f32[2,128]{1,0:T(2,128)S(1)}, u32[]{:S(2)}, u32[]{:S(2)}) %collective-permute-start.1) | collective-permute-done | bytes 1056 | tf_op jit(solution)/shard_map/ppermute | solution.py:292
  11.3 0.0 copy-done.2
  11.4 0.0 copy-start.3
  11.4 13.7 %all-gather = f32[8,56,128]{2,1,0:T(8,128)S(1)} all-gather(f32[2,56,128]{2,1,0:T(8,128)S(1)} %concatenate.11), channel_id=2, replica_groups=mesh['grp'=4,'gx'=32,'gy'=4] {'grp'}, dimensions={0}, use_global_device_ids=true | all-gather | bytes 286720 | tf_op jit(solution)/shard_map/all_gather | solution.py:299
  25.1 0.0 copy-done.3
  25.1 1.4 %shard_map.95 = (bf16[256,128]{1,0:T(8,128)(2,1)}, f32[8,128]{1,0:T(8,128)S(1)}, f32[8,128]{1,0:T(8,128)S(1)}) custom-call(f32[4,2,56,128]{3,2,1,0:T(8,128)S(1)} %bitcast.10, s32[2,48,128]{2,1,0:T(8,128)S(1)} %copy-done.3), custom_call_target="tpu_custom_call" | custom-call | tf_op jit(solution)/shard_map/pallas_call | solution.py:32
  26.5 0.0 copy-start.6
  26.5 9.8 %all-to-all-start = ((bf16[32,8,128]{2,1,0:T(8,128)(2,1)}), bf16[32,8,128]{2,1,0:T(8,128)(2,1)S(1)}, u32[]{:S(2)}, u32[]{:S(2)}) async-start(bf16[32,8,128]{2,1,0:T(8,128)(2,1)} %bitcast.4), calls=%async_computation | async-start | bytes 131072 | tf_op jit(solution)/shard_map/all_to_all | solution.py:309
  36.3 3.1 %collective-permute-start.2 = (f32[8,128]{1,0:T(8,128)S(1)}, f32[8,128]{1,0:T(8,128)S(1)}, u32[]{:S(2)}, u32[]{:S(2)}) collective-permute-start(f32[8,128]{1,0:T(8,128)S(1)} %get-tuple-element.23), channel_id=1, source_target_pairs={{0,4},{4,8},{8,12},{12,16},{16,20},{20,24},{24,28},{28,32},{32,36}... | collective-permute-start | bytes 12296 | tf_op jit(solution)/shard_map/ppermute | solution.py:292
  39.4 1.3 %collective-permute-start.3 = (f32[8,128]{1,0:T(8,128)S(1)}, f32[8,128]{1,0:T(8,128)S(1)}, u32[]{:S(2)}, u32[]{:S(2)}) collective-permute-start(f32[8,128]{1,0:T(8,128)S(1)} %get-tuple-element.24), channel_id=1, source_target_pairs={{4,0},{8,4},{12,8},{16,12},{20,16},{24,20},{28,24},{32,28},{36,32}... | collective-permute-start | bytes 12296 | tf_op jit(solution)/shard_map/ppermute | solution.py:292
  40.7 0.0 copy-done.6
  40.8 0.0 copy-start.7
  40.8 0.0 copy-start.5
  40.8 0.1 copy.16
  40.9 0.5 copy-done.7
  41.4 0.1 copy.13
  41.5 0.0 copy-done.5
  41.6 0.1 copy.14
  41.7 0.0 copy-start.4
  41.7 0.6 copy-done.4
  42.3 0.0 copy-start
  42.3 0.6 shard_map.97.refs_1_
  42.9 0.0 collective-permute-done.2.refs_2_
  42.9 1.2 %collective-permute-done.3.refs_3_ = f32[8,128]{1,0:T(8,128)S(1)} collective-permute-done((f32[8,128]{1,0:T(8,128)S(1)}, f32[8,128]{1,0:T(8,128)S(1)}, u32[]{:S(2)}, u32[]{:S(2)}) %collective-permute-start.3) | collective-permute-done | bytes 4128 | tf_op jit(solution)/shard_map/ppermute | solution.py:292
  44.1 1.1 %all-to-all-done.refs_0_ = bf16[32,8,128]{2,1,0:T(8,128)(2,1)S(1)} async-done(((bf16[32,8,128]{2,1,0:T(8,128)(2,1)}), bf16[32,8,128]{2,1,0:T(8,128)(2,1)S(1)}, u32[]{:S(2)}, u32[]{:S(2)}) %all-to-all-start) | async-done | bytes 65568 | tf_op jit(solution)/shard_map/all_to_all | solution.py:309
  45.1 0.0 copy-done
  45.2 3.0 %shard_map.98 = bf16[32,24,128]{2,1,0:T(8,128)(2,1)S(1)} custom-call(bf16[32,8,128]{2,1,0:T(8,128)(2,1)S(1)} %all-to-all-done.refs_0_, bf16[128,4096]{1,0:T(8,128)(2,1)S(1)} %shard_map.97.refs_1_, bf16[64,8]{1,0:T(8,128)(2,1)S(1)} %pad.7.refs_2_.lift_ref, bf16[64,64]{1,0:T(8,128)(2,1)S(1)} %bitcast.14, bf16[2048,128]{1,0:T(8,128)(2,1)S(1)} %copy-done, ...), custom_call_target="tpu_custom_call" | custom-call | tf_op jit(solution)/shard_map/pallas_call | solution.py:32
  48.1 18.7 %all_to_all.15.recv_ref = bf16[32,24,128]{2,1,0:T(8,128)(2,1)S(1)} all-to-all(bf16[32,24,128]{2,1,0:T(8,128)(2,1)S(1)} %shard_map.98), channel_id=1, replica_groups=mesh['grp'=4,'gx'=32,'gy'=4] {'gx'}, dimensions={0} | all-to-all | bytes 393216 | tf_op jit(solution)/shard_map/all_to_all | solution.py:339
  66.8 1.0 %shard_map.99 = f32[16,8,128]{2,1,0:T(8,128)} custom-call(bf16[32,24,128]{2,1,0:T(8,128)(2,1)S(1)} %all_to_all.15.recv_ref), custom_call_target="tpu_custom_call" | custom-call | tf_op jit(solution)/shard_map/pallas_call | solution.py:32
  67.8 10.4 %all-to-all-start.2 = ((f32[16,8,128]{2,1,0:T(8,128)}), f32[16,8,128]{2,1,0:T(8,128)S(1)}, u32[]{:S(2)}, u32[]{:S(2)}) async-start(f32[16,8,128]{2,1,0:T(8,128)} %shard_map.99), calls=%async_computation.2 | async-start | bytes 131072 | tf_op jit(solution)/shard_map/all_to_all | solution.py:346
  78.2 1.1 %shard_map.96 = f32[3,2,48,128]{3,2,1,0:T(8,128)} custom-call(f32[4,2,56,128]{3,2,1,0:T(8,128)S(1)} %bitcast.11, s32[2,48,128]{2,1,0:T(8,128)S(1)} %copy-done.3, f32[8,128]{1,0:T(8,128)S(1)} %collective-permute-done.2.refs_2_, f32[8,128]{1,0:T(8,128)S(1)} %collective-permute-done.3.refs_3_), custom_call_target="tpu_custom_call" | custom-call | tf_op jit(solution)/shard_map/pallas_call | solution.py:32
  79.3 6.5 %all-to-all-done.2.recv_ref = f32[16,8,128]{2,1,0:T(8,128)S(1)} async-done(((f32[16,8,128]{2,1,0:T(8,128)}), f32[16,8,128]{2,1,0:T(8,128)S(1)}, u32[]{:S(2)}, u32[]{:S(2)}) %all-to-all-start.2) | async-done | bytes 65568 | tf_op jit(solution)/shard_map/all_to_all | solution.py:346
  85.8 0.7 shard_map.100
  (6 shorter events, 0.1 us)
Async XLA Ops:
  0.6 0.8 copy-start.1
  1.4 9.9 %copy-start.2 = (f32[1,2,48,128]{3,2,1,0:T(8,128)S(1)}, f32[1,2,48,128]{3,2,1,0:T(8,128)}, u32[]{:S(2)}) copy-start(f32[1,2,48,128]{3,2,1,0:T(8,128)} %param.7) | copy-start | bytes 147460
  1.5 6.1 %collective-permute-start = (f32[2,128]{1,0:T(2,128)S(1)}, f32[2,128]{1,0:T(2,128)S(1)}, u32[]{:S(2)}, u32[]{:S(2)}) collective-permute-start(f32[2,128]{1,0:T(2,128)S(1)} %get-tuple-element.17), channel_id=1, source_target_pairs={{0,1},{1,2},{2,3},{4,5},{5,6},{6,7},{8,9},{9,10},{10,11},{12,13},{... | collective-permute-start | bytes 3080 | tf_op jit(solution)/shard_map/ppermute | solution.py:292
  6.4 5.0 %collective-permute-start.1 = (f32[2,128]{1,0:T(2,128)S(1)}, f32[2,128]{1,0:T(2,128)S(1)}, u32[]{:S(2)}, u32[]{:S(2)}) collective-permute-start(f32[2,128]{1,0:T(2,128)S(1)} %get-tuple-element.18), channel_id=1, source_target_pairs={{1,0},{2,1},{3,2},{5,4},{6,5},{7,6},{9,8},{10,9},{11,10},{13,12},{... | collective-permute-start | bytes 3080 | tf_op jit(solution)/shard_map/ppermute | solution.py:292
  11.4 13.7 %copy-start.3 = (s32[2,48,128]{2,1,0:T(8,128)S(1)}, s32[2,48,128]{2,1,0:T(8,128)}, u32[]{:S(2)}) copy-start(s32[2,48,128]{2,1,0:T(8,128)} %refs_1_.3) | copy-start | bytes 147460
  26.5 14.3 %copy-start.6 = (bf16[64,3]{0,1:T(4,128)(2,1)S(1)}, bf16[64,3]{0,1:T(4,128)(2,1)}, u32[]{:S(2)}) copy-start(bf16[64,3]{0,1:T(4,128)(2,1)} %param.12) | copy-start | bytes 1156
  26.5 18.7 %all-to-all-start = ((bf16[32,8,128]{2,1,0:T(8,128)(2,1)}), bf16[32,8,128]{2,1,0:T(8,128)(2,1)S(1)}, u32[]{:S(2)}, u32[]{:S(2)}) async-start(bf16[32,8,128]{2,1,0:T(8,128)(2,1)} %bitcast.4), calls=%async_computation | async-start | bytes 131072 | tf_op jit(solution)/shard_map/all_to_all | solution.py:309
  36.3 6.6 %collective-permute-start.2 = (f32[8,128]{1,0:T(8,128)S(1)}, f32[8,128]{1,0:T(8,128)S(1)}, u32[]{:S(2)}, u32[]{:S(2)}) collective-permute-start(f32[8,128]{1,0:T(8,128)S(1)} %get-tuple-element.23), channel_id=1, source_target_pairs={{0,4},{4,8},{8,12},{12,16},{16,20},{20,24},{24,28},{28,32},{32,36}... | collective-permute-start | bytes 12296 | tf_op jit(solution)/shard_map/ppermute | solution.py:292
  39.4 4.6 %collective-permute-start.3 = (f32[8,128]{1,0:T(8,128)S(1)}, f32[8,128]{1,0:T(8,128)S(1)}, u32[]{:S(2)}, u32[]{:S(2)}) collective-permute-start(f32[8,128]{1,0:T(8,128)S(1)} %get-tuple-element.24), channel_id=1, source_target_pairs={{4,0},{8,4},{12,8},{16,12},{20,16},{24,20},{28,24},{32,28},{36,32}... | collective-permute-start | bytes 12296 | tf_op jit(solution)/shard_map/ppermute | solution.py:292
  40.8 0.7 copy-start.7
  40.8 0.8 copy-start.5
  41.7 0.7 copy-start.4
  42.3 2.8 %copy-start = (bf16[2048,128]{1,0:T(8,128)(2,1)S(1)}, bf16[2048,128]{1,0:T(8,128)(2,1)}, u32[]{:S(2)}) copy-start(bf16[2048,128]{1,0:T(8,128)(2,1)} %refs_4_.1) | copy-start | bytes 1572868
  67.8 17.9 %all-to-all-start.2 = ((f32[16,8,128]{2,1,0:T(8,128)}), f32[16,8,128]{2,1,0:T(8,128)S(1)}, u32[]{:S(2)}, u32[]{:S(2)}) async-start(f32[16,8,128]{2,1,0:T(8,128)} %shard_map.99), calls=%async_computation.2 | async-start | bytes 131072 | tf_op jit(solution)/shard_map/all_to_all | solution.py:346

commit v4 on v3

--- a/solution.py
+++ b/solution.py
@@ -60,7 +60,7 @@
         tile = centre[f][z]
         below = above = 0.0
         if rims is not None:
-            below, above = (ref[2 * f + z : 2 * f + z + 1, :] for ref in rims)
+            below, above = (rim[2 * f + z : 2 * f + z + 1, :] for rim in rims)
         x_down = jnp.where(row == 0, below, pltpu.roll(tile, 1, 0))
         x_up = jnp.where(row == rows - 1, above, pltpu.roll(tile, rows - 1, 0))
         sides = []
@@ -94,27 +94,41 @@
     return results
 
 
-def source_kernel(rows, fields_ref, solid_ref, send_ref, low_ref, high_ref):
+def source_kernel(rows, fields_ref, solid_ref, send_ref, rim_ref):
+    blocks = send_ref.shape[0]
     lanes = fields_ref.shape[3]
     role = lax.axis_index("grp")
+    own = lax.axis_index("gx")
     results = section(rows, fields_ref, solid_ref, None)
     for f in range(4):
         for z in range(2):
-            low_ref[2 * f + z : 2 * f + z + 1, :] = fields_ref[f, z, 0:1, :]
-            high_ref[2 * f + z : 2 * f + z + 1, :] = fields_ref[f, z, rows - 1 : rows, :]
+            for k, row in ((0, 0), (1, rows - 1)):
+                rim_ref[k, 2 * f + z : 2 * f + z + 1, :] = fields_ref[f, z, row : row + 1, :]
+    rims = []
+    for k in range(2):
+        high = rim_ref[k].astype(BF16).astype(F32)
+        rims.append(jnp.concatenate([high, rim_ref[k] - high], axis=0))
     values = [jnp.concatenate([p.astype(BF16) for p in parts], axis=1) for parts in results]
     pad = jnp.zeros((128 - 2 * rows, 8 * lanes), BF16)
     stacked = jnp.concatenate(values + [pad], axis=0)
-    count = send_ref.shape[0]
-    out_row = iota((count, 8 * lanes), 0)
-    column = iota((count, 8 * lanes), 1)
-    wanted = (out_row & 7) * lanes + (out_row >> 3) + role * (count // 8)
-    pick = jnp.where(column == wanted, 1.0, 0.0).astype(BF16)
-    send_ref[...] = dot(pick, stacked, NT).astype(BF16)
-
-
-def velocity_kernel(rows, fields_ref, solid_ref, below_ref, above_ref, new_ref):
-    results = section(rows, fields_ref, solid_ref, (below_ref, above_ref))
+    shape = (blocks * 8, 8 * lanes)
+    out_row = iota(shape, 0)
+    wanted = (out_row & 7) * lanes + (out_row >> 3) + role * blocks
+    pick = jnp.where(iota(shape, 1) == wanted, 1.0, 0.0).astype(BF16)
+    lines = dot(pick, stacked, NT)
+    for b in range(blocks):
+        rim = jnp.where(b > own, rims[1], rims[0])
+        send_ref[b] = jnp.concatenate([lines[8 * b : 8 * b + 8], rim], axis=0).astype(BF16)
+
+
+def velocity_kernel(rows, fields_ref, solid_ref, recv_ref, new_ref):
+    last = recv_ref.shape[0] - 1
+    own = lax.axis_index("gx")
+    rims = []
+    for index, inside in ((own - 1, own > 0), (own + 1, own < last)):
+        message = recv_ref[jnp.minimum(jnp.maximum(index, 0), last)].astype(F32)
+        rims.append(jnp.where(inside, message[8:16] + message[16:24], 0.0))
+    results = section(rows, fields_ref, solid_ref, rims)
     for z in range(2):
         for f in range(3):
             new_ref[f, z] = results[z][3 + f]
@@ -142,7 +156,7 @@
     blocks = recv_ref.shape[0]
     cells = blocks * 128
     rows = 48
-    lines = jnp.concatenate([recv_ref[b] for b in range(blocks)], axis=1)
+    lines = jnp.concatenate([recv_ref[b, 0:8, :] for b in range(blocks)], axis=1)
     both = table_ref[...]
     lifted = dot(lift_ref[...], lines, NN).astype(BF16)
     coeffs = dot(both, lifted, NT) * scale_dft
@@ -298,31 +312,26 @@
     payload = jnp.concatenate([tile, rims], axis=1)
     fields = lax.all_gather(payload, "grp", axis=0)
 
-    rim = jax.ShapeDtypeStruct((8, lanes), F32)
-    send, low, high = call(
+    send = call(
         lambda *refs: source_kernel(rows, *refs),
-        [jax.ShapeDtypeStruct((blocks * 8, 128), BF16), rim, rim],
+        jax.ShapeDtypeStruct((blocks, 24, 128), BF16),
         fields,
         solid,
-    )
-    mode_index, low, high, send = lax.optimization_barrier((mode_index, low, high, send))
-    recv = lax.all_to_all(
-        send.reshape(blocks, 8, 128), "gx", split_axis=0, concat_axis=0, tiled=True
-    )
+        scratch=[pltpu.VMEM((2, 8, lanes), F32)],
+    )
+    mode_index, send = lax.optimization_barrier((mode_index, send))
+    recv = lines = lax.all_to_all(send, "gx", split_axis=0, concat_axis=0, tiled=True)
     table = call(
         lambda *refs: table_kernel(blocks, rows, *refs),
         jax.ShapeDtypeStruct((128, blocks * 128), BF16),
         mode_index.reshape(1, -1),
     )
-    below, above = shift(high, "gx", 1), shift(low, "gx", -1)
-    recv, below, above = lax.optimization_barrier((recv, below, above))
     new_velocity = call(
         lambda *refs: velocity_kernel(rows, *refs),
         jax.ShapeDtypeStruct((3, planes, rows, lanes), F32),
         fields,
         solid,
-        below,
-        above,
+        lines,
     )
     send = call(
         lambda *refs: line_kernel(scale_dft, loss_scale, *refs),

time: 87.1 us -> 83.6 us (0.960)
  starting transfers between devices: 30.7 us -> 26.2 us
  waiting for transfers between devices: 12.4 us -> 16.7 us
  blocking collectives: 32.4 us -> 28.5 us
    all_to_all x1, waiting for transfers between devices: 1.07 us -> 6.61 us  [local(): lax.all_to_all(send, 'gx', split_axis=0, concat_axis=0, tiled=True)]
    ppermute x4 -> x2, starting transfers between devices: 10.5 us -> 6.12 us  [shift(): return lax.ppermute(array, axis, pairs)]
    all_to_all x1, blocking collectives: 18.7 us -> 14.8 us  [local(): recv = lax.all_to_all(send, 'gx', split_axis=0, concat_axis=0, tiled=True)]
    ppermute x4 -> x2, waiting for transfers between devices: 4.81 us -> 3.65 us  [shift(): return lax.ppermute(array, axis, pairs)]
  transfers between devices with their start and end apart: 6 -> 4, of which waited for: 4 -> 3; matrix products, arithmetic and copies ran while one was open for 0% -> 0% of each run, Pallas kernels for 2% -> 2%
where the time goes in v4:
time: 83.6 us; the launch traced here: 83 us
  blocking collectives  28.5 us (34%)
  starting transfers between devices  26.2 us (31%)
  waiting for transfers between devices  16.7 us (20%)
  Pallas kernels  7.88 us (9%)
  local copies, waits for them, and re-layouts  3.01 us (4%)
    all_to_all x1, blocking collectives, local(): recv = lax.all_to_all(send, 'gx', split_axis=0, concat_axis=0, tiled=True)  14.8 us
    all_gather x1, blocking collectives, local(): fields = lax.all_gather(payload, 'grp', axis=0)  13.7 us
    all_to_all x1, starting transfers between devices, local(): lax.all_to_all(send, ('grp', 'gy'), split_axis=0, concat_axis=0, tiled=True)  10.3 us
    all_to_all x1, starting transfers between devices, local(): lax.all_to_all(send, 'gx', split_axis=0, concat_axis=0, tiled=True)  9.8 us
    pallas_call x7, Pallas kernels, call(): pl.pallas_call(kernel, out_shape=out_shape, in_specs=[VMEM] * len(args),...  7.88 us
    all_to_all x1, waiting for transfers between devices, local(): lax.all_to_all(send, 'gx', split_axis=0, concat_axis=0, tiled=True)  6.61 us
    all_to_all x1, waiting for transfers between devices, local(): lax.all_to_all(send, ('grp', 'gy'), split_axis=0, concat_axis=0, tiled=True)  6.48 us
    ppermute x2, starting transfers between devices, shift(): return lax.ppermute(array, axis, pairs)  6.12 us
  transfers between devices with their start and end apart: 4, of which 3 were waited for; matrix products, arithmetic and copies ran while one was open for 0% of the time, Pallas kernels for 2%

profile of v4, /device:TPU:1, one launch (start us, length us, event | category | flops | bytes accessed | tf_op | source)
XLA Modules:
  0.0 83.0 jit_solution(10006962402301430857)
XLA Ops:
  0.6 0.0 copy-start.2
  0.6 0.8 copy-done.2
  1.4 0.0 copy-start.3
  1.4 0.1 shard_map.94
  1.5 4.8 %collective-permute-start = (f32[2,128]{1,0:T(2,128)S(1)}, f32[2,128]{1,0:T(2,128)S(1)}, u32[]{:S(2)}, u32[]{:S(2)}) collective-permute-start(f32[2,128]{1,0:T(2,128)S(1)} %get-tuple-element.9), channel_id=1, source_target_pairs={{0,1},{1,2},{2,3},{4,5},{5,6},{6,7},{8,9},{9,10},{10,11},{12,13},{... | collective-permute-start | bytes 3080 | tf_op jit(solution)/shard_map/ppermute | solution.py:306
  6.4 1.3 %collective-permute-start.1 = (f32[2,128]{1,0:T(2,128)S(1)}, f32[2,128]{1,0:T(2,128)S(1)}, u32[]{:S(2)}, u32[]{:S(2)}) collective-permute-start(f32[2,128]{1,0:T(2,128)S(1)} %get-tuple-element.10), channel_id=1, source_target_pairs={{1,0},{2,1},{3,2},{5,4},{6,5},{7,6},{9,8},{10,9},{11,10},{13,12},{... | collective-permute-start | bytes 3080 | tf_op jit(solution)/shard_map/ppermute | solution.py:306
  7.7 0.0 collective-permute-done
  7.7 3.6 %collective-permute-done.1 = f32[2,128]{1,0:T(2,128)S(1)} collective-permute-done((f32[2,128]{1,0:T(2,128)S(1)}, f32[2,128]{1,0:T(2,128)S(1)}, u32[]{:S(2)}, u32[]{:S(2)}) %collective-permute-start.1) | collective-permute-done | bytes 1056 | tf_op jit(solution)/shard_map/ppermute | solution.py:306
  11.3 0.0 copy-done.3
  11.4 0.0 copy-start.1
  11.4 13.7 %all-gather = f32[8,56,128]{2,1,0:T(8,128)S(1)} all-gather(f32[2,56,128]{2,1,0:T(8,128)S(1)} %concatenate.11), channel_id=2, replica_groups=mesh['grp'=4,'gx'=32,'gy'=4] {'grp'}, dimensions={0}, use_global_device_ids=true | all-gather | bytes 286720 | tf_op jit(solution)/shard_map/all_gather | solution.py:313
  25.1 0.0 copy-done.1
  25.1 1.5 %shard_map.95 = bf16[32,24,128]{2,1,0:T(8,128)(2,1)} custom-call(f32[4,2,56,128]{3,2,1,0:T(8,128)S(1)} %bitcast.9, s32[2,48,128]{2,1,0:T(8,128)S(1)} %copy-done.1), custom_call_target="tpu_custom_call" | custom-call | tf_op jit(solution)/shard_map/pallas_call | solution.py:32
  26.5 0.0 copy-start.7
  26.5 9.8 %all-to-all-start = ((bf16[32,24,128]{2,1,0:T(8,128)(2,1)}), bf16[32,24,128]{2,1,0:T(8,128)(2,1)S(1)}, u32[]{:S(2)}, u32[]{:S(2)}) async-start(bf16[32,24,128]{2,1,0:T(8,128)(2,1)} %shard_map.95), calls=%async_computation | async-start | bytes 393216 | tf_op jit(solution)/shard_map/all_to_all | solution.py:323
  36.3 0.0 copy-done.7
  36.4 0.0 copy-start.5
  36.4 0.1 copy.13
  36.5 0.6 copy-done.5
  37.1 0.0 copy-start.6
  37.1 0.1 copy.14
  37.2 0.6 copy-done.6
  37.8 0.1 copy.16
  37.9 0.0 copy-start.4
  37.9 0.6 copy-done.4
  38.6 0.0 copy-start
  38.6 0.6 shard_map.97.refs_1_
  39.1 6.6 %all-to-all-done.refs_2_.refs_0_ = bf16[32,24,128]{2,1,0:T(8,128)(2,1)S(1)} async-done(((bf16[32,24,128]{2,1,0:T(8,128)(2,1)}), bf16[32,24,128]{2,1,0:T(8,128)(2,1)S(1)}, u32[]{:S(2)}, u32[]{:S(2)}) %all-to-all-start) | async-done | bytes 196640 | tf_op jit(solution)/shard_map/all_to_all | solution.py:323
  45.7 0.0 copy-done
  45.8 3.0 %shard_map.98 = bf16[32,24,128]{2,1,0:T(8,128)(2,1)S(1)} custom-call(bf16[32,24,128]{2,1,0:T(8,128)(2,1)S(1)} %all-to-all-done.refs_2_.refs_0_, bf16[128,4096]{1,0:T(8,128)(2,1)S(1)} %shard_map.97.refs_1_, bf16[64,8]{1,0:T(8,128)(2,1)S(1)} %pad.7.refs_2_.lift_ref, bf16[64,64]{1,0:T(8,128)(2,1)S(1)} %bitcast.13, bf16[2048,128]{1,0:T(8,128)(2,1)S(1)} %copy-done, ...), custom_call_target="tpu_custom_call" | custom-call | tf_op jit(solution)/shard_map/pallas_call | solution.py:32
  48.7 14.8 %all_to_all.15.recv_ref = bf16[32,24,128]{2,1,0:T(8,128)(2,1)S(1)} all-to-all(bf16[32,24,128]{2,1,0:T(8,128)(2,1)S(1)} %shard_map.98), channel_id=1, replica_groups=mesh['grp'=4,'gx'=32,'gy'=4] {'gx'}, dimensions={0} | all-to-all | bytes 393216 | tf_op jit(solution)/shard_map/all_to_all | solution.py:348
  63.5 1.0 %shard_map.99 = f32[16,8,128]{2,1,0:T(8,128)} custom-call(bf16[32,24,128]{2,1,0:T(8,128)(2,1)S(1)} %all_to_all.15.recv_ref), custom_call_target="tpu_custom_call" | custom-call | tf_op jit(solution)/shard_map/pallas_call | solution.py:32
  64.5 10.3 %all-to-all-start.2 = ((f32[16,8,128]{2,1,0:T(8,128)}), f32[16,8,128]{2,1,0:T(8,128)S(1)}, u32[]{:S(2)}, u32[]{:S(2)}) async-start(f32[16,8,128]{2,1,0:T(8,128)} %shard_map.99), calls=%async_computation.2 | async-start | bytes 131072 | tf_op jit(solution)/shard_map/all_to_all | solution.py:355
  74.7 1.1 %shard_map.96 = f32[3,2,48,128]{3,2,1,0:T(8,128)} custom-call(f32[4,2,56,128]{3,2,1,0:T(8,128)S(1)} %bitcast.10, s32[2,48,128]{2,1,0:T(8,128)S(1)} %copy-done.1, bf16[32,24,128]{2,1,0:T(8,128)(2,1)S(1)} %all-to-all-done.refs_2_.refs_0_), custom_call_target="tpu_custom_call" | custom-call | tf_op jit(solution)/shard_map/pallas_call | solution.py:32
  75.8 6.5 %all-to-all-done.2.recv_ref = f32[16,8,128]{2,1,0:T(8,128)S(1)} async-done(((f32[16,8,128]{2,1,0:T(8,128)}), f32[16,8,128]{2,1,0:T(8,128)S(1)}, u32[]{:S(2)}, u32[]{:S(2)}) %all-to-all-start.2) | async-done | bytes 65568 | tf_op jit(solution)/shard_map/all_to_all | solution.py:355
  82.3 0.7 shard_map.100
  (6 shorter events, 0.1 us)
Async XLA Ops:
  0.6 0.8 copy-start.2
  1.4 9.9 %copy-start.3 = (f32[1,2,48,128]{3,2,1,0:T(8,128)S(1)}, f32[1,2,48,128]{3,2,1,0:T(8,128)}, u32[]{:S(2)}) copy-start(f32[1,2,48,128]{3,2,1,0:T(8,128)} %param.7) | copy-start | bytes 147460
  1.5 6.1 %collective-permute-start = (f32[2,128]{1,0:T(2,128)S(1)}, f32[2,128]{1,0:T(2,128)S(1)}, u32[]{:S(2)}, u32[]{:S(2)}) collective-permute-start(f32[2,128]{1,0:T(2,128)S(1)} %get-tuple-element.9), channel_id=1, source_target_pairs={{0,1},{1,2},{2,3},{4,5},{5,6},{6,7},{8,9},{9,10},{10,11},{12,13},{... | collective-permute-start | bytes 3080 | tf_op jit(solution)/shard_map/ppermute | solution.py:306
  6.4 5.0 %collective-permute-start.1 = (f32[2,128]{1,0:T(2,128)S(1)}, f32[2,128]{1,0:T(2,128)S(1)}, u32[]{:S(2)}, u32[]{:S(2)}) collective-permute-start(f32[2,128]{1,0:T(2,128)S(1)} %get-tuple-element.10), channel_id=1, source_target_pairs={{1,0},{2,1},{3,2},{5,4},{6,5},{7,6},{9,8},{10,9},{11,10},{13,12},{... | collective-permute-start | bytes 3080 | tf_op jit(solution)/shard_map/ppermute | solution.py:306
  11.4 13.7 %copy-start.1 = (s32[2,48,128]{2,1,0:T(8,128)S(1)}, s32[2,48,128]{2,1,0:T(8,128)}, u32[]{:S(2)}) copy-start(s32[2,48,128]{2,1,0:T(8,128)} %refs_1_.3) | copy-start | bytes 147460
  26.5 9.8 %copy-start.7 = (bf16[3,64]{1,0:T(4,128)(2,1)S(1)}, bf16[3,64]{1,0:T(4,128)(2,1)}, u32[]{:S(2)}) copy-start(bf16[3,64]{1,0:T(4,128)(2,1)} %param.9) | copy-start | bytes 1156
  26.5 19.2 %all-to-all-start = ((bf16[32,24,128]{2,1,0:T(8,128)(2,1)}), bf16[32,24,128]{2,1,0:T(8,128)(2,1)S(1)}, u32[]{:S(2)}, u32[]{:S(2)}) async-start(bf16[32,24,128]{2,1,0:T(8,128)(2,1)} %shard_map.95), calls=%async_computation | async-start | bytes 393216 | tf_op jit(solution)/shard_map/all_to_all | solution.py:323
  36.4 0.7 copy-start.5
  37.1 0.7 copy-start.6
  37.9 0.7 copy-start.4
  38.6 7.2 %copy-start = (bf16[2048,128]{1,0:T(8,128)(2,1)S(1)}, bf16[2048,128]{1,0:T(8,128)(2,1)}, u32[]{:S(2)}) copy-start(bf16[2048,128]{1,0:T(8,128)(2,1)} %refs_4_.1) | copy-start | bytes 1572868
  64.5 17.9 %all-to-all-start.2 = ((f32[16,8,128]{2,1,0:T(8,128)}), f32[16,8,128]{2,1,0:T(8,128)S(1)}, u32[]{:S(2)}, u32[]{:S(2)}) async-start(f32[16,8,128]{2,1,0:T(8,128)} %shard_map.99), calls=%async_computation.2 | async-start | bytes 131072 | tf_op jit(solution)/shard_map/all_to_all | solution.py:355

commit v5 on v4

--- a/solution.py
+++ b/solution.py
@@ -104,10 +104,7 @@
         for z in range(2):
             for k, row in ((0, 0), (1, rows - 1)):
                 rim_ref[k, 2 * f + z : 2 * f + z + 1, :] = fields_ref[f, z, row : row + 1, :]
-    rims = []
-    for k in range(2):
-        high = rim_ref[k].astype(BF16).astype(F32)
-        rims.append(jnp.concatenate([high, rim_ref[k] - high], axis=0))
+    rims = [rim_ref[k] for k in range(2)]
     values = [jnp.concatenate([p.astype(BF16) for p in parts], axis=1) for parts in results]
     pad = jnp.zeros((128 - 2 * rows, 8 * lanes), BF16)
     stacked = jnp.concatenate(values + [pad], axis=0)
@@ -119,19 +116,6 @@
     for b in range(blocks):
         rim = jnp.where(b > own, rims[1], rims[0])
         send_ref[b] = jnp.concatenate([lines[8 * b : 8 * b + 8], rim], axis=0).astype(BF16)
-
-
-def velocity_kernel(rows, fields_ref, solid_ref, recv_ref, new_ref):
-    last = recv_ref.shape[0] - 1
-    own = lax.axis_index("gx")
-    rims = []
-    for index, inside in ((own - 1, own > 0), (own + 1, own < last)):
-        message = recv_ref[jnp.minimum(jnp.maximum(index, 0), last)].astype(F32)
-        rims.append(jnp.where(inside, message[8:16] + message[16:24], 0.0))
-    results = section(rows, fields_ref, solid_ref, rims)
-    for z in range(2):
-        for f in range(3):
-            new_ref[f, z] = results[z][3 + f]
 
 
 def neighbour_terms(lines, rows):
@@ -150,15 +134,16 @@
 
 
 def line_kernel(
-    scale_dft, loss_scale, recv_ref, table_ref, lift_ref, mix_ref, weight_ref, proj_ref, projt_ref,
-    send_ref, back_ref, coef_ref,
+    scale_dft, loss_scale, recv_ref, table_ref, small_ref, mix_ref, weight_ref, send_ref, back_ref,
+    coef_ref,
 ):
     blocks = recv_ref.shape[0]
     cells = blocks * 128
     rows = 48
     lines = jnp.concatenate([recv_ref[b, 0:8, :] for b in range(blocks)], axis=1)
     both = table_ref[...]
-    lifted = dot(lift_ref[...], lines, NN).astype(BF16)
+    lift, proj = small_ref[0:8, :], small_ref[8:16, :]
+    lifted = dot(lift, lines, TN).astype(BF16)
     coeffs = dot(both, lifted, NT) * scale_dft
     coeffs16 = coeffs.astype(BF16)
     wide = jnp.concatenate([coeffs16] * 32, axis=1)
@@ -175,22 +160,21 @@
         parts.append(turned[real] + product[imag])
     mixed = jnp.concatenate(parts, axis=0)
     mixed_t = jnp.transpose(mixed)[0:64].astype(BF16)
-    hidden = dot(mixed_t, both, NN) * (2.0 * scale_dft) + dot(mix_ref[...], lifted, NN)
+    hidden = dot(mixed_t, both, NN) * (2.0 * scale_dft) + dot(mix_ref[...], lifted, TN)
     square = hidden * hidden
     inner = GELU_A * (hidden + GELU_B * (square * hidden))
     tanh = jnp.tanh(inner)
     half = 0.5 * (1.0 + tanh)
     active = (hidden * half).astype(BF16)
     slope = half + (0.5 * GELU_A) * hidden * (1.0 - tanh * tanh) * (1.0 + (3.0 * GELU_B) * square)
-    predicted = dot(projt_ref[...], active, NN)
+    predicted = dot(proj, active, NN)
     wide_lines = lines.astype(F32)
     target = pltpu.roll(wide_lines, 5, 0) + neighbour_terms(wide_lines, rows)
     misfit = (predicted - target) * loss_scale
     misfit = jnp.where(iota(misfit.shape, 0) < 3, misfit, 0.0)
     high = misfit.astype(BF16)
     low = (misfit - high.astype(F32)).astype(BF16)
-    proj = proj_ref[...]
-    back = slope * (dot(proj, high, NN) + dot(proj, low, NN))
+    back = slope * (dot(proj, high, TN) + dot(proj, low, TN))
     back16 = back.astype(BF16)
     mix_terms = dot(lines, back16, NT)
     back_mixed = dot(both, back16, NT) * (2.0 * scale_dft)
@@ -198,22 +182,24 @@
     coef_ref[...] = jnp.concatenate([coeffs[0:64], coeffs[64:128]], axis=1)
     mix_high = mix_terms.astype(BF16)
     mix_low = (mix_terms - mix_high.astype(F32)).astype(BF16)
-    tail = jnp.concatenate([mix_high, mix_low], axis=1)
+    tail = jnp.concatenate([mix_high, mix_low], axis=1).astype(F32)[0:4]
+    lane = iota((4, 128), 1) & 63
     for j in range(8):
-        chunk = jnp.concatenate(
-            [
-                back_ref[pl.ds(j, 8, stride=8), :],
-                coef_ref[pl.ds(j, 8, stride=8), :],
-                tail.astype(F32),
-            ],
-            axis=0,
-        ).astype(BF16)
-        for q in range(4):
-            send_ref[4 * j + q] = chunk
+        back_j = back_ref[pl.ds(j, 8, stride=8), :]
+        coef_j = coef_ref[pl.ds(j, 8, stride=8), :]
+        real, imag = coef_j[0:4], coef_j[4:8]
+        halves = (
+            jnp.where(lane < 32, real, pltpu.roll(imag, 32, 1)),
+            jnp.where(lane < 32, pltpu.roll(real, 96, 1), imag),
+        )
+        for k, half in enumerate(halves):
+            chunk = jnp.concatenate([back_j, half, tail], axis=0).astype(BF16)
+            send_ref[4 * j + 2 * k] = chunk
+            send_ref[4 * j + 2 * k + 1] = chunk
 
 
 def grad_kernel(recv_ref, send_ref, wide_ref, grad_ref):
-    quarter = lax.rem(lax.axis_index("gx"), 4)
+    side = lax.rem(lax.axis_index("gx"), 2)
     blocks, height = recv_ref.shape[:2]
     for b in range(blocks):
         wide_ref[b * height : (b + 1) * height, :] = recv_ref[b].astype(F32)
@@ -221,27 +207,22 @@
     def rows(k):
         return wide_ref[pl.ds(k, blocks, stride=height), :]
 
+    lane = iota((32, 128), 1)
     for g in range(4):
-        back_re, back_im, coef_re, coef_im = rows(g), rows(4 + g), rows(8 + g), rows(12 + g)
-        outs = []
-        for left, right in (
-            ([coef_re, coef_im], [back_re, back_im]),
-            ([coef_re, -coef_im], [back_im, back_re]),
-        ):
-            left = jnp.concatenate(left, axis=0).astype(BF16)
-            right = jnp.concatenate(right, axis=0).astype(BF16)
-            outs.append(dot(left, right, TN))
-        real, imag = outs
-        lane = iota(real.shape, 1)
-        low = jnp.where(lane < 64, real, pltpu.roll(imag, 64, 1))
-        high = jnp.where(lane < 64, pltpu.roll(real, 64, 1), imag)
-        grad_ref[g] = low[0:64] + high[64:128]
+        coef = rows(8 + g).astype(BF16)
+        by_real = dot(coef, rows(g).astype(BF16), TN)
+        by_imag = dot(coef, rows(4 + g).astype(BF16), TN)
+        real = [by_real[k : k + 32] + by_imag[k + 32 : k + 64] for k in (0, 64)]
+        imag = [by_imag[k : k + 32] - by_real[k + 32 : k + 64] for k in (0, 64)]
+        low = real[0] + pltpu.roll(real[1], 64, 1)
+        high = pltpu.roll(imag[0], 64, 1) + imag[1]
+        grad_ref[g] = jnp.where(lane < 64, low, high)
     mix = []
     for i in range(3):
-        total = jnp.sum(rows(16 + i), axis=0, keepdims=True)
+        total = jnp.sum(rows(12 + i), axis=0, keepdims=True)
         mix.append(total + pltpu.roll(total, 64, 1))
     for g in range(4):
-        own = grad_ref[g, pl.ds(quarter * 16, 16), :]
+        own = grad_ref[g, pl.ds(side * 16, 16), :]
         for c in range(4):
             k = 4 * g + c
             send_ref[k, 0:4, :] = own[4 * c : 4 * c + 4]
@@ -250,15 +231,31 @@
             send_ref[k, 7:8, :] = mix[0]
 
 
-def final_kernel(recv_ref, lift_ref, grad_ref, mix_ref):
+def final_kernel(
+    rows, recv_ref, small_ref, fields_ref, solid_ref, lines_ref, grad_ref, mix_ref, new_ref
+):
+    last = lines_ref.shape[0] - 1
+    own = lax.axis_index("gx")
+    rims = []
+    for index, inside in ((own - 1, own > 0), (own + 1, own < last)):
+        message = lines_ref[jnp.minimum(jnp.maximum(index, 0), last)].astype(F32)
+        rims.append(jnp.where(inside, message[8:16], 0.0))
+    results = section(rows, fields_ref, solid_ref, rims)
+    for z in range(2):
+        for f in range(3):
+            new_ref[f, z] = results[z][3 + f]
     total = recv_ref[0]
     for k in range(1, recv_ref.shape[0]):
         total = total + recv_ref[k]
     grad_ref[...] = total[0:4]
-    lift = lift_ref[...].astype(F32)
-    mix = lift[:, 0:1] * total[4:5, 0:64]
-    mix = mix + lift[:, 1:2] * total[5:6, 0:64]
-    mix_ref[...] = mix + lift[:, 2:3] * total[6:7, 0:64]
+    mix = lax.dot_general(
+        small_ref[0:8, :].astype(F32),
+        pltpu.roll(total, 4, 0),
+        TN,
+        precision=lax.Precision.HIGHEST,
+        preferred_element_type=F32,
+    )
+    mix_ref[...] = mix[:, 0:64]
 
 
 def table_kernel(blocks, rows, mode_ref, table_ref):
@@ -295,10 +292,8 @@
     cell_total = x_length * lanes * lax.axis_size("gy") * planes
     loss_scale = 16.0 / math.sqrt(cell_total)
     scale_dft = 1.0 / math.sqrt(x_length)
-    lift_t = jnp.pad(lift_weight.T, ((0, 0), (0, 5)))
-    mix_t = mix_weight.T
-    proj = jnp.pad(project_weight, ((0, 0), (0, 5)))
-    proj_t = proj.T
+    none = jnp.zeros((5, lift_weight.shape[1]), BF16)
+    small = jnp.concatenate([lift_weight, none, project_weight.T, none], axis=0)
 
     def shift(array, axis, step):
         count = lax.axis_size(axis)
@@ -310,39 +305,30 @@
     rims = [shift(right, "gy", 1), shift(left, "gy", -1)]
     rims = jnp.stack(rims + [jnp.zeros_like(right)] * 6, axis=1)
     payload = jnp.concatenate([tile, rims], axis=1)
-    fields = lax.all_gather(payload, "grp", axis=0)
-
-    send = call(
-        lambda *refs: source_kernel(rows, *refs),
-        jax.ShapeDtypeStruct((blocks, 24, 128), BF16),
-        fields,
-        solid,
-        scratch=[pltpu.VMEM((2, 8, lanes), F32)],
-    )
-    mode_index, send = lax.optimization_barrier((mode_index, send))
-    recv = lines = lax.all_to_all(send, "gx", split_axis=0, concat_axis=0, tiled=True)
     table = call(
         lambda *refs: table_kernel(blocks, rows, *refs),
         jax.ShapeDtypeStruct((128, blocks * 128), BF16),
         mode_index.reshape(1, -1),
     )
-    new_velocity = call(
-        lambda *refs: velocity_kernel(rows, *refs),
-        jax.ShapeDtypeStruct((3, planes, rows, lanes), F32),
+    payload, table, small = lax.optimization_barrier((payload, table, small))
+    fields = lax.all_gather(payload, "grp", axis=0)
+
+    send = call(
+        lambda *refs: source_kernel(rows, *refs),
+        jax.ShapeDtypeStruct((blocks, 16, 128), BF16),
         fields,
         solid,
-        lines,
-    )
+        scratch=[pltpu.VMEM((2, 8, lanes), F32)],
+    )
+    recv = lines = lax.all_to_all(send, "gx", split_axis=0, concat_axis=0, tiled=True)
     send = call(
         lambda *refs: line_kernel(scale_dft, loss_scale, *refs),
-        jax.ShapeDtypeStruct((blocks, 24, 128), BF16),
+        jax.ShapeDtypeStruct((blocks, 16, 128), BF16),
         recv,
         table,
-        lift_t,
-        mix_t,
+        small,
+        mix_weight,
         spectral_weight,
-        proj,
-        proj_t,
         scratch=[pltpu.VMEM((64, 128), F32), pltpu.VMEM((64, 128), F32)],
     )
     recv = lax.all_to_all(send, "gx", split_axis=0, concat_axis=0, tiled=True)
@@ -350,14 +336,21 @@
         grad_kernel,
         jax.ShapeDtypeStruct((16, 8, 128), F32),
         recv,
-        scratch=[pltpu.VMEM((blocks * 24, 128), F32), pltpu.VMEM((4, 64, 128), F32)],
+        scratch=[pltpu.VMEM((blocks * 16, 128), F32), pltpu.VMEM((4, 32, 128), F32)],
     )
     recv = lax.all_to_all(send, ("grp", "gy"), split_axis=0, concat_axis=0, tiled=True)
-    spectral_grad, mix_grad = call(
-        final_kernel,
-        [jax.ShapeDtypeStruct((4, 128), F32), jax.ShapeDtypeStruct((64, 64), F32)],
+    spectral_grad, mix_grad, new_velocity = call(
+        lambda *refs: final_kernel(rows, *refs),
+        [
+            jax.ShapeDtypeStruct((4, 128), F32),
+            jax.ShapeDtypeStruct((64, 64), F32),
+            jax.ShapeDtypeStruct((3, planes, rows, lanes), F32),
+        ],
         recv,
-        lift_t,
+        small,
+        fields,
+        solid,
+        lines,
     )
     return new_velocity, spectral_grad, mix_grad
 

time: 83.6 us -> 80.8 us (0.967)
  blocking collectives: 28.5 us -> 63.7 us
  starting transfers between devices: 26.2 us -> 6.12 us
  waiting for transfers between devices: 16.7 us -> 1.7 us
  Pallas kernels: 7.88 us -> 5.93 us
  local copies, waits for them, and re-layouts: 3.01 us -> 2.17 us
    all_to_all x0 -> x2, blocking collectives: none -> 36.6 us  [the longest x1 18.6 us: local(): lax.all_to_all(send, 'gx', split_axis=0, concat_axis=0, tiled=True)]
    all_to_all x2 -> x0, starting transfers between devices: 20.1 us -> none  [the longest x1 10.3 us: local(): lax.all_to_all(send, ('grp', 'gy'), split_axis=0, concat_axis=0, tiled=True)]
    all_to_all x2 -> x0, waiting for transfers between devices: 13.1 us -> none  [the longest x1 6.61 us: local(): lax.all_to_all(send, 'gx', split_axis=0, concat_axis=0, tiled=True)]
    pallas_call x7 -> x6, Pallas kernels: 7.88 us -> 5.93 us  [call(): pl.pallas_call(kernel, out_shape=out_shape, in_specs=[VMEM] * len(args),...]
    ppermute x2, waiting for transfers between devices: 3.65 us -> 1.7 us  [shift(): return lax.ppermute(array, axis, pairs)]
    all_to_all x1, blocking collectives: 14.8 us -> 13.4 us  [local(): recv = lax.all_to_all(send, 'gx', split_axis=0, concat_axis=0, tiled=True)]
    unnamed x19 -> x16, local copies, waits for them, and re-layouts: 2.96 us -> 2.13 us
  transfers between devices with their start and end apart: 4 -> 2, of which waited for: 3 -> 1; matrix products, arithmetic and copies ran while one was open for 0% -> 0% of each run, Pallas kernels for 2% -> 1%
where the time goes in v5:
time: 80.8 us; the launch traced here: 80.3 us
  blocking collectives  63.7 us (79%)
  starting transfers between devices  6.12 us (8%)
  Pallas kernels  5.93 us (7%)
  local copies, waits for them, and re-layouts  2.17 us (3%)
  waiting for transfers between devices  1.7 us (2%)
    all_to_all x1, blocking collectives, local(): lax.all_to_all(send, 'gx', split_axis=0, concat_axis=0, tiled=True)  18.6 us
    all_to_all x1, blocking collectives, local(): lax.all_to_all(send, ('grp', 'gy'), split_axis=0, concat_axis=0, tiled=True)  18 us
    all_gather x1, blocking collectives, local(): fields = lax.all_gather(payload, 'grp', axis=0)  13.7 us
    all_to_all x1, blocking collectives, local(): recv = lax.all_to_all(send, 'gx', split_axis=0, concat_axis=0, tiled=True)  13.4 us
    ppermute x2, starting transfers between devices, shift(): return lax.ppermute(array, axis, pairs)  6.12 us
    pallas_call x6, Pallas kernels, call(): pl.pallas_call(kernel, out_shape=out_shape, in_specs=[VMEM] * len(args),...  5.93 us
    unnamed x16, local copies, waits for them, and re-layouts  2.13 us
    ppermute x2, waiting for transfers between devices, shift(): return lax.ppermute(array, axis, pairs)  1.7 us
  transfers between devices with their start and end apart: 2, of which 1 were waited for; matrix products, arithmetic and copies ran while one was open for 0% of the time, Pallas kernels for 1%

profile of v5, /device:TPU:1, one launch (start us, length us, event | category | flops | bytes accessed | tf_op | source)
XLA Modules:
  0.0 80.3 jit_solution(6330404860545323055)
XLA Ops:
  0.6 0.0 copy-start.2
  0.6 0.8 copy-done.2
  1.4 0.1 shard_map.94
  1.5 4.8 %collective-permute-start = (f32[2,128]{1,0:T(2,128)S(1)}, f32[2,128]{1,0:T(2,128)S(1)}, u32[]{:S(2)}, u32[]{:S(2)}) collective-permute-start(f32[2,128]{1,0:T(2,128)S(1)} %get-tuple-element.11), channel_id=1, source_target_pairs={{0,1},{1,2},{2,3},{4,5},{5,6},{6,7},{8,9},{9,10},{10,11},{12,13},{... | collective-permute-start | bytes 3080 | tf_op jit(solution)/shard_map/ppermute | solution.py:301
  6.4 1.3 %collective-permute-start.1 = (f32[2,128]{1,0:T(2,128)S(1)}, f32[2,128]{1,0:T(2,128)S(1)}, u32[]{:S(2)}, u32[]{:S(2)}) collective-permute-start(f32[2,128]{1,0:T(2,128)S(1)} %get-tuple-element.12), channel_id=1, source_target_pairs={{1,0},{2,1},{3,2},{5,4},{6,5},{7,6},{9,8},{10,9},{11,10},{13,12},{... | collective-permute-start | bytes 3080 | tf_op jit(solution)/shard_map/ppermute | solution.py:301
  7.7 0.0 copy-start.6
  7.7 0.0 copy-start.7
  7.7 0.6 copy-done.6
  8.3 0.0 copy-done.7
  8.4 0.0 copy-start.5
  8.4 0.6 copy-done.5
  9.0 0.0 copy-start.3
  9.0 0.0 copy-start.1
  9.0 0.6 shard_map.95.refs_1_
  9.6 0.0 collective-permute-done
  9.6 1.7 %collective-permute-done.1 = f32[2,128]{1,0:T(2,128)S(1)} collective-permute-done((f32[2,128]{1,0:T(2,128)S(1)}, f32[2,128]{1,0:T(2,128)S(1)}, u32[]{:S(2)}, u32[]{:S(2)}) %collective-permute-start.1) | collective-permute-done | bytes 1056 | tf_op jit(solution)/shard_map/ppermute | solution.py:301
  11.3 0.0 copy-done.3
  11.3 0.0 copy-start
  11.4 13.7 %all-gather = f32[8,56,128]{2,1,0:T(8,128)S(1)} all-gather(f32[2,56,128]{2,1,0:T(8,128)S(1)} %concatenate.14), channel_id=2, replica_groups=mesh['grp'=4,'gx'=32,'gy'=4] {'grp'}, dimensions={0}, use_global_device_ids=true | all-gather | bytes 286720 | tf_op jit(solution)/shard_map/all_gather | solution.py:314
  25.1 0.0 copy-done.1
  25.1 0.8 shard_map.96
  25.9 0.0 copy-start.4
  25.9 18.6 %all_to_all.15.refs_0_.refs_4_ = bf16[32,16,128]{2,1,0:T(8,128)(2,1)S(1)} all-to-all(bf16[32,16,128]{2,1,0:T(8,128)(2,1)S(1)} %shard_map.96), channel_id=1, replica_groups=mesh['grp'=4,'gx'=32,'gy'=4] {'gx'}, dimensions={0} | all-to-all | bytes 262144 | tf_op jit(solution)/shard_map/all_to_all | solution.py:323
  44.5 0.0 copy-done
  44.5 0.0 copy-done.4
  44.5 3.0 %shard_map.97 = bf16[32,16,128]{2,1,0:T(8,128)(2,1)S(1)} custom-call(bf16[32,16,128]{2,1,0:T(8,128)(2,1)S(1)} %all_to_all.15.refs_0_.refs_4_, bf16[128,4096]{1,0:T(8,128)(2,1)S(1)} %shard_map.95.refs_1_, bf16[16,64]{1,0:T(8,128)(2,1)S(1)} %pad_maximum_fusion.refs_2_.refs_1_, bf16[64,64]{1,0:T(8,128)(2,1)S(1)} %copy-done.4, bf16[2048,128]{1,0:T(8,128)(2,1)S(1)} %copy-done), custom_call_target="tpu_custom_call" | custom-call | tf_op jit(solution)/shard_map/pallas_call | solution.py:32
  47.5 13.4 %all_to_all.16.recv_ref = bf16[32,16,128]{2,1,0:T(8,128)(2,1)S(1)} all-to-all(bf16[32,16,128]{2,1,0:T(8,128)(2,1)S(1)} %shard_map.97), channel_id=1, replica_groups=mesh['grp'=4,'gx'=32,'gy'=4] {'gx'}, dimensions={0} | all-to-all | bytes 262144 | tf_op jit(solution)/shard_map/all_to_all | solution.py:334
  60.9 0.4 shard_map.98
  61.2 18.0 %all_to_all.17.refs_0_ = f32[16,8,128]{2,1,0:T(8,128)S(1)} all-to-all(f32[16,8,128]{2,1,0:T(8,128)S(1)} %shard_map.98), channel_id=1, replica_groups=mesh['grp'=4,'gx'=32,'gy'=4] {'grp','gy'}, dimensions={0} | all-to-all | bytes 131072 | tf_op jit(solution)/shard_map/all_to_all | solution.py:341
  79.2 1.1 %shard_map.99 = (f32[4,128]{1,0:T(4,128)}, f32[64,64]{1,0:T(8,128)}, f32[3,2,48,128]{3,2,1,0:T(8,128)}) custom-call(f32[16,8,128]{2,1,0:T(8,128)S(1)} %all_to_all.17.refs_0_, bf16[16,64]{1,0:T(8,128)(2,1)S(1)} %pad_maximum_fusion.refs_2_.refs_1_, f32[4,2,56,128]{3,2,1,0:T(8,128)S(1)} %bitcast.7, s32[2,48,128]{2,1,0:T(8,128)S(1)} %copy-done.1, ...), custom_call_target="tpu_custom_call" | custom-call | tf_op jit(solution)/shard_map/pallas_call | solution.py:32
  (5 shorter events, 0.0 us)
Async XLA Ops:
  0.6 0.8 copy-start.2
  1.5 8.1 %collective-permute-start = (f32[2,128]{1,0:T(2,128)S(1)}, f32[2,128]{1,0:T(2,128)S(1)}, u32[]{:S(2)}, u32[]{:S(2)}) collective-permute-start(f32[2,128]{1,0:T(2,128)S(1)} %get-tuple-element.11), channel_id=1, source_target_pairs={{0,1},{1,2},{2,3},{4,5},{5,6},{6,7},{8,9},{9,10},{10,11},{12,13},{... | collective-permute-start | bytes 3080 | tf_op jit(solution)/shard_map/ppermute | solution.py:301
  6.4 5.0 %collective-permute-start.1 = (f32[2,128]{1,0:T(2,128)S(1)}, f32[2,128]{1,0:T(2,128)S(1)}, u32[]{:S(2)}, u32[]{:S(2)}) collective-permute-start(f32[2,128]{1,0:T(2,128)S(1)} %get-tuple-element.12), channel_id=1, source_target_pairs={{1,0},{2,1},{3,2},{5,4},{6,5},{7,6},{9,8},{10,9},{11,10},{13,12},{... | collective-permute-start | bytes 3080 | tf_op jit(solution)/shard_map/ppermute | solution.py:301
  7.7 0.7 copy-start.6
  7.7 0.7 copy-start.7
  8.4 0.7 copy-start.5
  9.0 2.3 %copy-start.3 = (f32[1,2,48,128]{3,2,1,0:T(8,128)S(1)}, f32[1,2,48,128]{3,2,1,0:T(8,128)}, u32[]{:S(2)}) copy-start(f32[1,2,48,128]{3,2,1,0:T(8,128)} %param.7) | copy-start | bytes 147460
  9.0 16.0 %copy-start.1 = (s32[2,48,128]{2,1,0:T(8,128)S(1)}, s32[2,48,128]{2,1,0:T(8,128)}, u32[]{:S(2)}) copy-start(s32[2,48,128]{2,1,0:T(8,128)} %refs_3_.3) | copy-start | bytes 147460
  11.3 33.2 %copy-start = (bf16[2048,128]{1,0:T(8,128)(2,1)S(1)}, bf16[2048,128]{1,0:T(8,128)(2,1)}, u32[]{:S(2)}) copy-start(bf16[2048,128]{1,0:T(8,128)(2,1)} %refs_4_.1) | copy-start | bytes 1572868
  25.9 18.6 %copy-start.4 = (bf16[64,64]{1,0:T(8,128)(2,1)S(1)}, bf16[64,64]{1,0:T(8,128)(2,1)}, u32[]{:S(2)}) copy-start(bf16[64,64]{1,0:T(8,128)(2,1)} %refs_3_.2) | copy-start | bytes 24580

commit v6 on v5

--- a/solution.py
+++ b/solution.py
@@ -39,22 +39,33 @@
     )(*args)
 
 
-def edge_kernel(tile_ref, right_ref, left_ref):
+def as_row(column, shape):
+    same = iota(shape, 0) == iota(shape, 1)
+    return jnp.sum(jnp.where(same, jnp.broadcast_to(column, shape), 0.0), axis=0, keepdims=True)
+
+
+def as_column(row, shape):
+    same = iota(shape, 0) == iota(shape, 1)
+    return jnp.sum(jnp.where(same, jnp.broadcast_to(row, shape), 0.0), axis=1, keepdims=True)
+
+
+def edge_kernel(tile_ref, solid_ref, first_ref, last_ref):
     rows, lanes = tile_ref.shape[1:]
-    same = iota((rows, lanes), 0) == iota((rows, lanes), 1)
+    shape = (rows, lanes)
+    first_ref[...] = jnp.zeros_like(first_ref)
+    last = []
     for z in range(2):
         tile = tile_ref[z]
-        for ref, lane in ((right_ref, lanes - 1), (left_ref, 0)):
-            column = jnp.broadcast_to(tile[:, lane : lane + 1], (rows, lanes))
-            ref[z : z + 1, :] = jnp.sum(jnp.where(same, column, 0.0), axis=0, keepdims=True)
-
-
-def section(rows, fields_ref, solid_ref, rims):
-    lanes = fields_ref.shape[3]
+        fluid = 1.0 - solid_ref[z].astype(F32)
+        for k, column in enumerate((tile[:, 0:1], tile[:, 1:2], fluid[:, 0:1])):
+            first_ref[2 * k + z : 2 * k + z + 1, :] = as_row(column, shape)
+        last.append(as_row(tile[:, lanes - 1 : lanes], shape))
+    last_ref[...] = jnp.broadcast_to(last[0] + pltpu.roll(last[1], 64, 1), last_ref.shape)
+
+
+def section(centre, sides, rims, fluids):
+    rows, lanes = centre[0][0].shape
     row = iota((rows, lanes), 0)
-    lane = iota((rows, lanes), 1)
-    same = row == lane
-    centre = [[fields_ref[f, z, 0:rows, :] for z in range(2)] for f in range(4)]
 
     def near(f, z):
         tile = centre[f][z]
@@ -63,17 +74,11 @@
             below, above = (rim[2 * f + z : 2 * f + z + 1, :] for rim in rims)
         x_down = jnp.where(row == 0, below, pltpu.roll(tile, 1, 0))
         x_up = jnp.where(row == rows - 1, above, pltpu.roll(tile, rows - 1, 0))
-        sides = []
-        for k in (0, 1):
-            line = jnp.broadcast_to(fields_ref[f, z, rows + k : rows + k + 1, :], (rows, lanes))
-            sides.append(jnp.sum(jnp.where(same, line, 0.0), axis=1, keepdims=True))
-        y_down = jnp.where(lane == 0, sides[0], pltpu.roll(tile, 1, 1))
-        y_up = jnp.where(lane == lanes - 1, sides[1], pltpu.roll(tile, lanes - 1, 1))
+        y_up, y_down = sides[f][z]
         return x_up, x_down, y_up, y_down
 
     results = []
     for z in range(2):
-        fluid = 1.0 - solid_ref[z].astype(F32)
         velocity = [centre[f][z] for f in range(3)]
         sign = 0.5 if z == 0 else -0.5
         px_up, px_down, py_up, py_down = near(3, z)
@@ -89,17 +94,38 @@
             )
             lap = other + x_up + x_down + y_up + y_down - 6.0 * velocity[f]
             update = velocity[f] + TIME_STEP * (VISCOSITY * lap - advect - press[f])
-            new.append(update * fluid)
-        results.append(velocity + new + [centre[3][z], fluid])
+            new.append(update * fluids[z])
+        results.append(velocity + new + [centre[3][z], fluids[z]])
     return results
 
 
-def source_kernel(rows, fields_ref, solid_ref, send_ref, rim_ref):
+def source_kernel(rows, fields_ref, solid_ref, edge_ref, send_ref, rim_ref):
     blocks = send_ref.shape[0]
     lanes = fields_ref.shape[3]
+    shape = (rows, lanes)
+    lane = iota(shape, 1)
+    end = lane == lanes - 1
     role = lax.axis_index("grp")
     own = lax.axis_index("gx")
-    results = section(rows, fields_ref, solid_ref, None)
+    last = lax.axis_index("gy") == lax.axis_size("gy") - 1
+    centre, sides = [], []
+    for f in range(4):
+        centre.append([])
+        sides.append([])
+        for z in range(2):
+            tile = fields_ref[f, z, 0:rows, :]
+            one, two = (
+                as_column(fields_ref[f, z, rows + k : rows + k + 1, :], shape) for k in (0, 1)
+            )
+            here = jnp.where(end, one, pltpu.roll(tile, lanes - 1, 1))
+            above = jnp.where((lane == lanes - 2) & last, 0.0, pltpu.roll(here, lanes - 1, 1))
+            centre[f].append(here)
+            sides[f].append((jnp.where(end, two, above), jnp.where(end & last, 0.0, tile)))
+    fluids = []
+    for z in range(2):
+        fluid = pltpu.roll(1.0 - solid_ref[z].astype(F32), lanes - 1, 1)
+        fluids.append(jnp.where(end, as_column(edge_ref[4 + z : 5 + z, :], shape), fluid))
+    results = section(centre, sides, None, fluids)
     for f in range(4):
         for z in range(2):
             for k, row in ((0, 0), (1, rows - 1)):
@@ -198,7 +224,7 @@
             send_ref[4 * j + 2 * k + 1] = chunk
 
 
-def grad_kernel(recv_ref, send_ref, wide_ref, grad_ref):
+def grad_kernel(recv_ref, last_ref, send_ref, wide_ref, grad_ref):
     side = lax.rem(lax.axis_index("gx"), 2)
     blocks, height = recv_ref.shape[:2]
     for b in range(blocks):
@@ -228,19 +254,39 @@
             send_ref[k, 0:4, :] = own[4 * c : 4 * c + 4]
             for i in range(3):
                 send_ref[k, 4 + i : 5 + i, :] = mix[i]
-            send_ref[k, 7:8, :] = mix[0]
+            send_ref[k, 7:8, :] = last_ref[0:1, :]
 
 
 def final_kernel(
     rows, recv_ref, small_ref, fields_ref, solid_ref, lines_ref, grad_ref, mix_ref, new_ref
 ):
+    lanes = fields_ref.shape[3]
+    shape = (rows, lanes)
+    lane = iota(shape, 1)
     last = lines_ref.shape[0] - 1
     own = lax.axis_index("gx")
     rims = []
     for index, inside in ((own - 1, own > 0), (own + 1, own < last)):
         message = lines_ref[jnp.minimum(jnp.maximum(index, 0), last)].astype(F32)
         rims.append(jnp.where(inside, message[8:16], 0.0))
-    results = section(rows, fields_ref, solid_ref, rims)
+    place, count = lax.axis_index("gy"), lax.axis_size("gy")
+    centre, sides = [], []
+    for f in range(4):
+        below = recv_ref[f * count + jnp.maximum(place - 1, 0)][7:8, :]
+        below = jnp.where(place > 0, below, 0.0)
+        centre.append([fields_ref[f, z, 0:rows, :] for z in range(2)])
+        sides.append([])
+        for z in range(2):
+            above = jnp.where(place < count - 1, fields_ref[f, z, rows : rows + 1, :], 0.0)
+            line = below if z == 0 else pltpu.roll(below, 64, 1)
+            tile = centre[f][z]
+            y_up = jnp.where(
+                lane == lanes - 1, as_column(above, shape), pltpu.roll(tile, lanes - 1, 1)
+            )
+            y_down = jnp.where(lane == 0, as_column(line, shape), pltpu.roll(tile, 1, 1))
+            sides[f].append((y_up, y_down))
+    fluids = [1.0 - solid_ref[z].astype(F32) for z in range(2)]
+    results = section(centre, sides, rims, fluids)
     for z in range(2):
         for f in range(3):
             new_ref[f, z] = results[z][3 + f]
@@ -297,13 +343,13 @@
 
     def shift(array, axis, step):
         count = lax.axis_size(axis)
-        pairs = [(i, i + step) for i in range(count) if 0 <= i + step < count]
+        pairs = [(i, (i + step) % count) for i in range(count)]
         return lax.ppermute(array, axis, pairs)
 
-    edge = jax.ShapeDtypeStruct((planes, lanes), F32)
-    right, left = call(edge_kernel, [edge] * 2, tile)
-    rims = [shift(right, "gy", 1), shift(left, "gy", -1)]
-    rims = jnp.stack(rims + [jnp.zeros_like(right)] * 6, axis=1)
+    edge = jax.ShapeDtypeStruct((8, lanes), F32)
+    first, last = call(edge_kernel, [edge] * 2, tile, solid)
+    edge = shift(first, "gy", -1)
+    rims = jnp.stack([edge[0:2], edge[2:4]] + [jnp.zeros_like(edge[0:2])] * 6, axis=1)
     payload = jnp.concatenate([tile, rims], axis=1)
     table = call(
         lambda *refs: table_kernel(blocks, rows, *refs),
@@ -318,6 +364,7 @@
         jax.ShapeDtypeStruct((blocks, 16, 128), BF16),
         fields,
         solid,
+        edge,
         scratch=[pltpu.VMEM((2, 8, lanes), F32)],
     )
     recv = lines = lax.all_to_all(send, "gx", split_axis=0, concat_axis=0, tiled=True)
@@ -336,6 +383,7 @@
         grad_kernel,
         jax.ShapeDtypeStruct((16, 8, 128), F32),
         recv,
+        last,
         scratch=[pltpu.VMEM((blocks * 16, 128), F32), pltpu.VMEM((4, 32, 128), F32)],
     )
     recv = lax.all_to_all(send, ("grp", "gy"), split_axis=0, concat_axis=0, tiled=True)

time: 80.8 us -> 79.7 us (0.986)
  blocking collectives: 63.7 us -> 60.1 us
  starting transfers between devices: 6.12 us -> 8.44 us
  waiting for transfers between devices: 1.7 us -> 0.01 us
  local copies, waits for them, and re-layouts: 2.17 us -> 3.14 us
    all_gather x1, blocking collectives: 13.7 us -> 11.4 us  [local(): fields = lax.all_gather(payload, 'grp', axis=0)]
    ppermute x2 -> x1, starting transfers between devices: 6.12 us -> 8.44 us  [shift(): return lax.ppermute(array, axis, pairs)]
    ppermute x2 -> x1, waiting for transfers between devices: 1.7 us -> 0.01 us  [shift(): return lax.ppermute(array, axis, pairs)]
    all_to_all x1, blocking collectives: 18 us -> 16.8 us  [local(): lax.all_to_all(send, ('grp', 'gy'), split_axis=0, concat_axis=0, tiled=True)]
    unnamed x16 -> x18, local copies, waits for them, and re-layouts: 2.13 us -> 3.1 us
  transfers between devices with their start and end apart: 2 -> 1, of which waited for: 1 -> 0; matrix products, arithmetic and copies ran while one was open for 0% -> 0% of each run, Pallas kernels for 1% -> 1%
where the time goes in v6:
time: 79.7 us; the launch traced here: 79.2 us
  blocking collectives  60.1 us (75%)
  starting transfers between devices  8.44 us (11%)
  Pallas kernels  6.71 us (8%)
  local copies, waits for them, and re-layouts  3.14 us (4%)
    all_to_all x1, blocking collectives, local(): lax.all_to_all(send, 'gx', split_axis=0, concat_axis=0, tiled=True)  18.6 us
    all_to_all x1, blocking collectives, local(): lax.all_to_all(send, ('grp', 'gy'), split_axis=0, concat_axis=0, tiled=True)  16.8 us
    all_to_all x1, blocking collectives, local(): recv = lax.all_to_all(send, 'gx', split_axis=0, concat_axis=0, tiled=True)  13.4 us
    all_gather x1, blocking collectives, local(): fields = lax.all_gather(payload, 'grp', axis=0)  11.4 us
    ppermute x1, starting transfers between devices, shift(): return lax.ppermute(array, axis, pairs)  8.44 us
    pallas_call x6, Pallas kernels, call(): pl.pallas_call(kernel, out_shape=out_shape, in_specs=[VMEM] * len(args),...  6.71 us
    unnamed x18, local copies, waits for them, and re-layouts  3.1 us
  transfers between devices with their start and end apart: 1, of which 0 were waited for; matrix products, arithmetic and copies ran while one was open for 0% of the time, Pallas kernels for 1%

profile of v6, /device:TPU:1, one launch (start us, length us, event | category | flops | bytes accessed | tf_op | source)
XLA Modules:
  0.0 79.2 jit_solution(8604865408566063803)
XLA Ops:
  0.6 0.0 copy-start.1
  0.6 0.8 copy-done.1
  1.4 0.0 copy-start.3
  1.4 0.8 %copy-done.3 = f32[1,2,48,128]{3,2,1,0:T(8,128)S(1)} copy-done((f32[1,2,48,128]{3,2,1,0:T(8,128)S(1)}, f32[1,2,48,128]{3,2,1,0:T(8,128)}, u32[]{:S(2)}) %copy-start.3) | copy-done | bytes 49176
  2.2 0.2 shard_map.94
  2.4 8.4 %collective-permute-start = (f32[8,128]{1,0:T(8,128)S(1)}, f32[8,128]{1,0:T(8,128)S(1)}, u32[]{:S(2)}, u32[]{:S(2)}) collective-permute-start(f32[8,128]{1,0:T(8,128)S(1)} %get-tuple-element.11), channel_id=1, source_target_pairs={{0,3},{1,0},{2,1},{3,2},{4,7},{5,4},{6,5},{7,6},{8,11},{9,8},{10,9... | collective-permute-start | bytes 12296 | tf_op jit(solution)/shard_map/ppermute | solution.py:347
  10.8 0.0 copy-start.7
  10.8 0.0 copy-start.8
  10.9 0.6 copy-done.7
  11.5 0.0 copy-done.8
  11.5 0.0 copy-start.6
  11.6 0.6 copy-done.6
  12.2 0.0 copy-start.4
  12.2 0.6 shard_map.95.refs_1_
  12.8 0.0 collective-permute-done.refs_2_
  12.8 0.0 copy-start.2
  12.8 0.2 copy-done.4
  13.0 0.0 copy-start
  13.0 11.4 %all-gather = f32[8,56,128]{2,1,0:T(8,128)S(1)} all-gather(f32[2,56,128]{2,1,0:T(8,128)S(1)} %concatenate.14), channel_id=2, replica_groups=mesh['grp'=4,'gx'=32,'gy'=4] {'grp'}, dimensions={0}, use_global_device_ids=true | all-gather | bytes 286720 | tf_op jit(solution)/shard_map/all_gather | solution.py:360
  24.4 0.0 copy-done.2
  24.4 1.3 %shard_map.96 = bf16[32,16,128]{2,1,0:T(8,128)(2,1)S(1)} custom-call(f32[4,2,56,128]{3,2,1,0:T(8,128)S(1)} %bitcast.10, s32[2,48,128]{2,1,0:T(8,128)S(1)} %copy-done.2, f32[8,128]{1,0:T(8,128)S(1)} %collective-permute-done.refs_2_), custom_call_target="tpu_custom_call" | custom-call | tf_op jit(solution)/shard_map/pallas_call | solution.py:32
  25.7 0.0 copy-start.5
  25.7 18.6 %all_to_all.15.refs_0_.refs_4_ = bf16[32,16,128]{2,1,0:T(8,128)(2,1)S(1)} all-to-all(bf16[32,16,128]{2,1,0:T(8,128)(2,1)S(1)} %shard_map.96), channel_id=1, replica_groups=mesh['grp'=4,'gx'=32,'gy'=4] {'gx'}, dimensions={0} | all-to-all | bytes 262144 | tf_op jit(solution)/shard_map/all_to_all | solution.py:370
  44.3 0.0 copy-done
  44.3 0.0 copy-done.5
  44.3 3.0 %shard_map.97 = bf16[32,16,128]{2,1,0:T(8,128)(2,1)S(1)} custom-call(bf16[32,16,128]{2,1,0:T(8,128)(2,1)S(1)} %all_to_all.15.refs_0_.refs_4_, bf16[128,4096]{1,0:T(8,128)(2,1)S(1)} %shard_map.95.refs_1_, bf16[16,64]{1,0:T(8,128)(2,1)S(1)} %pad_maximum_fusion.refs_2_.refs_1_, bf16[64,64]{1,0:T(8,128)(2,1)S(1)} %copy-done.5, bf16[2048,128]{1,0:T(8,128)(2,1)S(1)} %copy-done), custom_call_target="tpu_custom_call" | custom-call | tf_op jit(solution)/shard_map/pallas_call | solution.py:32
  47.3 13.4 %all_to_all.16.recv_ref = bf16[32,16,128]{2,1,0:T(8,128)(2,1)S(1)} all-to-all(bf16[32,16,128]{2,1,0:T(8,128)(2,1)S(1)} %shard_map.97), channel_id=1, replica_groups=mesh['grp'=4,'gx'=32,'gy'=4] {'gx'}, dimensions={0} | all-to-all | bytes 262144 | tf_op jit(solution)/shard_map/all_to_all | solution.py:381
  60.6 0.4 shard_map.98
  61.0 16.8 %all_to_all.17.refs_0_ = f32[16,8,128]{2,1,0:T(8,128)S(1)} all-to-all(f32[16,8,128]{2,1,0:T(8,128)S(1)} %shard_map.98), channel_id=1, replica_groups=mesh['grp'=4,'gx'=32,'gy'=4] {'grp','gy'}, dimensions={0} | all-to-all | bytes 131072 | tf_op jit(solution)/shard_map/all_to_all | solution.py:389
  77.9 1.3 %shard_map.99 = (f32[4,128]{1,0:T(4,128)}, f32[64,64]{1,0:T(8,128)}, f32[3,2,48,128]{3,2,1,0:T(8,128)}) custom-call(f32[16,8,128]{2,1,0:T(8,128)S(1)} %all_to_all.17.refs_0_, bf16[16,64]{1,0:T(8,128)(2,1)S(1)} %pad_maximum_fusion.refs_2_.refs_1_, f32[4,2,56,128]{3,2,1,0:T(8,128)S(1)} %bitcast.11, s32[2,48,128]{2,1,0:T(8,128)S(1)} %copy-done.2, ...), custom_call_target="tpu_custom_call" | custom-call | tf_op jit(solution)/shard_map/pallas_call | solution.py:32
  (6 shorter events, 0.1 us)
Async XLA Ops:
  0.6 0.8 %copy-start.1 = (s32[2,48,128]{2,1,0:T(8,128)S(1)}, s32[2,48,128]{2,1,0:T(8,128)}, u32[]{:S(2)}) copy-start(s32[2,48,128]{2,1,0:T(8,128)} %refs_3_.3) | copy-start | bytes 147460
  1.4 0.8 %copy-start.3 = (f32[1,2,48,128]{3,2,1,0:T(8,128)S(1)}, f32[1,2,48,128]{3,2,1,0:T(8,128)}, u32[]{:S(2)}) copy-start(f32[1,2,48,128]{3,2,1,0:T(8,128)} %param.7) | copy-start | bytes 147460
  2.4 10.4 %collective-permute-start = (f32[8,128]{1,0:T(8,128)S(1)}, f32[8,128]{1,0:T(8,128)S(1)}, u32[]{:S(2)}, u32[]{:S(2)}) collective-permute-start(f32[8,128]{1,0:T(8,128)S(1)} %get-tuple-element.11), channel_id=1, source_target_pairs={{0,3},{1,0},{2,1},{3,2},{4,7},{5,4},{6,5},{7,6},{8,11},{9,8},{10,9... | collective-permute-start | bytes 12296 | tf_op jit(solution)/shard_map/ppermute | solution.py:347
  10.8 0.7 copy-start.7
  10.8 0.7 copy-start.8
  11.5 0.7 copy-start.6
  12.2 0.8 %copy-start.4 = (f32[1,2,48,128]{3,2,1,0:T(8,128)S(1)}, f32[1,2,48,128]{3,2,1,0:T(8,128)}, u32[]{:S(2)}) copy-start(f32[1,2,48,128]{3,2,1,0:T(8,128)} %param.7) | copy-start | bytes 147460
  12.8 11.6 %copy-start.2 = (s32[2,48,128]{2,1,0:T(8,128)S(1)}, s32[2,48,128]{2,1,0:T(8,128)}, u32[]{:S(2)}) copy-start(s32[2,48,128]{2,1,0:T(8,128)} %refs_3_.3) | copy-start | bytes 147460
  13.0 31.3 %copy-start = (bf16[2048,128]{1,0:T(8,128)(2,1)S(1)}, bf16[2048,128]{1,0:T(8,128)(2,1)}, u32[]{:S(2)}) copy-start(bf16[2048,128]{1,0:T(8,128)(2,1)} %refs_4_.1) | copy-start | bytes 1572868
  25.7 18.6 %copy-start.5 = (bf16[64,64]{1,0:T(8,128)(2,1)S(1)}, bf16[64,64]{1,0:T(8,128)(2,1)}, u32[]{:S(2)}) copy-start(bf16[64,64]{1,0:T(8,128)(2,1)} %refs_3_.2) | copy-start | bytes 24580

commit v7 on v6

--- a/solution.py
+++ b/solution.py
@@ -27,15 +27,15 @@
     return lax.broadcasted_iota(jnp.int32, shape, axis)
 
 
-def call(kernel, out_shape, *args, scratch=()):
+def call(kernel, out_shape, *args, scratch=(), space=VMEM, limit=40):
     count = len(out_shape) if isinstance(out_shape, (tuple, list)) else 1
     return pl.pallas_call(
         kernel,
         out_shape=out_shape,
-        in_specs=[VMEM] * len(args),
+        in_specs=[space] * len(args),
         out_specs=[VMEM] * count if isinstance(out_shape, (tuple, list)) else VMEM,
         scratch_shapes=list(scratch),
-        compiler_params=pltpu.CompilerParams(vmem_limit_bytes=40 * 1024 * 1024),
+        compiler_params=pltpu.CompilerParams(vmem_limit_bytes=limit * 1024 * 1024),
     )(*args)
 
 
@@ -49,7 +49,20 @@
     return jnp.sum(jnp.where(same, jnp.broadcast_to(row, shape), 0.0), axis=1, keepdims=True)
 
 
-def edge_kernel(tile_ref, solid_ref, first_ref, last_ref):
+def turned(rows):
+    pad = jnp.zeros((128 - rows.shape[0], 128), F32)
+    return jnp.transpose(jnp.concatenate([rows, pad], axis=0))
+
+
+def edge_kernel(tile_hbm, solid_hbm, first_ref, last_ref, tile_ref, solid_ref, sems):
+    copies = [
+        pltpu.make_async_copy(tile_hbm, tile_ref, sems.at[0]),
+        pltpu.make_async_copy(solid_hbm, solid_ref, sems.at[1]),
+    ]
+    for copy in copies:
+        copy.start()
+    for copy in copies:
+        copy.wait()
     rows, lanes = tile_ref.shape[1:]
     shape = (rows, lanes)
     first_ref[...] = jnp.zeros_like(first_ref)
@@ -108,19 +121,21 @@
     role = lax.axis_index("grp")
     own = lax.axis_index("gx")
     last = lax.axis_index("gy") == lax.axis_size("gy") - 1
+    blocks_of = [fields_ref[f, z, rows : rows + 8, :] for f in range(4) for z in range(2)]
+    columns = turned(jnp.concatenate(blocks_of, axis=0))[0:rows]
     centre, sides = [], []
     for f in range(4):
         centre.append([])
         sides.append([])
         for z in range(2):
             tile = fields_ref[f, z, 0:rows, :]
-            one, two = (
-                as_column(fields_ref[f, z, rows + k : rows + k + 1, :], shape) for k in (0, 1)
-            )
-            here = jnp.where(end, one, pltpu.roll(tile, lanes - 1, 1))
-            above = jnp.where((lane == lanes - 2) & last, 0.0, pltpu.roll(here, lanes - 1, 1))
-            centre[f].append(here)
-            sides[f].append((jnp.where(end, two, above), jnp.where(end & last, 0.0, tile)))
+            place = 8 * (2 * f + z)
+            one = pltpu.roll(columns, lanes - 1 - place, 1)
+            two = pltpu.roll(columns, lanes - 2 - place, 1)
+            above = jnp.where(lane >= lanes - 2, two, pltpu.roll(tile, lanes - 2, 1))
+            above = jnp.where((lane == lanes - 2) & last, 0.0, above)
+            centre[f].append(jnp.where(end, one, pltpu.roll(tile, lanes - 1, 1)))
+            sides[f].append((above, jnp.where(end & last, 0.0, tile)))
     fluids = []
     for z in range(2):
         fluid = pltpu.roll(1.0 - solid_ref[z].astype(F32), lanes - 1, 1)
@@ -160,50 +175,50 @@
 
 
 def line_kernel(
-    scale_dft, loss_scale, recv_ref, table_ref, small_ref, mix_ref, weight_ref, send_ref, back_ref,
-    coef_ref,
+    scale_dft, loss_scale, recv_ref, table_ref, turned_ref, small_ref, mix_ref, weight_ref, send_ref,
+    back_ref, coef_ref,
 ):
     blocks = recv_ref.shape[0]
-    cells = blocks * 128
     rows = 48
     lines = jnp.concatenate([recv_ref[b, 0:8, :] for b in range(blocks)], axis=1)
     both = table_ref[...]
+    cells_by_modes = turned_ref[...]
     lift, proj = small_ref[0:8, :], small_ref[8:16, :]
     lifted = dot(lift, lines, TN).astype(BF16)
-    coeffs = dot(both, lifted, NT) * scale_dft
+    coeffs = jnp.transpose(dot(lifted, cells_by_modes, NN) * scale_dft)
     coeffs16 = coeffs.astype(BF16)
     wide = jnp.concatenate([coeffs16] * 32, axis=1)
     mode_row = iota(wide.shape, 0) & 31
     mode_col = iota(wide.shape, 1) >> 6
     wide = jnp.where(mode_row == mode_col, wide, jnp.zeros_like(wide))
     product = dot(wide, weight_ref[...], NN)
-    turned = pltpu.roll(product, 64, 1)
+    swapped = pltpu.roll(product, 64, 1)
     parts = []
     for line in range(2):
         real = slice(64 * line, 64 * line + 32)
         imag = slice(64 * line + 32, 64 * line + 64)
-        parts.append(product[real] - turned[imag])
-        parts.append(turned[real] + product[imag])
+        parts.append(product[real] - swapped[imag])
+        parts.append(swapped[real] + product[imag])
     mixed = jnp.concatenate(parts, axis=0)
     mixed_t = jnp.transpose(mixed)[0:64].astype(BF16)
     hidden = dot(mixed_t, both, NN) * (2.0 * scale_dft) + dot(mix_ref[...], lifted, TN)
     square = hidden * hidden
-    inner = GELU_A * (hidden + GELU_B * (square * hidden))
-    tanh = jnp.tanh(inner)
-    half = 0.5 * (1.0 + tanh)
+    tanh = jnp.tanh(hidden * (GELU_A + (GELU_A * GELU_B) * square))
+    half = 0.5 + 0.5 * tanh
     active = (hidden * half).astype(BF16)
-    slope = half + (0.5 * GELU_A) * hidden * (1.0 - tanh * tanh) * (1.0 + (3.0 * GELU_B) * square)
+    rise = 0.5 * GELU_A + (1.5 * GELU_A * GELU_B) * square
+    slope = half + hidden * (1.0 - tanh * tanh) * rise
     predicted = dot(proj, active, NN)
     wide_lines = lines.astype(F32)
     target = pltpu.roll(wide_lines, 5, 0) + neighbour_terms(wide_lines, rows)
     misfit = (predicted - target) * loss_scale
     misfit = jnp.where(iota(misfit.shape, 0) < 3, misfit, 0.0)
-    high = misfit.astype(BF16)
-    low = (misfit - high.astype(F32)).astype(BF16)
-    back = slope * (dot(proj, high, TN) + dot(proj, low, TN))
-    back16 = back.astype(BF16)
-    mix_terms = dot(lines, back16, NT)
-    back_mixed = dot(both, back16, NT) * (2.0 * scale_dft)
+    high = misfit.astype(BF16).astype(F32)
+    parts = jnp.concatenate([high, misfit - high], axis=0).astype(BF16)
+    twice = jnp.concatenate([proj.astype(F32)] * 2, axis=0).astype(BF16)
+    back16 = (slope * dot(twice, parts, TN)).astype(BF16)
+    mix_terms = jnp.transpose(dot(back16, lines, NT))
+    back_mixed = jnp.transpose(dot(back16, cells_by_modes, NN)) * (2.0 * scale_dft)
     back_ref[...] = jnp.concatenate([back_mixed[0:64], back_mixed[64:128]], axis=1)
     coef_ref[...] = jnp.concatenate([coeffs[0:64], coeffs[64:128]], axis=1)
     mix_high = mix_terms.astype(BF16)
@@ -270,20 +285,26 @@
         message = lines_ref[jnp.minimum(jnp.maximum(index, 0), last)].astype(F32)
         rims.append(jnp.where(inside, message[8:16], 0.0))
     place, count = lax.axis_index("gy"), lax.axis_size("gy")
+    stack = []
+    for f in range(4):
+        below = recv_ref[f * count + jnp.maximum(place - 1, 0)][7:8, :]
+        for z in range(2):
+            line = below if z == 0 else pltpu.roll(below, 64, 1)
+            block = fields_ref[f, z, rows : rows + 8, :]
+            stack.append(jnp.where(iota(block.shape, 0) == 2, line, block))
+    columns = turned(jnp.concatenate(stack, axis=0))[0:rows]
     centre, sides = [], []
     for f in range(4):
-        below = recv_ref[f * count + jnp.maximum(place - 1, 0)][7:8, :]
-        below = jnp.where(place > 0, below, 0.0)
         centre.append([fields_ref[f, z, 0:rows, :] for z in range(2)])
         sides.append([])
         for z in range(2):
-            above = jnp.where(place < count - 1, fields_ref[f, z, rows : rows + 1, :], 0.0)
-            line = below if z == 0 else pltpu.roll(below, 64, 1)
+            at = 8 * (2 * f + z)
             tile = centre[f][z]
-            y_up = jnp.where(
-                lane == lanes - 1, as_column(above, shape), pltpu.roll(tile, lanes - 1, 1)
-            )
-            y_down = jnp.where(lane == 0, as_column(line, shape), pltpu.roll(tile, 1, 1))
+            edge = jnp.where(place < count - 1, pltpu.roll(columns, lanes - 1 - at, 1), 0.0)
+            y_up = jnp.where(lane == lanes - 1, edge, pltpu.roll(tile, lanes - 1, 1))
+            edge = pltpu.roll(columns, (lanes - 2 - at) % lanes, 1)
+            edge = jnp.where(place > 0, edge, 0.0)
+            y_down = jnp.where(lane == 0, edge, pltpu.roll(tile, 1, 1))
             sides[f].append((y_up, y_down))
     fluids = [1.0 - solid_ref[z].astype(F32) for z in range(2)]
     results = section(centre, sides, rims, fluids)
@@ -304,30 +325,38 @@
     mix_ref[...] = mix[:, 0:64]
 
 
-def table_kernel(blocks, rows, mode_ref, table_ref):
+def table_kernel(blocks, rows, mode_ref, table_ref, turned_ref):
     modes = mode_ref.shape[1]
-    square = (modes, modes)
-    index = jnp.where(iota(square, 0) == iota(square, 1), mode_ref[...].astype(F32), 0.0)
-    index = jnp.sum(index, axis=1, keepdims=True).astype(jnp.int32)
-    shape = (modes, 128)
-    lane = iota(shape, 1)
     unit = 2.0 * math.pi / (blocks * rows)
-    outer = unit * (((index * lane) & (blocks - 1)) * rows).astype(F32)
-    cell = jnp.where(lane >= rows, lane - rows, lane)
-    cell = jnp.where(lane < 2 * rows, cell, 0)
-    inner = unit * (index * cell).astype(F32)
-    outer_cos, outer_sin = jnp.cos(outer), jnp.sin(outer)
-    inner_cos, inner_sin = jnp.cos(inner), jnp.sin(inner)
-    planes = [lane < rows, (lane >= rows) & (lane < 2 * rows)]
-    factors = [(jnp.where(p, inner_cos, 0.0), jnp.where(p, inner_sin, 0.0)) for p in planes]
+    along = mode_ref[...].astype(F32)
+    along = jnp.concatenate([along] * (128 // modes), axis=1)
+    down = jnp.where((iota((128, 128), 0) == iota((128, 128), 1)), along, 0.0)
+    down = jnp.sum(down, axis=1, keepdims=True).astype(jnp.int32)
+    along = along.astype(jnp.int32)
+
+    def factors(index, axis):
+        other = iota((128, 128), 1 - axis)
+        kind = iota((128, 128), axis)
+        imag = ((kind // modes) & 1) == 1
+        outer = unit * (((index * other) & (blocks - 1)) * rows).astype(F32)
+        cell = other - jnp.where(kind >= 2 * modes, rows, 0)
+        valid = (cell >= 0) & (cell < rows)
+        inner = unit * (index * jnp.where(valid, cell, 0)).astype(F32)
+        outer_cos, outer_sin = jnp.cos(outer), jnp.sin(outer)
+        by_cos = jnp.where(imag, -outer_sin, outer_cos)
+        by_sin = jnp.where(imag, -outer_cos, -outer_sin)
+        inner_cos = jnp.where(valid, jnp.cos(inner), 0.0)
+        inner_sin = jnp.where(valid, jnp.sin(inner), 0.0)
+        return by_cos, by_sin, inner_cos, inner_sin
+
+    by_cos, by_sin, inner_cos, inner_sin = factors(down, 0)
     for b in range(blocks):
-        cos_b = outer_cos[:, b : b + 1]
-        sin_b = outer_sin[:, b : b + 1]
-        parts = []
-        for cos_c, sin_c in factors:
-            parts.append(cos_b * cos_c - sin_b * sin_c)
-            parts.append(-(sin_b * cos_c) - cos_b * sin_c)
-        table_ref[:, b * 128 : (b + 1) * 128] = jnp.concatenate(parts, axis=0).astype(BF16)
+        block = by_cos[:, b : b + 1] * inner_cos + by_sin[:, b : b + 1] * inner_sin
+        table_ref[:, b * 128 : (b + 1) * 128] = block.astype(BF16)
+    by_cos, by_sin, inner_cos, inner_sin = factors(along, 1)
+    for b in range(blocks):
+        block = by_cos[b : b + 1, :] * inner_cos + by_sin[b : b + 1, :] * inner_sin
+        turned_ref[b * 128 : (b + 1) * 128, :] = block.astype(BF16)
 
 
 def local(slot_field, solid, lift_weight, spectral_weight, mix_weight, project_weight, mode_index):
@@ -347,16 +376,33 @@
         return lax.ppermute(array, axis, pairs)
 
     edge = jax.ShapeDtypeStruct((8, lanes), F32)
-    first, last = call(edge_kernel, [edge] * 2, tile, solid)
+    first, last = call(
+        edge_kernel,
+        [edge] * 2,
+        tile,
+        solid,
+        scratch=[
+            pltpu.VMEM(tile.shape, F32),
+            pltpu.VMEM(solid.shape, jnp.int32),
+            pltpu.SemaphoreType.DMA((2,)),
+        ],
+        space=pl.BlockSpec(memory_space=pl.ANY),
+        limit=60,
+    )
     edge = shift(first, "gy", -1)
     rims = jnp.stack([edge[0:2], edge[2:4]] + [jnp.zeros_like(edge[0:2])] * 6, axis=1)
     payload = jnp.concatenate([tile, rims], axis=1)
-    table = call(
+    table, cells_by_modes = call(
         lambda *refs: table_kernel(blocks, rows, *refs),
-        jax.ShapeDtypeStruct((128, blocks * 128), BF16),
+        [
+            jax.ShapeDtypeStruct((128, blocks * 128), BF16),
+            jax.ShapeDtypeStruct((blocks * 128, 128), BF16),
+        ],
         mode_index.reshape(1, -1),
     )
-    payload, table, small = lax.optimization_barrier((payload, table, small))
+    payload, table, cells_by_modes, small = lax.optimization_barrier(
+        (payload, table, cells_by_modes, small)
+    )
     fields = lax.all_gather(payload, "grp", axis=0)
 
     send = call(
@@ -373,6 +419,7 @@
         jax.ShapeDtypeStruct((blocks, 16, 128), BF16),
         recv,
         table,
+        cells_by_modes,
         small,
         mix_weight,
         spectral_weight,

time: 79.7 us -> 79.7 us (level)
  Pallas kernels: 6.71 us -> 8.51 us
  local copies, waits for them, and re-layouts: 3.14 us -> 1.39 us
    pallas_call x6, Pallas kernels: 6.71 us -> 8.51 us  [call(): pl.pallas_call(kernel, out_shape=out_shape, in_specs=[space] * len(args),...]
    unnamed x18 -> x16, local copies, waits for them, and re-layouts: 3.1 us -> 1.35 us
  transfers between devices with their start and end apart: 1 -> 1, of which waited for: 0 -> 0; matrix products, arithmetic and copies ran while one was open for 0% -> 0% of each run, Pallas kernels for 1% -> 3%
where the time goes in v7:
time: 79.7 us; the launch traced here: 79.3 us
  blocking collectives  60.1 us (75%)
  Pallas kernels  8.51 us (11%)
  starting transfers between devices  8.45 us (11%)
  local copies, waits for them, and re-layouts  1.39 us (2%)
    all_to_all x1, blocking collectives, local(): lax.all_to_all(send, 'gx', split_axis=0, concat_axis=0, tiled=True)  18.6 us
    all_to_all x1, blocking collectives, local(): lax.all_to_all(send, ('grp', 'gy'), split_axis=0, concat_axis=0, tiled=True)  16.8 us
    all_to_all x1, blocking collectives, local(): recv = lax.all_to_all(send, 'gx', split_axis=0, concat_axis=0, tiled=True)  13.4 us
    all_gather x1, blocking collectives, local(): fields = lax.all_gather(payload, 'grp', axis=0)  11.3 us
    pallas_call x6, Pallas kernels, call(): pl.pallas_call(kernel, out_shape=out_shape, in_specs=[space] * len(args),...  8.51 us
    ppermute x1, starting transfers between devices, shift(): return lax.ppermute(array, axis, pairs)  8.45 us
  transfers between devices with their start and end apart: 1, of which 0 were waited for; matrix products, arithmetic and copies ran while one was open for 0% of the time, Pallas kernels for 3%

profile of v7, /device:TPU:1, one launch (start us, length us, event | category | flops | bytes accessed | tf_op | source)
XLA Modules:
  0.0 79.3 jit_solution(7988511544815184933)
XLA Ops:
  0.6 0.0 copy-start.5
  0.6 1.6 %shard_map.94 = (f32[8,128]{1,0:T(8,128)}, f32[8,128]{1,0:T(8,128)}) custom-call(f32[2,48,128]{2,1,0:T(8,128)} %bitcast.13, s32[2,48,128]{2,1,0:T(8,128)} %refs_3_.1), custom_call_target="tpu_custom_call" | custom-call | tf_op jit(solution)/shard_map/pallas_call | solution.py:32
  2.3 8.4 %collective-permute-start = (f32[8,128]{1,0:T(8,128)}, f32[8,128]{1,0:T(8,128)S(1)}, u32[]{:S(2)}, u32[]{:S(2)}) collective-permute-start(f32[8,128]{1,0:T(8,128)} %get-tuple-element.14), channel_id=1, source_target_pairs={{0,3},{1,0},{2,1},{3,2},{4,7},{5,4},{6,5},{7,6},{8,11},{9,8},{10,9... | collective-permute-start | bytes 12296 | tf_op jit(solution)/shard_map/ppermute | solution.py:376
  10.7 0.0 copy-start.6
  10.7 0.0 copy-start.7
  10.8 0.6 copy-done.6
  11.4 0.0 copy-done.7
  11.4 0.0 copy-start.4
  11.5 0.6 copy-done.4
  12.1 2.1 %shard_map.95 = (bf16[128,4096]{1,0:T(8,128)(2,1)S(1)}, bf16[4096,128]{1,0:T(8,128)(2,1)S(1)}) custom-call(s32[1,32]{1,0:T(1,128)S(1)} %bitcast.12), custom_call_target="tpu_custom_call" | custom-call | tf_op jit(solution)/shard_map/pallas_call | solution.py:32
  14.2 0.0 collective-permute-done.refs_2_
  14.3 0.0 copy-start.1
  14.3 0.0 copy-done.5
  14.3 0.0 copy-start
  14.3 11.3 %all-gather = f32[8,56,128]{2,1,0:T(8,128)S(1)} all-gather(f32[2,56,128]{2,1,0:T(8,128)S(1)} %concatenate.14), channel_id=2, replica_groups=mesh['grp'=4,'gx'=32,'gy'=4] {'grp'}, dimensions={0}, use_global_device_ids=true | all-gather | bytes 286720 | tf_op jit(solution)/shard_map/all_gather | solution.py:406
  25.6 0.0 copy-done.1
  25.6 0.8 shard_map.96
  26.4 0.0 copy-start.2
  26.4 18.6 %all_to_all.15.refs_0_.refs_4_ = bf16[32,16,128]{2,1,0:T(8,128)(2,1)S(1)} all-to-all(bf16[32,16,128]{2,1,0:T(8,128)(2,1)S(1)} %shard_map.96), channel_id=1, replica_groups=mesh['grp'=4,'gx'=32,'gy'=4] {'gx'}, dimensions={0} | all-to-all | bytes 262144 | tf_op jit(solution)/shard_map/all_to_all | solution.py:416
  45.0 0.0 copy-done
  45.0 0.0 copy-done.2
  45.0 2.5 %shard_map.97 = bf16[32,16,128]{2,1,0:T(8,128)(2,1)S(1)} custom-call(bf16[32,16,128]{2,1,0:T(8,128)(2,1)S(1)} %all_to_all.15.refs_0_.refs_4_, bf16[128,4096]{1,0:T(8,128)(2,1)S(1)} %get-tuple-element.18.refs_1_, bf16[4096,128]{1,0:T(8,128)(2,1)S(1)} %get-tuple-element.19.refs_2_, bf16[16,64]{1,0:T(8,128)(2,1)S(1)} %pad_maximum_fusion.refs_3_.refs_1_, ...), custom_call_target="tpu_custom_call" | custom-call | tf_op jit(solution)/shard_map/pallas_call | solution.py:32
  47.6 0.0 copy-start.3
  47.6 13.4 %all_to_all.16.recv_ref = bf16[32,16,128]{2,1,0:T(8,128)(2,1)S(1)} all-to-all(bf16[32,16,128]{2,1,0:T(8,128)(2,1)S(1)} %shard_map.97), channel_id=1, replica_groups=mesh['grp'=4,'gx'=32,'gy'=4] {'gx'}, dimensions={0} | all-to-all | bytes 262144 | tf_op jit(solution)/shard_map/all_to_all | solution.py:428
  61.0 0.0 copy-done.3
  61.0 0.4 shard_map.98
  61.4 16.8 %all_to_all.17.refs_0_ = f32[16,8,128]{2,1,0:T(8,128)S(1)} all-to-all(f32[16,8,128]{2,1,0:T(8,128)S(1)} %shard_map.98), channel_id=1, replica_groups=mesh['grp'=4,'gx'=32,'gy'=4] {'grp','gy'}, dimensions={0} | all-to-all | bytes 131072 | tf_op jit(solution)/shard_map/all_to_all | solution.py:436
  78.2 1.1 %shard_map.99 = (f32[4,128]{1,0:T(4,128)}, f32[64,64]{1,0:T(8,128)}, f32[3,2,48,128]{3,2,1,0:T(8,128)}) custom-call(f32[16,8,128]{2,1,0:T(8,128)S(1)} %all_to_all.17.refs_0_, bf16[16,64]{1,0:T(8,128)(2,1)S(1)} %pad_maximum_fusion.refs_3_.refs_1_, f32[4,2,56,128]{3,2,1,0:T(8,128)S(1)} %bitcast.11, s32[2,48,128]{2,1,0:T(8,128)S(1)} %copy-done.1, ...), custom_call_target="tpu_custom_call" | custom-call | tf_op jit(solution)/shard_map/pallas_call | solution.py:32
  (6 shorter events, 0.1 us)
Async XLA Ops:
  0.6 13.7 %copy-start.5 = (f32[1,2,48,128]{3,2,1,0:T(8,128)S(1)}, f32[1,2,48,128]{3,2,1,0:T(8,128)}, u32[]{:S(2)}) copy-start(f32[1,2,48,128]{3,2,1,0:T(8,128)} %param.7) | copy-start | bytes 147460
  2.3 12.0 %collective-permute-start = (f32[8,128]{1,0:T(8,128)}, f32[8,128]{1,0:T(8,128)S(1)}, u32[]{:S(2)}, u32[]{:S(2)}) collective-permute-start(f32[8,128]{1,0:T(8,128)} %get-tuple-element.14), channel_id=1, source_target_pairs={{0,3},{1,0},{2,1},{3,2},{4,7},{5,4},{6,5},{7,6},{8,11},{9,8},{10,9... | collective-permute-start | bytes 12296 | tf_op jit(solution)/shard_map/ppermute | solution.py:376
  10.7 0.7 copy-start.6
  10.7 0.7 copy-start.7
  11.4 0.7 copy-start.4
  14.3 11.4 %copy-start.1 = (s32[2,48,128]{2,1,0:T(8,128)S(1)}, s32[2,48,128]{2,1,0:T(8,128)}, u32[]{:S(2)}) copy-start(s32[2,48,128]{2,1,0:T(8,128)} %refs_3_.1) | copy-start | bytes 147460
  14.3 30.7 %copy-start = (bf16[2048,128]{1,0:T(8,128)(2,1)S(1)}, bf16[2048,128]{1,0:T(8,128)(2,1)}, u32[]{:S(2)}) copy-start(bf16[2048,128]{1,0:T(8,128)(2,1)} %refs_5_.1) | copy-start | bytes 1572868
  26.4 18.6 %copy-start.2 = (bf16[64,64]{1,0:T(8,128)(2,1)S(1)}, bf16[64,64]{1,0:T(8,128)(2,1)}, u32[]{:S(2)}) copy-start(bf16[64,64]{1,0:T(8,128)(2,1)} %refs_4_.1) | copy-start | bytes 24580
  47.6 13.4 %copy-start.3 = (f32[8,128]{1,0:T(8,128)S(1)}, f32[8,128]{1,0:T(8,128)}, u32[]{:S(2)}) copy-start(f32[8,128]{1,0:T(8,128)} %get-tuple-element.21.last_ref) | copy-start | bytes 12292

commit v8 on v7

--- a/solution.py
+++ b/solution.py
@@ -27,15 +27,15 @@
     return lax.broadcasted_iota(jnp.int32, shape, axis)
 
 
-def call(kernel, out_shape, *args, scratch=(), space=VMEM, limit=40):
+def call(kernel, out_shape, *args, scratch=()):
     count = len(out_shape) if isinstance(out_shape, (tuple, list)) else 1
     return pl.pallas_call(
         kernel,
         out_shape=out_shape,
-        in_specs=[space] * len(args),
+        in_specs=[VMEM] * len(args),
         out_specs=[VMEM] * count if isinstance(out_shape, (tuple, list)) else VMEM,
         scratch_shapes=list(scratch),
-        compiler_params=pltpu.CompilerParams(vmem_limit_bytes=limit * 1024 * 1024),
+        compiler_params=pltpu.CompilerParams(vmem_limit_bytes=40 * 1024 * 1024),
     )(*args)
 
 
@@ -44,36 +44,25 @@
     return jnp.sum(jnp.where(same, jnp.broadcast_to(column, shape), 0.0), axis=0, keepdims=True)
 
 
-def as_column(row, shape):
-    same = iota(shape, 0) == iota(shape, 1)
-    return jnp.sum(jnp.where(same, jnp.broadcast_to(row, shape), 0.0), axis=1, keepdims=True)
-
-
 def turned(rows):
     pad = jnp.zeros((128 - rows.shape[0], 128), F32)
     return jnp.transpose(jnp.concatenate([rows, pad], axis=0))
 
 
-def edge_kernel(tile_hbm, solid_hbm, first_ref, last_ref, tile_ref, solid_ref, sems):
-    copies = [
-        pltpu.make_async_copy(tile_hbm, tile_ref, sems.at[0]),
-        pltpu.make_async_copy(solid_hbm, solid_ref, sems.at[1]),
-    ]
-    for copy in copies:
-        copy.start()
-    for copy in copies:
-        copy.wait()
-    rows, lanes = tile_ref.shape[1:]
-    shape = (rows, lanes)
-    first_ref[...] = jnp.zeros_like(first_ref)
-    last = []
+def edge_kernel(fields_ref, solid_ref, edge_ref):
+    lanes = fields_ref.shape[3]
+    lane = iota(edge_ref.shape, 1)
+    edge = jnp.zeros(edge_ref.shape, F32)
+    for f in range(4):
+        for z in range(2):
+            place = 2 * (2 * f + z)
+            tile = fields_ref[f, z]
+            tile = pltpu.roll(tile, place, 1) if place else tile
+            edge = jnp.where((lane >> 1) == 2 * f + z, tile, edge)
     for z in range(2):
-        tile = tile_ref[z]
-        fluid = 1.0 - solid_ref[z].astype(F32)
-        for k, column in enumerate((tile[:, 0:1], tile[:, 1:2], fluid[:, 0:1])):
-            first_ref[2 * k + z : 2 * k + z + 1, :] = as_row(column, shape)
-        last.append(as_row(tile[:, lanes - 1 : lanes], shape))
-    last_ref[...] = jnp.broadcast_to(last[0] + pltpu.roll(last[1], 64, 1), last_ref.shape)
+        fluid = pltpu.roll(1.0 - solid_ref[z].astype(F32), 16 + z, 1)
+        edge = jnp.where(lane == 16 + z, fluid, edge)
+    edge_ref[...] = edge
 
 
 def section(centre, sides, rims, fluids):
@@ -112,24 +101,22 @@
     return results
 
 
-def source_kernel(rows, fields_ref, solid_ref, edge_ref, send_ref, rim_ref):
+def source_kernel(fields_ref, solid_ref, edge_ref, send_ref, rim_ref):
     blocks = send_ref.shape[0]
-    lanes = fields_ref.shape[3]
-    shape = (rows, lanes)
-    lane = iota(shape, 1)
+    rows, lanes = fields_ref.shape[2:]
+    lane = iota((rows, lanes), 1)
     end = lane == lanes - 1
     role = lax.axis_index("grp")
     own = lax.axis_index("gx")
     last = lax.axis_index("gy") == lax.axis_size("gy") - 1
-    blocks_of = [fields_ref[f, z, rows : rows + 8, :] for f in range(4) for z in range(2)]
-    columns = turned(jnp.concatenate(blocks_of, axis=0))[0:rows]
+    columns = edge_ref[...]
     centre, sides = [], []
     for f in range(4):
         centre.append([])
         sides.append([])
         for z in range(2):
-            tile = fields_ref[f, z, 0:rows, :]
-            place = 8 * (2 * f + z)
+            tile = fields_ref[f, z]
+            place = 2 * (2 * f + z)
             one = pltpu.roll(columns, lanes - 1 - place, 1)
             two = pltpu.roll(columns, lanes - 2 - place, 1)
             above = jnp.where(lane >= lanes - 2, two, pltpu.roll(tile, lanes - 2, 1))
@@ -139,7 +126,7 @@
     fluids = []
     for z in range(2):
         fluid = pltpu.roll(1.0 - solid_ref[z].astype(F32), lanes - 1, 1)
-        fluids.append(jnp.where(end, as_column(edge_ref[4 + z : 5 + z, :], shape), fluid))
+        fluids.append(jnp.where(end, pltpu.roll(columns, lanes - 17 - z, 1), fluid))
     results = section(centre, sides, None, fluids)
     for f in range(4):
         for z in range(2):
@@ -273,11 +260,10 @@
 
 
 def final_kernel(
-    rows, recv_ref, small_ref, fields_ref, solid_ref, lines_ref, grad_ref, mix_ref, new_ref
+    recv_ref, small_ref, fields_ref, solid_ref, edge_ref, lines_ref, grad_ref, mix_ref, new_ref
 ):
-    lanes = fields_ref.shape[3]
-    shape = (rows, lanes)
-    lane = iota(shape, 1)
+    rows, lanes = fields_ref.shape[2:]
+    lane = iota((rows, lanes), 1)
     last = lines_ref.shape[0] - 1
     own = lax.axis_index("gx")
     rims = []
@@ -288,22 +274,19 @@
     stack = []
     for f in range(4):
         below = recv_ref[f * count + jnp.maximum(place - 1, 0)][7:8, :]
-        for z in range(2):
-            line = below if z == 0 else pltpu.roll(below, 64, 1)
-            block = fields_ref[f, z, rows : rows + 8, :]
-            stack.append(jnp.where(iota(block.shape, 0) == 2, line, block))
-    columns = turned(jnp.concatenate(stack, axis=0))[0:rows]
+        stack += [below, pltpu.roll(below, 64, 1)]
+    lower = jnp.where(place > 0, turned(jnp.concatenate(stack, axis=0))[0:rows], 0.0)
+    upper = jnp.where(place < count - 1, edge_ref[...], 0.0)
     centre, sides = [], []
     for f in range(4):
-        centre.append([fields_ref[f, z, 0:rows, :] for z in range(2)])
+        centre.append([fields_ref[f, z] for z in range(2)])
         sides.append([])
         for z in range(2):
-            at = 8 * (2 * f + z)
+            at = 2 * f + z
             tile = centre[f][z]
-            edge = jnp.where(place < count - 1, pltpu.roll(columns, lanes - 1 - at, 1), 0.0)
+            edge = pltpu.roll(upper, lanes - 1 - 2 * at, 1)
             y_up = jnp.where(lane == lanes - 1, edge, pltpu.roll(tile, lanes - 1, 1))
-            edge = pltpu.roll(columns, (lanes - 2 - at) % lanes, 1)
-            edge = jnp.where(place > 0, edge, 0.0)
+            edge = pltpu.roll(lower, lanes - at, 1) if at else lower
             y_down = jnp.where(lane == 0, edge, pltpu.roll(tile, 1, 1))
             sides[f].append((y_up, y_down))
     fluids = [1.0 - solid_ref[z].astype(F32) for z in range(2)]
@@ -325,35 +308,34 @@
     mix_ref[...] = mix[:, 0:64]
 
 
-def table_kernel(blocks, rows, mode_ref, table_ref, turned_ref):
+def table_kernel(blocks, mode_ref, tile_ref, table_ref, turned_ref, last_ref):
+    rows, lanes = tile_ref.shape[1:]
+    ends = [as_row(tile_ref[z, :, lanes - 1 : lanes], (rows, lanes)) for z in range(2)]
+    last_ref[...] = jnp.broadcast_to(ends[0] + pltpu.roll(ends[1], 64, 1), last_ref.shape)
     modes = mode_ref.shape[1]
     unit = 2.0 * math.pi / (blocks * rows)
-    along = mode_ref[...].astype(F32)
-    along = jnp.concatenate([along] * (128 // modes), axis=1)
-    down = jnp.where((iota((128, 128), 0) == iota((128, 128), 1)), along, 0.0)
-    down = jnp.sum(down, axis=1, keepdims=True).astype(jnp.int32)
-    along = along.astype(jnp.int32)
-
-    def factors(index, axis):
-        other = iota((128, 128), 1 - axis)
-        kind = iota((128, 128), axis)
-        imag = ((kind // modes) & 1) == 1
-        outer = unit * (((index * other) & (blocks - 1)) * rows).astype(F32)
-        cell = other - jnp.where(kind >= 2 * modes, rows, 0)
-        valid = (cell >= 0) & (cell < rows)
-        inner = unit * (index * jnp.where(valid, cell, 0)).astype(F32)
-        outer_cos, outer_sin = jnp.cos(outer), jnp.sin(outer)
-        by_cos = jnp.where(imag, -outer_sin, outer_cos)
-        by_sin = jnp.where(imag, -outer_cos, -outer_sin)
-        inner_cos = jnp.where(valid, jnp.cos(inner), 0.0)
-        inner_sin = jnp.where(valid, jnp.sin(inner), 0.0)
-        return by_cos, by_sin, inner_cos, inner_sin
-
-    by_cos, by_sin, inner_cos, inner_sin = factors(down, 0)
+    square = (modes, modes)
+    index = jnp.where(iota(square, 0) == iota(square, 1), mode_ref[...].astype(F32), 0.0)
+    index = jnp.sum(index, axis=1, keepdims=True).astype(jnp.int32)
+    lane = iota((modes, 128), 1)
+    outer = unit * (((index * lane) & (blocks - 1)) * rows).astype(F32)
+    cell = jnp.where(lane >= rows, lane - rows, lane)
+    inner = unit * (index * jnp.where(lane < 2 * rows, cell, 0)).astype(F32)
+    outer_cos, outer_sin = jnp.cos(outer), jnp.sin(outer)
+    inner_cos, inner_sin = jnp.cos(inner), jnp.sin(inner)
+    by_cos = jnp.concatenate([outer_cos, -outer_sin] * 2, axis=0)
+    by_sin = jnp.concatenate([-outer_sin, -outer_cos] * 2, axis=0)
+    low = iota((128, 128), 0) < 2 * modes
+    lane = iota((128, 128), 1)
+    start = jnp.where(low, 0, rows)
+    valid = (lane >= start) & (lane < start + rows)
+    inner_cos = jnp.where(valid, jnp.concatenate([inner_cos] * 4, axis=0), 0.0)
+    inner_sin = jnp.where(valid, jnp.concatenate([inner_sin] * 4, axis=0), 0.0)
     for b in range(blocks):
         block = by_cos[:, b : b + 1] * inner_cos + by_sin[:, b : b + 1] * inner_sin
         table_ref[:, b * 128 : (b + 1) * 128] = block.astype(BF16)
-    by_cos, by_sin, inner_cos, inner_sin = factors(along, 1)
+    by_cos, by_sin = jnp.transpose(by_cos), jnp.transpose(by_sin)
+    inner_cos, inner_sin = jnp.transpose(inner_cos), jnp.transpose(inner_sin)
     for b in range(blocks):
         block = by_cos[b : b + 1, :] * inner_cos + by_sin[b : b + 1, :] * inner_sin
         turned_ref[b * 128 : (b + 1) * 128, :] = block.astype(BF16)
@@ -375,38 +357,24 @@
         pairs = [(i, (i + step) % count) for i in range(count)]
         return lax.ppermute(array, axis, pairs)
 
-    edge = jax.ShapeDtypeStruct((8, lanes), F32)
-    first, last = call(
-        edge_kernel,
-        [edge] * 2,
-        tile,
-        solid,
-        scratch=[
-            pltpu.VMEM(tile.shape, F32),
-            pltpu.VMEM(solid.shape, jnp.int32),
-            pltpu.SemaphoreType.DMA((2,)),
-        ],
-        space=pl.BlockSpec(memory_space=pl.ANY),
-        limit=60,
-    )
-    edge = shift(first, "gy", -1)
-    rims = jnp.stack([edge[0:2], edge[2:4]] + [jnp.zeros_like(edge[0:2])] * 6, axis=1)
-    payload = jnp.concatenate([tile, rims], axis=1)
-    table, cells_by_modes = call(
-        lambda *refs: table_kernel(blocks, rows, *refs),
+    fields = lax.all_gather(slot_field, "grp", axis=0, tiled=True)
+    edge = call(edge_kernel, jax.ShapeDtypeStruct((rows, lanes), F32), fields, solid)
+    edge = shift(edge, "gy", -1)
+    table, cells_by_modes, last = call(
+        lambda *refs: table_kernel(blocks, *refs),
         [
             jax.ShapeDtypeStruct((128, blocks * 128), BF16),
             jax.ShapeDtypeStruct((blocks * 128, 128), BF16),
+            jax.ShapeDtypeStruct((8, lanes), F32),
         ],
         mode_index.reshape(1, -1),
-    )
-    payload, table, cells_by_modes, small = lax.optimization_barrier(
-        (payload, table, cells_by_modes, small)
-    )
-    fields = lax.all_gather(payload, "grp", axis=0)
-
+        tile,
+    )
+    edge, table, cells_by_modes, last, small = lax.optimization_barrier(
+        (edge, table, cells_by_modes, last, small)
+    )
     send = call(
-        lambda *refs: source_kernel(rows, *refs),
+        source_kernel,
         jax.ShapeDtypeStruct((blocks, 16, 128), BF16),
         fields,
         solid,
@@ -435,7 +403,7 @@
     )
     recv = lax.all_to_all(send, ("grp", "gy"), split_axis=0, concat_axis=0, tiled=True)
     spectral_grad, mix_grad, new_velocity = call(
-        lambda *refs: final_kernel(rows, *refs),
+        final_kernel,
         [
             jax.ShapeDtypeStruct((4, 128), F32),
             jax.ShapeDtypeStruct((64, 64), F32),
@@ -445,6 +413,7 @@
         small,
         fields,
         solid,
+        edge,
         lines,
     )
     return new_velocity, spectral_grad, mix_grad

time: 79.7 us -> 76.5 us (0.960)
  blocking collectives: 60.1 us -> 66.1 us
  starting transfers between devices: 8.45 us -> 3.07 us
  Pallas kernels: 8.51 us -> 5.77 us
  local copies, waits for them, and re-layouts: 1.39 us -> 0.03 us
    ppermute x1, starting transfers between devices: 8.45 us -> 3.07 us  [shift(): return lax.ppermute(array, axis, pairs)]
    all_gather x1, blocking collectives: 11.3 us -> 16.6 us  [local(): fields = lax.all_gather(slot_field, 'grp', axis=0, tiled=True)]
    pallas_call x6, Pallas kernels: 8.51 us -> 5.77 us  [call(): pl.pallas_call(kernel, out_shape=out_shape, in_specs=[VMEM] * len(args),...]
    all_to_all x1, blocking collectives: 16.8 us -> 18.6 us  [local(): lax.all_to_all(send, ('grp', 'gy'), split_axis=0, concat_axis=0, tiled=True)]
    unnamed x16 -> x14, local copies, waits for them, and re-layouts: 1.35 us -> 0.03 us
  transfers between devices with their start and end apart: 1 -> 1, of which waited for: 0 -> 1; matrix products, arithmetic and copies ran while one was open for 0% -> 0% of each run, Pallas kernels for 3% -> 1%
where the time goes in v8:
time: 76.5 us; the launch traced here: 76.2 us
  blocking collectives  66.1 us (86%)
  Pallas kernels  5.77 us (8%)
  starting transfers between devices  3.07 us (4%)
  between operations  0.77 us (1%)
    all_to_all x1, blocking collectives, local(): lax.all_to_all(send, ('grp', 'gy'), split_axis=0, concat_axis=0, tiled=True)  18.6 us
    all_to_all x1, blocking collectives, local(): lax.all_to_all(send, 'gx', split_axis=0, concat_axis=0, tiled=True)  18.2 us
    all_gather x1, blocking collectives, local(): fields = lax.all_gather(slot_field, 'grp', axis=0, tiled=True)  16.6 us
    all_to_all x1, blocking collectives, local(): recv = lax.all_to_all(send, 'gx', split_axis=0, concat_axis=0, tiled=True)  12.7 us
    pallas_call x6, Pallas kernels, call(): pl.pallas_call(kernel, out_shape=out_shape, in_specs=[VMEM] * len(args),...  5.77 us
    ppermute x1, starting transfers between devices, shift(): return lax.ppermute(array, axis, pairs)  3.07 us
  transfers between devices with their start and end apart: 1, of which 1 were waited for; matrix products, arithmetic and copies ran while one was open for 0% of the time, Pallas kernels for 1%

profile of v8, /device:TPU:1, one launch (start us, length us, event | category | flops | bytes accessed | tf_op | source)
XLA Modules:
  0.0 76.2 jit_solution(5771860647076020886)
XLA Ops:
  0.6 0.0 copy-start.1
  0.6 0.0 copy-start.5
  0.7 0.0 copy-start.6
  0.7 0.0 copy-start.2
  0.7 0.0 copy-start.4
  0.7 16.6 %all_gather.3.fields_ref = f32[4,2,48,128]{3,2,1,0:T(8,128)S(1)} all-gather(f32[1,2,48,128]{3,2,1,0:T(8,128)} %param.7), channel_id=1, replica_groups=mesh['grp'=4,'gx'=32,'gy'=4] {'grp'}, dimensions={0}, use_global_device_ids=true | all-gather | bytes 245760 | tf_op jit(solution)/shard_map/all_gather | solution.py:360
  17.3 0.0 copy-done.1
  17.3 0.0 copy-start
  17.3 0.1 shard_map.94
  17.4 3.1 %collective-permute-start = (f32[48,128]{1,0:T(8,128)S(1)}, f32[48,128]{1,0:T(8,128)S(1)}, u32[]{:S(2)}, u32[]{:S(2)}) collective-permute-start(f32[48,128]{1,0:T(8,128)S(1)} %shard_map.94), channel_id=1, source_target_pairs={{0,3},{1,0},{2,1},{3,2},{4,7},{5,4},{6,5},{7,6},{8,11},{9,8},{10,9... | collective-permute-start | bytes 73736 | tf_op jit(solution)/shard_map/ppermute | solution.py:358
  20.5 0.0 copy-done.5
  20.5 0.0 copy-done.6
  20.5 0.0 copy-done.2
  20.5 0.0 copy-done.4
  20.5 1.1 %shard_map.95 = (bf16[128,4096]{1,0:T(8,128)(2,1)S(1)}, bf16[4096,128]{1,0:T(8,128)(2,1)S(1)}, f32[8,128]{1,0:T(8,128)S(1)}) custom-call(s32[1,32]{1,0:T(1,128)S(1)} %bitcast.4, f32[2,48,128]{2,1,0:T(8,128)S(1)} %bitcast.3), custom_call_target="tpu_custom_call" | custom-call | tf_op jit(solution)/shard_map/pallas_call | solution.py:32
  21.6 0.5 collective-permute-done.edge_ref
  22.1 0.6 shard_map.96
  22.7 0.0 copy-start.3
  22.7 18.2 %all_to_all.15.refs_0_.lines_ref = bf16[32,16,128]{2,1,0:T(8,128)(2,1)S(1)} all-to-all(bf16[32,16,128]{2,1,0:T(8,128)(2,1)S(1)} %shard_map.96), channel_id=1, replica_groups=mesh['grp'=4,'gx'=32,'gy'=4] {'gx'}, dimensions={0} | all-to-all | bytes 262144 | tf_op jit(solution)/shard_map/all_to_all | solution.py:384
  40.8 0.0 copy-done
  40.8 0.0 copy-done.3
  40.8 2.6 %shard_map.97 = bf16[32,16,128]{2,1,0:T(8,128)(2,1)S(1)} custom-call(bf16[32,16,128]{2,1,0:T(8,128)(2,1)S(1)} %all_to_all.15.refs_0_.lines_ref, bf16[128,4096]{1,0:T(8,128)(2,1)S(1)} %get-tuple-element.18.refs_1_, bf16[4096,128]{1,0:T(8,128)(2,1)S(1)} %get-tuple-element.19.refs_2_, bf16[16,64]{1,0:T(8,128)(2,1)S(1)} %pad_maximum_fusion.refs_3_.small_ref, ...), custom_call_target="tpu_custom_call" | custom-call | tf_op jit(solution)/shard_map/pallas_call | solution.py:32
  43.4 12.7 %all_to_all.16.recv_ref = bf16[32,16,128]{2,1,0:T(8,128)(2,1)S(1)} all-to-all(bf16[32,16,128]{2,1,0:T(8,128)(2,1)S(1)} %shard_map.97), channel_id=1, replica_groups=mesh['grp'=4,'gx'=32,'gy'=4] {'gx'}, dimensions={0} | all-to-all | bytes 262144 | tf_op jit(solution)/shard_map/all_to_all | solution.py:396
  56.1 0.4 shard_map.98
  56.5 18.6 %all_to_all.17.recv_ref = f32[16,8,128]{2,1,0:T(8,128)S(1)} all-to-all(f32[16,8,128]{2,1,0:T(8,128)S(1)} %shard_map.98), channel_id=1, replica_groups=mesh['grp'=4,'gx'=32,'gy'=4] {'grp','gy'}, dimensions={0} | all-to-all | bytes 131072 | tf_op jit(solution)/shard_map/all_to_all | solution.py:404
  75.1 1.1 %shard_map.99 = (f32[4,128]{1,0:T(4,128)}, f32[64,64]{1,0:T(8,128)}, f32[3,2,48,128]{3,2,1,0:T(8,128)}) custom-call(f32[16,8,128]{2,1,0:T(8,128)S(1)} %all_to_all.17.recv_ref, bf16[16,64]{1,0:T(8,128)(2,1)S(1)} %pad_maximum_fusion.refs_3_.small_ref, f32[4,2,48,128]{3,2,1,0:T(8,128)S(1)} %all_gather.3.fields_ref, s32[2,48,128]{2,1,0:T(8,128)S(1)} %copy-done.1, ...), custom_call_target="tpu_custom_call" | custom-call | tf_op jit(solution)/shard_map/pallas_call | solution.py:32
  (2 shorter events, 0.0 us)
Async XLA Ops:
  0.6 16.6 %copy-start.1 = (s32[2,48,128]{2,1,0:T(8,128)S(1)}, s32[2,48,128]{2,1,0:T(8,128)}, u32[]{:S(2)}) copy-start(s32[2,48,128]{2,1,0:T(8,128)} %solid_ref.5) | copy-start | bytes 147460
  0.6 19.8 %copy-start.5 = (bf16[64,3]{0,1:T(4,128)(2,1)S(1)}, bf16[64,3]{0,1:T(4,128)(2,1)}, u32[]{:S(2)}) copy-start(bf16[64,3]{0,1:T(4,128)(2,1)} %param.12) | copy-start | bytes 1156
  0.7 19.8 %copy-start.6 = (bf16[3,64]{1,0:T(4,128)(2,1)S(1)}, bf16[3,64]{1,0:T(4,128)(2,1)}, u32[]{:S(2)}) copy-start(bf16[3,64]{1,0:T(4,128)(2,1)} %param.9) | copy-start | bytes 1156
  0.7 19.8 %copy-start.2 = (f32[1,2,48,128]{3,2,1,0:T(8,128)S(1)}, f32[1,2,48,128]{3,2,1,0:T(8,128)}, u32[]{:S(2)}) copy-start(f32[1,2,48,128]{3,2,1,0:T(8,128)} %param.7) | copy-start | bytes 147460
  0.7 19.8 %copy-start.4 = (s32[32]{0:T(128)S(1)}, s32[32]{0:T(128)}, u32[]{:S(2)}) copy-start(s32[32]{0:T(128)} %param.13) | copy-start | bytes 388
  17.3 23.6 %copy-start = (bf16[2048,128]{1,0:T(8,128)(2,1)S(1)}, bf16[2048,128]{1,0:T(8,128)(2,1)}, u32[]{:S(2)}) copy-start(bf16[2048,128]{1,0:T(8,128)(2,1)} %refs_5_.1) | copy-start | bytes 1572868
  17.4 4.7 %collective-permute-start = (f32[48,128]{1,0:T(8,128)S(1)}, f32[48,128]{1,0:T(8,128)S(1)}, u32[]{:S(2)}, u32[]{:S(2)}) collective-permute-start(f32[48,128]{1,0:T(8,128)S(1)} %shard_map.94), channel_id=1, source_target_pairs={{0,3},{1,0},{2,1},{3,2},{4,7},{5,4},{6,5},{7,6},{8,11},{9,8},{10,9... | collective-permute-start | bytes 73736 | tf_op jit(solution)/shard_map/ppermute | solution.py:358
  22.7 18.2 %copy-start.3 = (bf16[64,64]{1,0:T(8,128)(2,1)S(1)}, bf16[64,64]{1,0:T(8,128)(2,1)}, u32[]{:S(2)}) copy-start(bf16[64,64]{1,0:T(8,128)(2,1)} %refs_4_.1) | copy-start | bytes 24580

commit v9 on v8

--- a/solution.py
+++ b/solution.py
@@ -49,8 +49,8 @@
     return jnp.transpose(jnp.concatenate([rows, pad], axis=0))
 
 
-def edge_kernel(fields_ref, solid_ref, edge_ref):
-    lanes = fields_ref.shape[3]
+def edge_kernel(fields_ref, solid_ref, edge_ref, low_ref, high_ref):
+    rows, lanes = fields_ref.shape[2:]
     lane = iota(edge_ref.shape, 1)
     edge = jnp.zeros(edge_ref.shape, F32)
     for f in range(4):
@@ -59,6 +59,8 @@
             tile = fields_ref[f, z]
             tile = pltpu.roll(tile, place, 1) if place else tile
             edge = jnp.where((lane >> 1) == 2 * f + z, tile, edge)
+            low_ref[2 * f + z : 2 * f + z + 1, :] = fields_ref[f, z, 0:1, :]
+            high_ref[2 * f + z : 2 * f + z + 1, :] = fields_ref[f, z, rows - 1 : rows, :]
     for z in range(2):
         fluid = pltpu.roll(1.0 - solid_ref[z].astype(F32), 16 + z, 1)
         edge = jnp.where(lane == 16 + z, fluid, edge)
@@ -101,13 +103,12 @@
     return results
 
 
-def source_kernel(fields_ref, solid_ref, edge_ref, send_ref, rim_ref):
-    blocks = send_ref.shape[0]
+def source_kernel(fields_ref, solid_ref, edge_ref, send_ref):
+    blocks = send_ref.shape[0] // 8
     rows, lanes = fields_ref.shape[2:]
     lane = iota((rows, lanes), 1)
     end = lane == lanes - 1
     role = lax.axis_index("grp")
-    own = lax.axis_index("gx")
     last = lax.axis_index("gy") == lax.axis_size("gy") - 1
     columns = edge_ref[...]
     centre, sides = [], []
@@ -128,11 +129,6 @@
         fluid = pltpu.roll(1.0 - solid_ref[z].astype(F32), lanes - 1, 1)
         fluids.append(jnp.where(end, pltpu.roll(columns, lanes - 17 - z, 1), fluid))
     results = section(centre, sides, None, fluids)
-    for f in range(4):
-        for z in range(2):
-            for k, row in ((0, 0), (1, rows - 1)):
-                rim_ref[k, 2 * f + z : 2 * f + z + 1, :] = fields_ref[f, z, row : row + 1, :]
-    rims = [rim_ref[k] for k in range(2)]
     values = [jnp.concatenate([p.astype(BF16) for p in parts], axis=1) for parts in results]
     pad = jnp.zeros((128 - 2 * rows, 8 * lanes), BF16)
     stacked = jnp.concatenate(values + [pad], axis=0)
@@ -141,9 +137,7 @@
     wanted = (out_row & 7) * lanes + (out_row >> 3) + role * blocks
     pick = jnp.where(iota(shape, 1) == wanted, 1.0, 0.0).astype(BF16)
     lines = dot(pick, stacked, NT)
-    for b in range(blocks):
-        rim = jnp.where(b > own, rims[1], rims[0])
-        send_ref[b] = jnp.concatenate([lines[8 * b : 8 * b + 8], rim], axis=0).astype(BF16)
+    send_ref[...] = lines.astype(BF16)
 
 
 def neighbour_terms(lines, rows):
@@ -260,16 +254,12 @@
 
 
 def final_kernel(
-    recv_ref, small_ref, fields_ref, solid_ref, edge_ref, lines_ref, grad_ref, mix_ref, new_ref
+    recv_ref, small_ref, fields_ref, solid_ref, edge_ref, below_ref, above_ref, grad_ref, mix_ref,
+    new_ref,
 ):
     rows, lanes = fields_ref.shape[2:]
     lane = iota((rows, lanes), 1)
-    last = lines_ref.shape[0] - 1
-    own = lax.axis_index("gx")
-    rims = []
-    for index, inside in ((own - 1, own > 0), (own + 1, own < last)):
-        message = lines_ref[jnp.minimum(jnp.maximum(index, 0), last)].astype(F32)
-        rims.append(jnp.where(inside, message[8:16], 0.0))
+    rims = [below_ref[...], above_ref[...]]
     place, count = lax.axis_index("gy"), lax.axis_size("gy")
     stack = []
     for f in range(4):
@@ -352,14 +342,18 @@
     none = jnp.zeros((5, lift_weight.shape[1]), BF16)
     small = jnp.concatenate([lift_weight, none, project_weight.T, none], axis=0)
 
-    def shift(array, axis, step):
+    def shift(array, axis, step, ring):
         count = lax.axis_size(axis)
-        pairs = [(i, (i + step) % count) for i in range(count)]
+        pairs = [(i, (i + step) % count) for i in range(count) if ring or 0 <= i + step < count]
         return lax.ppermute(array, axis, pairs)
 
     fields = lax.all_gather(slot_field, "grp", axis=0, tiled=True)
-    edge = call(edge_kernel, jax.ShapeDtypeStruct((rows, lanes), F32), fields, solid)
-    edge = shift(edge, "gy", -1)
+    rim = jax.ShapeDtypeStruct((8, lanes), F32)
+    edge, low, high = call(
+        edge_kernel, [jax.ShapeDtypeStruct((rows, lanes), F32), rim, rim], fields, solid
+    )
+    edge = shift(edge, "gy", -1, True)
+    below, above = shift(high, "gx", 1, False), shift(low, "gx", -1, False)
     table, cells_by_modes, last = call(
         lambda *refs: table_kernel(blocks, *refs),
         [
@@ -370,18 +364,18 @@
         mode_index.reshape(1, -1),
         tile,
     )
-    edge, table, cells_by_modes, last, small = lax.optimization_barrier(
-        (edge, table, cells_by_modes, last, small)
+    edge, below, above, table, cells_by_modes, last, small = lax.optimization_barrier(
+        (edge, below, above, table, cells_by_modes, last, small)
     )
     send = call(
         source_kernel,
-        jax.ShapeDtypeStruct((blocks, 16, 128), BF16),
+        jax.ShapeDtypeStruct((blocks * 8, 128), BF16),
         fields,
         solid,
         edge,
-        scratch=[pltpu.VMEM((2, 8, lanes), F32)],
-    )
-    recv = lines = lax.all_to_all(send, "gx", split_axis=0, concat_axis=0, tiled=True)
+    )
+    send = send.reshape(blocks, 8, 128)
+    recv = lax.all_to_all(send, "gx", split_axis=0, concat_axis=0, tiled=True)
     send = call(
         lambda *refs: line_kernel(scale_dft, loss_scale, *refs),
         jax.ShapeDtypeStruct((blocks, 16, 128), BF16),
@@ -414,7 +408,8 @@
         fields,
         solid,
         edge,
-        lines,
+        below,
+        above,
     )
     return new_velocity, spectral_grad, mix_grad
 

time: 76.5 us -> 82.9 us (1.084)
  starting transfers between devices: 3.07 us -> 7.43 us
  blocking collectives: 66.1 us -> 67.2 us
    all_to_all x1 -> x2, blocking collectives: 12.7 us -> 32.7 us  [local(): recv = lax.all_to_all(send, 'gx', split_axis=0, concat_axis=0, tiled=True)]
    all_to_all x1 -> x0, blocking collectives: 18.2 us -> none  [local(): lax.all_to_all(send, 'gx', split_axis=0, concat_axis=0, tiled=True)]
    ppermute x1 -> x3, starting transfers between devices: 3.07 us -> 7.43 us  [shift(): return lax.ppermute(array, axis, pairs)]
  transfers between devices with their start and end apart: 1 -> 3, of which waited for: 1 -> 0; matrix products, arithmetic and copies ran while one was open for 0% -> 1% of each run, Pallas kernels for 1% -> 1%
where the time goes in v9:
time: 82.9 us; the launch traced here: 82.5 us
  blocking collectives  67.2 us (81%)
  starting transfers between devices  7.43 us (9%)
  Pallas kernels  5.76 us (7%)
    all_to_all x2, blocking collectives, local(): recv = lax.all_to_all(send, 'gx', split_axis=0, concat_axis=0, tiled=True)  32.7 us
    all_to_all x1, blocking collectives, local(): lax.all_to_all(send, ('grp', 'gy'), split_axis=0, concat_axis=0, tiled=True)  17.9 us
    all_gather x1, blocking collectives, local(): fields = lax.all_gather(slot_field, 'grp', axis=0, tiled=True)  16.6 us
    ppermute x3, starting transfers between devices, shift(): return lax.ppermute(array, axis, pairs)  7.43 us
    pallas_call x6, Pallas kernels, call(): pl.pallas_call(kernel, out_shape=out_shape, in_specs=[VMEM] * len(args),...  5.76 us
  transfers between devices with their start and end apart: 3, of which 0 were waited for; matrix products, arithmetic and copies ran while one was open for 1% of the time, Pallas kernels for 1%

profile of v9, /device:TPU:1, one launch (start us, length us, event | category | flops | bytes accessed | tf_op | source)
XLA Modules:
  0.0 82.5 jit_solution(5203262848244880491)
XLA Ops:
  0.6 0.0 copy-start.1
  0.6 0.0 copy-start.2
  0.7 0.0 copy-start
  0.7 16.6 %all_gather.3.fields_ref = f32[4,2,48,128]{3,2,1,0:T(8,128)S(1)} all-gather(f32[1,2,48,128]{3,2,1,0:T(8,128)} %param.7), channel_id=1, replica_groups=mesh['grp'=4,'gx'=32,'gy'=4] {'grp'}, dimensions={0}, use_global_device_ids=true | all-gather | bytes 245760 | tf_op jit(solution)/shard_map/all_gather | solution.py:350
  17.2 0.0 copy-done.1
  17.2 0.1 shard_map.94
  17.4 1.3 %collective-permute-start.1 = (f32[8,128]{1,0:T(8,128)S(1)}, f32[8,128]{1,0:T(8,128)S(1)}, u32[]{:S(2)}, u32[]{:S(2)}) collective-permute-start(f32[8,128]{1,0:T(8,128)S(1)} %get-tuple-element.20), channel_id=1, source_target_pairs={{0,4},{4,8},{8,12},{12,16},{16,20},{20,24},{24,28},{28,32},{32,36}... | collective-permute-start | bytes 12296 | tf_op jit(solution)/shard_map/ppermute | solution.py:348
  18.7 1.3 %collective-permute-start.2 = (f32[8,128]{1,0:T(8,128)S(1)}, f32[8,128]{1,0:T(8,128)S(1)}, u32[]{:S(2)}, u32[]{:S(2)}) collective-permute-start(f32[8,128]{1,0:T(8,128)S(1)} %get-tuple-element.21), channel_id=1, source_target_pairs={{4,0},{8,4},{12,8},{16,12},{20,16},{24,20},{28,24},{32,28},{36,32}... | collective-permute-start | bytes 12296 | tf_op jit(solution)/shard_map/ppermute | solution.py:348
  20.0 4.8 %collective-permute-start = (f32[48,128]{1,0:T(8,128)S(1)}, f32[48,128]{1,0:T(8,128)S(1)}, u32[]{:S(2)}, u32[]{:S(2)}) collective-permute-start(f32[48,128]{1,0:T(8,128)S(1)} %get-tuple-element.19), channel_id=1, source_target_pairs={{0,3},{1,0},{2,1},{3,2},{4,7},{5,4},{6,5},{7,6},{8,11},{9,8},{10,9... | collective-permute-start | bytes 73736 | tf_op jit(solution)/shard_map/ppermute | solution.py:348
  24.8 0.7 pad_maximum_fusion.refs_3_.small_ref
  25.5 0.0 copy-done.2
  25.5 0.0 copy-start.4
  25.5 0.6 copy-done.4
  26.2 1.1 %shard_map.95 = (bf16[128,4096]{1,0:T(8,128)(2,1)S(1)}, bf16[4096,128]{1,0:T(8,128)(2,1)S(1)}, f32[8,128]{1,0:T(8,128)S(1)}) custom-call(s32[1,32]{1,0:T(1,128)S(1)} %bitcast.6, f32[2,48,128]{2,1,0:T(8,128)S(1)} %bitcast.5), custom_call_target="tpu_custom_call" | custom-call | tf_op jit(solution)/shard_map/pallas_call | solution.py:32
  27.3 0.0 collective-permute-done.1.below_ref
  27.3 0.0 collective-permute-done.2.above_ref
  27.3 0.0 collective-permute-done.edge_ref
  27.3 0.6 shard_map.96
  27.9 0.0 copy-start.3
  27.9 20.3 %all_to_all.15.refs_0_ = bf16[32,8,128]{2,1,0:T(8,128)(2,1)S(1)} all-to-all(bf16[32,8,128]{2,1,0:T(8,128)(2,1)S(1)} %bitcast.4), channel_id=1, replica_groups=mesh['grp'=4,'gx'=32,'gy'=4] {'gx'}, dimensions={0} | all-to-all | bytes 131072 | tf_op jit(solution)/shard_map/all_to_all | solution.py:378
  48.2 0.0 copy-done
  48.2 0.0 copy-done.3
  48.2 2.6 %shard_map.97 = bf16[32,16,128]{2,1,0:T(8,128)(2,1)S(1)} custom-call(bf16[32,8,128]{2,1,0:T(8,128)(2,1)S(1)} %all_to_all.15.refs_0_, bf16[128,4096]{1,0:T(8,128)(2,1)S(1)} %get-tuple-element.26.refs_1_, bf16[4096,128]{1,0:T(8,128)(2,1)S(1)} %get-tuple-element.27.refs_2_, bf16[16,64]{1,0:T(8,128)(2,1)S(1)} %pad_maximum_fusion.refs_3_.small_ref, ...), custom_call_target="tpu_custom_call" | custom-call | tf_op jit(solution)/shard_map/pallas_call | solution.py:32
  50.8 12.3 %all_to_all.16.recv_ref = bf16[32,16,128]{2,1,0:T(8,128)(2,1)S(1)} all-to-all(bf16[32,16,128]{2,1,0:T(8,128)(2,1)S(1)} %shard_map.97), channel_id=1, replica_groups=mesh['grp'=4,'gx'=32,'gy'=4] {'gx'}, dimensions={0} | all-to-all | bytes 262144 | tf_op jit(solution)/shard_map/all_to_all | solution.py:390
  63.2 0.4 shard_map.98
  63.5 17.9 %all_to_all.17.recv_ref = f32[16,8,128]{2,1,0:T(8,128)S(1)} all-to-all(f32[16,8,128]{2,1,0:T(8,128)S(1)} %shard_map.98), channel_id=1, replica_groups=mesh['grp'=4,'gx'=32,'gy'=4] {'grp','gy'}, dimensions={0} | all-to-all | bytes 131072 | tf_op jit(solution)/shard_map/all_to_all | solution.py:398
  81.5 1.1 %shard_map.99 = (f32[4,128]{1,0:T(4,128)}, f32[64,64]{1,0:T(8,128)}, f32[3,2,48,128]{3,2,1,0:T(8,128)}) custom-call(f32[16,8,128]{2,1,0:T(8,128)S(1)} %all_to_all.17.recv_ref, bf16[16,64]{1,0:T(8,128)(2,1)S(1)} %pad_maximum_fusion.refs_3_.small_ref, f32[4,2,48,128]{3,2,1,0:T(8,128)S(1)} %all_gather.3.fields_ref, s32[2,48,128]{2,1,0:T(8,128)S(1)} %copy-done.1, ...), custom_call_target="tpu_custom_call" | custom-call | tf_op jit(solution)/shard_map/pallas_call | solution.py:32
  (1 shorter events, 0.0 us)
Async XLA Ops:
  0.6 16.6 %copy-start.1 = (s32[2,48,128]{2,1,0:T(8,128)S(1)}, s32[2,48,128]{2,1,0:T(8,128)}, u32[]{:S(2)}) copy-start(s32[2,48,128]{2,1,0:T(8,128)} %solid_ref.5) | copy-start | bytes 147460
  0.6 24.9 %copy-start.2 = (f32[1,2,48,128]{3,2,1,0:T(8,128)S(1)}, f32[1,2,48,128]{3,2,1,0:T(8,128)}, u32[]{:S(2)}) copy-start(f32[1,2,48,128]{3,2,1,0:T(8,128)} %param.7) | copy-start | bytes 147460
  0.7 47.6 %copy-start = (bf16[2048,128]{1,0:T(8,128)(2,1)S(1)}, bf16[2048,128]{1,0:T(8,128)(2,1)}, u32[]{:S(2)}) copy-start(bf16[2048,128]{1,0:T(8,128)(2,1)} %refs_5_.1) | copy-start | bytes 1572868
  17.4 9.9 %collective-permute-start.1 = (f32[8,128]{1,0:T(8,128)S(1)}, f32[8,128]{1,0:T(8,128)S(1)}, u32[]{:S(2)}, u32[]{:S(2)}) collective-permute-start(f32[8,128]{1,0:T(8,128)S(1)} %get-tuple-element.20), channel_id=1, source_target_pairs={{0,4},{4,8},{8,12},{12,16},{16,20},{20,24},{24,28},{28,32},{32,36}... | collective-permute-start | bytes 12296 | tf_op jit(solution)/shard_map/ppermute | solution.py:348
  18.7 8.6 %collective-permute-start.2 = (f32[8,128]{1,0:T(8,128)S(1)}, f32[8,128]{1,0:T(8,128)S(1)}, u32[]{:S(2)}, u32[]{:S(2)}) collective-permute-start(f32[8,128]{1,0:T(8,128)S(1)} %get-tuple-element.21), channel_id=1, source_target_pairs={{4,0},{8,4},{12,8},{16,12},{20,16},{24,20},{28,24},{32,28},{36,32}... | collective-permute-start | bytes 12296 | tf_op jit(solution)/shard_map/ppermute | solution.py:348
  20.0 7.3 %collective-permute-start = (f32[48,128]{1,0:T(8,128)S(1)}, f32[48,128]{1,0:T(8,128)S(1)}, u32[]{:S(2)}, u32[]{:S(2)}) collective-permute-start(f32[48,128]{1,0:T(8,128)S(1)} %get-tuple-element.19), channel_id=1, source_target_pairs={{0,3},{1,0},{2,1},{3,2},{4,7},{5,4},{6,5},{7,6},{8,11},{9,8},{10,9... | collective-permute-start | bytes 73736 | tf_op jit(solution)/shard_map/ppermute | solution.py:348
  25.5 0.7 copy-start.4
  27.9 20.4 %copy-start.3 = (bf16[64,64]{1,0:T(8,128)(2,1)S(1)}, bf16[64,64]{1,0:T(8,128)(2,1)}, u32[]{:S(2)}) copy-start(bf16[64,64]{1,0:T(8,128)(2,1)} %refs_4_.1) | copy-start | bytes 24580

commit v10 on v8

--- a/solution.py
+++ b/solution.py
@@ -50,9 +50,9 @@
 
 
 def edge_kernel(fields_ref, solid_ref, edge_ref):
-    lanes = fields_ref.shape[3]
-    lane = iota(edge_ref.shape, 1)
-    edge = jnp.zeros(edge_ref.shape, F32)
+    rows, lanes = fields_ref.shape[2:]
+    lane = iota((rows, lanes), 1)
+    edge = jnp.zeros((rows, lanes), F32)
     for f in range(4):
         for z in range(2):
             place = 2 * (2 * f + z)
@@ -62,7 +62,15 @@
     for z in range(2):
         fluid = pltpu.roll(1.0 - solid_ref[z].astype(F32), 16 + z, 1)
         edge = jnp.where(lane == 16 + z, fluid, edge)
-    edge_ref[...] = edge
+    folded = edge[0:8]
+    for k in range(1, rows // 8):
+        folded = folded + pltpu.roll(edge[8 * k : 8 * k + 8], 18 * k, 1)
+    edge_ref[...] = folded
+
+
+def unfolded(folded, rows):
+    parts = [pltpu.roll(folded, 128 - 18 * k, 1) if k else folded for k in range(rows // 8)]
+    return jnp.concatenate(parts, axis=0)
 
 
 def section(centre, sides, rims, fluids):
@@ -109,7 +117,7 @@
     role = lax.axis_index("grp")
     own = lax.axis_index("gx")
     last = lax.axis_index("gy") == lax.axis_size("gy") - 1
-    columns = edge_ref[...]
+    columns = unfolded(edge_ref[...], rows)
     centre, sides = [], []
     for f in range(4):
         centre.append([])
@@ -276,7 +284,7 @@
         below = recv_ref[f * count + jnp.maximum(place - 1, 0)][7:8, :]
         stack += [below, pltpu.roll(below, 64, 1)]
     lower = jnp.where(place > 0, turned(jnp.concatenate(stack, axis=0))[0:rows], 0.0)
-    upper = jnp.where(place < count - 1, edge_ref[...], 0.0)
+    upper = jnp.where(place < count - 1, unfolded(edge_ref[...], rows), 0.0)
     centre, sides = [], []
     for f in range(4):
         centre.append([fields_ref[f, z] for z in range(2)])
@@ -358,7 +366,7 @@
         return lax.ppermute(array, axis, pairs)
 
     fields = lax.all_gather(slot_field, "grp", axis=0, tiled=True)
-    edge = call(edge_kernel, jax.ShapeDtypeStruct((rows, lanes), F32), fields, solid)
+    edge = call(edge_kernel, jax.ShapeDtypeStruct((8, lanes), F32), fields, solid)
     edge = shift(edge, "gy", -1)
     table, cells_by_modes, last = call(
         lambda *refs: table_kernel(blocks, *refs),

time: 76.5 us -> 76.2 us (level)
  no operation moved by 1% of the time
where the time goes in v10:
time: 76.2 us; the launch traced here: 75.9 us
  blocking collectives  66 us (87%)
  Pallas kernels  5.86 us (8%)
  starting transfers between devices  2.94 us (4%)
  between operations  0.77 us (1%)
    all_to_all x1, blocking collectives, local(): lax.all_to_all(send, 'gx', split_axis=0, concat_axis=0, tiled=True)  18.5 us
    all_to_all x1, blocking collectives, local(): lax.all_to_all(send, ('grp', 'gy'), split_axis=0, concat_axis=0, tiled=True)  18.2 us
    all_gather x1, blocking collectives, local(): fields = lax.all_gather(slot_field, 'grp', axis=0, tiled=True)  16.6 us
    all_to_all x1, blocking collectives, local(): recv = lax.all_to_all(send, 'gx', split_axis=0, concat_axis=0, tiled=True)  12.8 us
    pallas_call x6, Pallas kernels, call(): pl.pallas_call(kernel, out_shape=out_shape, in_specs=[VMEM] * len(args),...  5.86 us
    ppermute x1, starting transfers between devices, shift(): return lax.ppermute(array, axis, pairs)  2.94 us
  transfers between devices with their start and end apart: 1, of which 1 were waited for; matrix products, arithmetic and copies ran while one was open for 0% of the time, Pallas kernels for 1%

profile of v10, /device:TPU:1, one launch (start us, length us, event | category | flops | bytes accessed | tf_op | source)
XLA Modules:
  0.0 75.9 jit_solution(12887789501426811692)
XLA Ops:
  0.6 0.0 copy-start.1
  0.6 0.0 copy-start.5
  0.7 0.0 copy-start.6
  0.7 0.0 copy-start.2
  0.7 0.0 copy-start.4
  0.7 16.6 %all_gather.3.fields_ref = f32[4,2,48,128]{3,2,1,0:T(8,128)S(1)} all-gather(f32[1,2,48,128]{3,2,1,0:T(8,128)} %param.7), channel_id=1, replica_groups=mesh['grp'=4,'gx'=32,'gy'=4] {'grp'}, dimensions={0}, use_global_device_ids=true | all-gather | bytes 245760 | tf_op jit(solution)/shard_map/all_gather | solution.py:368
  17.3 0.0 copy-done.1
  17.3 0.0 copy-start
  17.3 0.2 shard_map.94
  17.4 2.9 %collective-permute-start = (f32[8,128]{1,0:T(8,128)S(1)}, f32[8,128]{1,0:T(8,128)S(1)}, u32[]{:S(2)}, u32[]{:S(2)}) collective-permute-start(f32[8,128]{1,0:T(8,128)S(1)} %shard_map.94), channel_id=1, source_target_pairs={{0,3},{1,0},{2,1},{3,2},{4,7},{5,4},{6,5},{7,6},{8,11},{9,8},{10,9... | collective-permute-start | bytes 12296 | tf_op jit(solution)/shard_map/ppermute | solution.py:366
  20.4 0.0 copy-done.5
  20.4 0.0 copy-done.6
  20.4 0.0 copy-done.2
  20.4 0.0 copy-done.4
  20.4 1.1 %shard_map.95 = (bf16[128,4096]{1,0:T(8,128)(2,1)S(1)}, bf16[4096,128]{1,0:T(8,128)(2,1)S(1)}, f32[8,128]{1,0:T(8,128)S(1)}) custom-call(s32[1,32]{1,0:T(1,128)S(1)} %bitcast.4, f32[2,48,128]{2,1,0:T(8,128)S(1)} %bitcast.3), custom_call_target="tpu_custom_call" | custom-call | tf_op jit(solution)/shard_map/pallas_call | solution.py:32
  21.5 0.2 collective-permute-done.edge_ref
  21.8 0.6 shard_map.96
  22.4 0.0 copy-start.3
  22.4 18.5 %all_to_all.15.refs_0_.lines_ref = bf16[32,16,128]{2,1,0:T(8,128)(2,1)S(1)} all-to-all(bf16[32,16,128]{2,1,0:T(8,128)(2,1)S(1)} %shard_map.96), channel_id=1, replica_groups=mesh['grp'=4,'gx'=32,'gy'=4] {'gx'}, dimensions={0} | all-to-all | bytes 262144 | tf_op jit(solution)/shard_map/all_to_all | solution.py:392
  40.9 0.0 copy-done
  40.9 0.0 copy-done.3
  40.9 2.6 %shard_map.97 = bf16[32,16,128]{2,1,0:T(8,128)(2,1)S(1)} custom-call(bf16[32,16,128]{2,1,0:T(8,128)(2,1)S(1)} %all_to_all.15.refs_0_.lines_ref, bf16[128,4096]{1,0:T(8,128)(2,1)S(1)} %get-tuple-element.18.refs_1_, bf16[4096,128]{1,0:T(8,128)(2,1)S(1)} %get-tuple-element.19.refs_2_, bf16[16,64]{1,0:T(8,128)(2,1)S(1)} %pad_maximum_fusion.refs_3_.small_ref, ...), custom_call_target="tpu_custom_call" | custom-call | tf_op jit(solution)/shard_map/pallas_call | solution.py:32
  43.5 12.8 %all_to_all.16.recv_ref = bf16[32,16,128]{2,1,0:T(8,128)(2,1)S(1)} all-to-all(bf16[32,16,128]{2,1,0:T(8,128)(2,1)S(1)} %shard_map.97), channel_id=1, replica_groups=mesh['grp'=4,'gx'=32,'gy'=4] {'gx'}, dimensions={0} | all-to-all | bytes 262144 | tf_op jit(solution)/shard_map/all_to_all | solution.py:404
  56.3 0.4 shard_map.98
  56.6 18.2 %all_to_all.17.recv_ref = f32[16,8,128]{2,1,0:T(8,128)S(1)} all-to-all(f32[16,8,128]{2,1,0:T(8,128)S(1)} %shard_map.98), channel_id=1, replica_groups=mesh['grp'=4,'gx'=32,'gy'=4] {'grp','gy'}, dimensions={0} | all-to-all | bytes 131072 | tf_op jit(solution)/shard_map/all_to_all | solution.py:412
  74.8 1.1 %shard_map.99 = (f32[4,128]{1,0:T(4,128)}, f32[64,64]{1,0:T(8,128)}, f32[3,2,48,128]{3,2,1,0:T(8,128)}) custom-call(f32[16,8,128]{2,1,0:T(8,128)S(1)} %all_to_all.17.recv_ref, bf16[16,64]{1,0:T(8,128)(2,1)S(1)} %pad_maximum_fusion.refs_3_.small_ref, f32[4,2,48,128]{3,2,1,0:T(8,128)S(1)} %all_gather.3.fields_ref, s32[2,48,128]{2,1,0:T(8,128)S(1)} %copy-done.1, ...), custom_call_target="tpu_custom_call" | custom-call | tf_op jit(solution)/shard_map/pallas_call | solution.py:32
  (2 shorter events, 0.0 us)
Async XLA Ops:
  0.6 16.6 %copy-start.1 = (s32[2,48,128]{2,1,0:T(8,128)S(1)}, s32[2,48,128]{2,1,0:T(8,128)}, u32[]{:S(2)}) copy-start(s32[2,48,128]{2,1,0:T(8,128)} %solid_ref.5) | copy-start | bytes 147460
  0.6 19.8 %copy-start.5 = (bf16[64,3]{0,1:T(4,128)(2,1)S(1)}, bf16[64,3]{0,1:T(4,128)(2,1)}, u32[]{:S(2)}) copy-start(bf16[64,3]{0,1:T(4,128)(2,1)} %param.12) | copy-start | bytes 1156
  0.7 19.8 %copy-start.6 = (bf16[3,64]{1,0:T(4,128)(2,1)S(1)}, bf16[3,64]{1,0:T(4,128)(2,1)}, u32[]{:S(2)}) copy-start(bf16[3,64]{1,0:T(4,128)(2,1)} %param.9) | copy-start | bytes 1156
  0.7 19.8 %copy-start.2 = (f32[1,2,48,128]{3,2,1,0:T(8,128)S(1)}, f32[1,2,48,128]{3,2,1,0:T(8,128)}, u32[]{:S(2)}) copy-start(f32[1,2,48,128]{3,2,1,0:T(8,128)} %param.7) | copy-start | bytes 147460
  0.7 19.8 %copy-start.4 = (s32[32]{0:T(128)S(1)}, s32[32]{0:T(128)}, u32[]{:S(2)}) copy-start(s32[32]{0:T(128)} %param.13) | copy-start | bytes 388
  17.3 23.6 %copy-start = (bf16[2048,128]{1,0:T(8,128)(2,1)S(1)}, bf16[2048,128]{1,0:T(8,128)(2,1)}, u32[]{:S(2)}) copy-start(bf16[2048,128]{1,0:T(8,128)(2,1)} %refs_5_.1) | copy-start | bytes 1572868
  17.4 4.3 %collective-permute-start = (f32[8,128]{1,0:T(8,128)S(1)}, f32[8,128]{1,0:T(8,128)S(1)}, u32[]{:S(2)}, u32[]{:S(2)}) collective-permute-start(f32[8,128]{1,0:T(8,128)S(1)} %shard_map.94), channel_id=1, source_target_pairs={{0,3},{1,0},{2,1},{3,2},{4,7},{5,4},{6,5},{7,6},{8,11},{9,8},{10,9... | collective-permute-start | bytes 12296 | tf_op jit(solution)/shard_map/ppermute | solution.py:366
  22.4 18.5 %copy-start.3 = (bf16[64,64]{1,0:T(8,128)(2,1)S(1)}, bf16[64,64]{1,0:T(8,128)(2,1)}, u32[]{:S(2)}) copy-start(bf16[64,64]{1,0:T(8,128)(2,1)} %refs_4_.1) | copy-start | bytes 24580

commit v11 on v10

--- a/solution.py
+++ b/solution.py
@@ -360,14 +360,14 @@
     none = jnp.zeros((5, lift_weight.shape[1]), BF16)
     small = jnp.concatenate([lift_weight, none, project_weight.T, none], axis=0)
 
-    def shift(array, axis, step):
-        count = lax.axis_size(axis)
-        pairs = [(i, (i + step) % count) for i in range(count)]
-        return lax.ppermute(array, axis, pairs)
-
     fields = lax.all_gather(slot_field, "grp", axis=0, tiled=True)
     edge = call(edge_kernel, jax.ShapeDtypeStruct((8, lanes), F32), fields, solid)
-    edge = shift(edge, "gy", -1)
+    groups, count = lax.axis_size("grp"), lax.axis_size("gy")
+    pairs = []
+    for g in range(groups):
+        pairs += [(g * count + i + 1, g * count + i) for i in range(count - 1)]
+        pairs.append(((g + groups // 2) % groups * count, g * count + count - 1))
+    edge = lax.ppermute(edge, ("grp", "gy"), pairs)
     table, cells_by_modes, last = call(
         lambda *refs: table_kernel(blocks, *refs),
         [

time: 76.2 us -> 75.7 us (level)
  blocking collectives: 66 us -> 63.3 us
  starting transfers between devices: 2.94 us -> 5.29 us
    all_to_all x1, blocking collectives: 18.2 us -> 15.2 us  [local(): lax.all_to_all(send, ('grp', 'gy'), split_axis=0, concat_axis=0, tiled=True)]
    ppermute x1, starting transfers between devices: 2.94 us -> 5.29 us  [local(): edge = lax.ppermute(edge, ('grp', 'gy'), pairs)]
  transfers between devices with their start and end apart: 1 -> 1, of which waited for: 1 -> 0; matrix products, arithmetic and copies ran while one was open for 0% -> 0% of each run, Pallas kernels for 1% -> 1%
where the time goes in v11:
time: 75.7 us; the launch traced here: 75.3 us
  blocking collectives  63.3 us (84%)
  Pallas kernels  5.87 us (8%)
  starting transfers between devices  5.29 us (7%)
  between operations  0.77 us (1%)
    all_to_all x1, blocking collectives, local(): lax.all_to_all(send, 'gx', split_axis=0, concat_axis=0, tiled=True)  18.7 us
    all_gather x1, blocking collectives, local(): fields = lax.all_gather(slot_field, 'grp', axis=0, tiled=True)  16.6 us
    all_to_all x1, blocking collectives, local(): lax.all_to_all(send, ('grp', 'gy'), split_axis=0, concat_axis=0, tiled=True)  15.2 us
    all_to_all x1, blocking collectives, local(): recv = lax.all_to_all(send, 'gx', split_axis=0, concat_axis=0, tiled=True)  12.8 us
    pallas_call x6, Pallas kernels, call(): pl.pallas_call(kernel, out_shape=out_shape, in_specs=[VMEM] * len(args),...  5.87 us
    ppermute x1, starting transfers between devices, local(): edge = lax.ppermute(edge, ('grp', 'gy'), pairs)  5.29 us
  transfers between devices with their start and end apart: 1, of which 0 were waited for; matrix products, arithmetic and copies ran while one was open for 0% of the time, Pallas kernels for 1%

profile of v11, /device:TPU:1, one launch (start us, length us, event | category | flops | bytes accessed | tf_op | source)
XLA Modules:
  0.0 75.3 jit_solution(10659585554928186105)
XLA Ops:
  0.6 0.0 copy-start.1
  0.6 0.0 copy-start.5
  0.7 0.0 copy-start.6
  0.7 0.0 copy-start.2
  0.7 0.0 copy-start.4
  0.7 16.6 %all_gather.3.fields_ref = f32[4,2,48,128]{3,2,1,0:T(8,128)S(1)} all-gather(f32[1,2,48,128]{3,2,1,0:T(8,128)} %param.7), channel_id=1, replica_groups=mesh['grp'=4,'gx'=32,'gy'=4] {'grp'}, dimensions={0}, use_global_device_ids=true | all-gather | bytes 245760 | tf_op jit(solution)/shard_map/all_gather | solution.py:363
  17.3 0.0 copy-done.1
  17.3 0.0 copy-start
  17.3 0.2 shard_map.94
  17.4 5.3 %collective-permute-start = (f32[8,128]{1,0:T(8,128)S(1)}, f32[8,128]{1,0:T(8,128)S(1)}, u32[]{:S(2)}, u32[]{:S(2)}) collective-permute-start(f32[8,128]{1,0:T(8,128)S(1)} %shard_map.94), channel_id=1, source_target_pairs={{1,0},{2,1},{3,2},{256,3},{129,128},{130,129},{131,130},{384,131},... | collective-permute-start | bytes 12296 | tf_op jit(solution)/shard_map/ppermute | solution.py:370
  22.7 0.0 copy-done.5
  22.8 0.0 copy-done.6
  22.8 0.0 copy-done.2
  22.8 0.0 copy-done.4
  22.8 1.1 %shard_map.95 = (bf16[128,4096]{1,0:T(8,128)(2,1)S(1)}, bf16[4096,128]{1,0:T(8,128)(2,1)S(1)}, f32[8,128]{1,0:T(8,128)S(1)}) custom-call(s32[1,32]{1,0:T(1,128)S(1)} %bitcast.4, f32[2,48,128]{2,1,0:T(8,128)S(1)} %bitcast.3), custom_call_target="tpu_custom_call" | custom-call | tf_op jit(solution)/shard_map/pallas_call | solution.py:32
  23.9 0.0 collective-permute-done.edge_ref
  23.9 0.6 shard_map.96
  24.5 0.0 copy-start.3
  24.5 18.7 %all_to_all.15.refs_0_.lines_ref = bf16[32,16,128]{2,1,0:T(8,128)(2,1)S(1)} all-to-all(bf16[32,16,128]{2,1,0:T(8,128)(2,1)S(1)} %shard_map.96), channel_id=1, replica_groups=mesh['grp'=4,'gx'=32,'gy'=4] {'gx'}, dimensions={0} | all-to-all | bytes 262144 | tf_op jit(solution)/shard_map/all_to_all | solution.py:392
  43.2 0.0 copy-done
  43.2 0.0 copy-done.3
  43.2 2.6 %shard_map.97 = bf16[32,16,128]{2,1,0:T(8,128)(2,1)S(1)} custom-call(bf16[32,16,128]{2,1,0:T(8,128)(2,1)S(1)} %all_to_all.15.refs_0_.lines_ref, bf16[128,4096]{1,0:T(8,128)(2,1)S(1)} %get-tuple-element.18.refs_1_, bf16[4096,128]{1,0:T(8,128)(2,1)S(1)} %get-tuple-element.19.refs_2_, bf16[16,64]{1,0:T(8,128)(2,1)S(1)} %pad_maximum_fusion.refs_3_.small_ref, ...), custom_call_target="tpu_custom_call" | custom-call | tf_op jit(solution)/shard_map/pallas_call | solution.py:32
  45.8 12.8 %all_to_all.16.recv_ref = bf16[32,16,128]{2,1,0:T(8,128)(2,1)S(1)} all-to-all(bf16[32,16,128]{2,1,0:T(8,128)(2,1)S(1)} %shard_map.97), channel_id=1, replica_groups=mesh['grp'=4,'gx'=32,'gy'=4] {'gx'}, dimensions={0} | all-to-all | bytes 262144 | tf_op jit(solution)/shard_map/all_to_all | solution.py:404
  58.6 0.4 shard_map.98
  59.0 15.2 %all_to_all.17.recv_ref = f32[16,8,128]{2,1,0:T(8,128)S(1)} all-to-all(f32[16,8,128]{2,1,0:T(8,128)S(1)} %shard_map.98), channel_id=1, replica_groups=mesh['grp'=4,'gx'=32,'gy'=4] {'grp','gy'}, dimensions={0} | all-to-all | bytes 131072 | tf_op jit(solution)/shard_map/all_to_all | solution.py:412
  74.3 1.1 %shard_map.99 = (f32[4,128]{1,0:T(4,128)}, f32[64,64]{1,0:T(8,128)}, f32[3,2,48,128]{3,2,1,0:T(8,128)}) custom-call(f32[16,8,128]{2,1,0:T(8,128)S(1)} %all_to_all.17.recv_ref, bf16[16,64]{1,0:T(8,128)(2,1)S(1)} %pad_maximum_fusion.refs_3_.small_ref, f32[4,2,48,128]{3,2,1,0:T(8,128)S(1)} %all_gather.3.fields_ref, s32[2,48,128]{2,1,0:T(8,128)S(1)} %copy-done.1, ...), custom_call_target="tpu_custom_call" | custom-call | tf_op jit(solution)/shard_map/pallas_call | solution.py:32
  (2 shorter events, 0.0 us)
Async XLA Ops:
  0.6 16.6 %copy-start.1 = (s32[2,48,128]{2,1,0:T(8,128)S(1)}, s32[2,48,128]{2,1,0:T(8,128)}, u32[]{:S(2)}) copy-start(s32[2,48,128]{2,1,0:T(8,128)} %solid_ref.5) | copy-start | bytes 147460
  0.6 22.1 %copy-start.5 = (bf16[64,3]{0,1:T(4,128)(2,1)S(1)}, bf16[64,3]{0,1:T(4,128)(2,1)}, u32[]{:S(2)}) copy-start(bf16[64,3]{0,1:T(4,128)(2,1)} %param.12) | copy-start | bytes 1156
  0.7 22.1 %copy-start.6 = (bf16[3,64]{1,0:T(4,128)(2,1)S(1)}, bf16[3,64]{1,0:T(4,128)(2,1)}, u32[]{:S(2)}) copy-start(bf16[3,64]{1,0:T(4,128)(2,1)} %param.9) | copy-start | bytes 1156
  0.7 22.1 %copy-start.2 = (f32[1,2,48,128]{3,2,1,0:T(8,128)S(1)}, f32[1,2,48,128]{3,2,1,0:T(8,128)}, u32[]{:S(2)}) copy-start(f32[1,2,48,128]{3,2,1,0:T(8,128)} %param.7) | copy-start | bytes 147460
  0.7 22.1 %copy-start.4 = (s32[32]{0:T(128)S(1)}, s32[32]{0:T(128)}, u32[]{:S(2)}) copy-start(s32[32]{0:T(128)} %param.13) | copy-start | bytes 388
  17.3 26.0 %copy-start = (bf16[2048,128]{1,0:T(8,128)(2,1)S(1)}, bf16[2048,128]{1,0:T(8,128)(2,1)}, u32[]{:S(2)}) copy-start(bf16[2048,128]{1,0:T(8,128)(2,1)} %refs_5_.1) | copy-start | bytes 1572868
  17.4 6.5 %collective-permute-start = (f32[8,128]{1,0:T(8,128)S(1)}, f32[8,128]{1,0:T(8,128)S(1)}, u32[]{:S(2)}, u32[]{:S(2)}) collective-permute-start(f32[8,128]{1,0:T(8,128)S(1)} %shard_map.94), channel_id=1, source_target_pairs={{1,0},{2,1},{3,2},{256,3},{129,128},{130,129},{131,130},{384,131},... | collective-permute-start | bytes 12296 | tf_op jit(solution)/shard_map/ppermute | solution.py:370
  24.5 18.7 %copy-start.3 = (bf16[64,64]{1,0:T(8,128)(2,1)S(1)}, bf16[64,64]{1,0:T(8,128)(2,1)}, u32[]{:S(2)}) copy-start(bf16[64,64]{1,0:T(8,128)(2,1)} %refs_4_.1) | copy-start | bytes 24580

commit v12 on v11

--- a/solution.py
+++ b/solution.py
@@ -109,12 +109,11 @@
     return results
 
 
-def source_kernel(fields_ref, solid_ref, edge_ref, send_ref, rim_ref):
+def source_kernel(fields_ref, solid_ref, edge_ref, pick_ref, send_ref, rim_ref):
     blocks = send_ref.shape[0]
     rows, lanes = fields_ref.shape[2:]
     lane = iota((rows, lanes), 1)
     end = lane == lanes - 1
-    role = lax.axis_index("grp")
     own = lax.axis_index("gx")
     last = lax.axis_index("gy") == lax.axis_size("gy") - 1
     columns = unfolded(edge_ref[...], rows)
@@ -144,11 +143,7 @@
     values = [jnp.concatenate([p.astype(BF16) for p in parts], axis=1) for parts in results]
     pad = jnp.zeros((128 - 2 * rows, 8 * lanes), BF16)
     stacked = jnp.concatenate(values + [pad], axis=0)
-    shape = (blocks * 8, 8 * lanes)
-    out_row = iota(shape, 0)
-    wanted = (out_row & 7) * lanes + (out_row >> 3) + role * blocks
-    pick = jnp.where(iota(shape, 1) == wanted, 1.0, 0.0).astype(BF16)
-    lines = dot(pick, stacked, NT)
+    lines = dot(pick_ref[...], stacked, NT)
     for b in range(blocks):
         rim = jnp.where(b > own, rims[1], rims[0])
         send_ref[b] = jnp.concatenate([lines[8 * b : 8 * b + 8], rim], axis=0).astype(BF16)
@@ -316,10 +311,13 @@
     mix_ref[...] = mix[:, 0:64]
 
 
-def table_kernel(blocks, mode_ref, tile_ref, table_ref, turned_ref, last_ref):
+def table_kernel(blocks, mode_ref, tile_ref, table_ref, turned_ref, last_ref, pick_ref):
     rows, lanes = tile_ref.shape[1:]
     ends = [as_row(tile_ref[z, :, lanes - 1 : lanes], (rows, lanes)) for z in range(2)]
     last_ref[...] = jnp.broadcast_to(ends[0] + pltpu.roll(ends[1], 64, 1), last_ref.shape)
+    wanted = iota(pick_ref.shape, 0)
+    wanted = (wanted & 7) * lanes + (wanted >> 3) + lax.axis_index("grp") * blocks
+    pick_ref[...] = jnp.where(iota(pick_ref.shape, 1) == wanted, 1.0, 0.0).astype(BF16)
     modes = mode_ref.shape[1]
     unit = 2.0 * math.pi / (blocks * rows)
     square = (modes, modes)
@@ -368,18 +366,19 @@
         pairs += [(g * count + i + 1, g * count + i) for i in range(count - 1)]
         pairs.append(((g + groups // 2) % groups * count, g * count + count - 1))
     edge = lax.ppermute(edge, ("grp", "gy"), pairs)
-    table, cells_by_modes, last = call(
+    table, cells_by_modes, last, pick = call(
         lambda *refs: table_kernel(blocks, *refs),
         [
             jax.ShapeDtypeStruct((128, blocks * 128), BF16),
             jax.ShapeDtypeStruct((blocks * 128, 128), BF16),
             jax.ShapeDtypeStruct((8, lanes), F32),
+            jax.ShapeDtypeStruct((blocks * 8, 8 * lanes), BF16),
         ],
         mode_index.reshape(1, -1),
         tile,
     )
-    edge, table, cells_by_modes, last, small = lax.optimization_barrier(
-        (edge, table, cells_by_modes, last, small)
+    edge, table, cells_by_modes, last, small, pick = lax.optimization_barrier(
+        (edge, table, cells_by_modes, last, small, pick)
     )
     send = call(
         source_kernel,
@@ -387,6 +386,7 @@
         fields,
         solid,
         edge,
+        pick,
         scratch=[pltpu.VMEM((2, 8, lanes), F32)],
     )
     recv = lines = lax.all_to_all(send, "gx", split_axis=0, concat_axis=0, tiled=True)

time: 75.7 us -> 75.5 us (level)
  blocking collectives: 63.3 us -> 61.7 us
  local copies, waits for them, and re-layouts: 0.03 us -> 1.34 us
    all_to_all x1, blocking collectives: 15.2 us -> 13.4 us  [local(): lax.all_to_all(send, ('grp', 'gy'), split_axis=0, concat_axis=0, tiled=True)]
    unnamed x14, local copies, waits for them, and re-layouts: 0.03 us -> 1.33 us
  transfers between devices with their start and end apart: 1 -> 1, of which waited for: 0 -> 0; matrix products, arithmetic and copies ran while one was open for 0% -> 0% of each run, Pallas kernels for 1% -> 2%
where the time goes in v12:
time: 75.5 us; the launch traced here: 75.1 us
  blocking collectives  61.7 us (82%)
  Pallas kernels  6.01 us (8%)
  starting transfers between devices  5.29 us (7%)
  local copies, waits for them, and re-layouts  1.34 us (2%)
    all_to_all x1, blocking collectives, local(): lax.all_to_all(send, 'gx', split_axis=0, concat_axis=0, tiled=True)  18.6 us
    all_gather x1, blocking collectives, local(): fields = lax.all_gather(slot_field, 'grp', axis=0, tiled=True)  16.4 us
    all_to_all x1, blocking collectives, local(): lax.all_to_all(send, ('grp', 'gy'), split_axis=0, concat_axis=0, tiled=True)  13.4 us
    all_to_all x1, blocking collectives, local(): recv = lax.all_to_all(send, 'gx', split_axis=0, concat_axis=0, tiled=True)  13.3 us
    pallas_call x6, Pallas kernels, call(): pl.pallas_call(kernel, out_shape=out_shape, in_specs=[VMEM] * len(args),...  6.01 us
    ppermute x1, starting transfers between devices, local(): edge = lax.ppermute(edge, ('grp', 'gy'), pairs)  5.29 us
  transfers between devices with their start and end apart: 1, of which 0 were waited for; matrix products, arithmetic and copies ran while one was open for 0% of the time, Pallas kernels for 2%

profile of v12, /device:TPU:1, one launch (start us, length us, event | category | flops | bytes accessed | tf_op | source)
XLA Modules:
  0.0 75.1 jit_solution(3443141733973138927)
XLA Ops:
  0.6 0.0 copy-start.1
  0.6 16.4 %all_gather.3.fields_ref = f32[4,2,48,128]{3,2,1,0:T(8,128)S(1)} all-gather(f32[1,2,48,128]{3,2,1,0:T(8,128)} %param.7), channel_id=1, replica_groups=mesh['grp'=4,'gx'=32,'gy'=4] {'grp'}, dimensions={0}, use_global_device_ids=true | all-gather | bytes 245760 | tf_op jit(solution)/shard_map/all_gather | solution.py:361
  17.1 0.0 copy-done.1
  17.1 0.0 copy-start.2
  17.1 0.2 shard_map.94
  17.3 5.3 %collective-permute-start = (f32[8,128]{1,0:T(8,128)S(1)}, f32[8,128]{1,0:T(8,128)S(1)}, u32[]{:S(2)}, u32[]{:S(2)}) collective-permute-start(f32[8,128]{1,0:T(8,128)S(1)} %shard_map.94), channel_id=1, source_target_pairs={{1,0},{2,1},{3,2},{256,3},{129,128},{130,129},{131,130},{384,131},... | collective-permute-start | bytes 12296 | tf_op jit(solution)/shard_map/ppermute | solution.py:368
  22.6 0.0 copy-start.5
  22.6 0.0 copy-start.6
  22.6 0.6 copy-done.5
  23.2 0.0 copy-done.6
  23.3 0.0 copy-start.4
  23.3 0.0 copy-done.2
  23.3 0.6 copy-done.4
  23.9 1.2 %shard_map.95 = (bf16[128,4096]{1,0:T(8,128)(2,1)S(1)}, bf16[4096,128]{1,0:T(8,128)(2,1)S(1)}, f32[8,128]{1,0:T(8,128)S(1)}, bf16[256,1024]{1,0:T(8,128)(2,1)S(1)}) custom-call(s32[1,32]{1,0:T(1,128)S(1)} %bitcast.4, f32[2,48,128]{2,1,0:T(8,128)S(1)} %bitcast.3), custom_call_target="tpu_custom_call" | custom-call | tf_op jit(solution)/shard_map/pallas_call | solution.py:32
  25.2 0.0 collective-permute-done.edge_ref
  25.2 0.0 copy-start
  25.2 0.6 shard_map.96
  25.8 0.0 copy-start.3
  25.8 18.6 %all_to_all.15.refs_0_.lines_ref = bf16[32,16,128]{2,1,0:T(8,128)(2,1)S(1)} all-to-all(bf16[32,16,128]{2,1,0:T(8,128)(2,1)S(1)} %shard_map.96), channel_id=1, replica_groups=mesh['grp'=4,'gx'=32,'gy'=4] {'gx'}, dimensions={0} | all-to-all | bytes 262144 | tf_op jit(solution)/shard_map/all_to_all | solution.py:392
  44.4 0.0 copy-done
  44.4 0.0 copy-done.3
  44.4 2.6 %shard_map.97 = bf16[32,16,128]{2,1,0:T(8,128)(2,1)S(1)} custom-call(bf16[32,16,128]{2,1,0:T(8,128)(2,1)S(1)} %all_to_all.15.refs_0_.lines_ref, bf16[128,4096]{1,0:T(8,128)(2,1)S(1)} %get-tuple-element.22.refs_1_, bf16[4096,128]{1,0:T(8,128)(2,1)S(1)} %get-tuple-element.23.refs_2_, bf16[16,64]{1,0:T(8,128)(2,1)S(1)} %pad_maximum_fusion.refs_3_.small_ref, ...), custom_call_target="tpu_custom_call" | custom-call | tf_op jit(solution)/shard_map/pallas_call | solution.py:32
  47.0 13.3 %all_to_all.16.recv_ref = bf16[32,16,128]{2,1,0:T(8,128)(2,1)S(1)} all-to-all(bf16[32,16,128]{2,1,0:T(8,128)(2,1)S(1)} %shard_map.97), channel_id=1, replica_groups=mesh['grp'=4,'gx'=32,'gy'=4] {'gx'}, dimensions={0} | all-to-all | bytes 262144 | tf_op jit(solution)/shard_map/all_to_all | solution.py:404
  60.3 0.4 shard_map.98
  60.7 13.4 %all_to_all.17.recv_ref = f32[16,8,128]{2,1,0:T(8,128)S(1)} all-to-all(f32[16,8,128]{2,1,0:T(8,128)S(1)} %shard_map.98), channel_id=1, replica_groups=mesh['grp'=4,'gx'=32,'gy'=4] {'grp','gy'}, dimensions={0} | all-to-all | bytes 131072 | tf_op jit(solution)/shard_map/all_to_all | solution.py:412
  74.1 1.1 %shard_map.99 = (f32[4,128]{1,0:T(4,128)}, f32[64,64]{1,0:T(8,128)}, f32[3,2,48,128]{3,2,1,0:T(8,128)}) custom-call(f32[16,8,128]{2,1,0:T(8,128)S(1)} %all_to_all.17.recv_ref, bf16[16,64]{1,0:T(8,128)(2,1)S(1)} %pad_maximum_fusion.refs_3_.small_ref, f32[4,2,48,128]{3,2,1,0:T(8,128)S(1)} %all_gather.3.fields_ref, s32[2,48,128]{2,1,0:T(8,128)S(1)} %copy-done.1, ...), custom_call_target="tpu_custom_call" | custom-call | tf_op jit(solution)/shard_map/pallas_call | solution.py:32
  (2 shorter events, 0.0 us)
Async XLA Ops:
  0.6 16.5 %copy-start.1 = (s32[2,48,128]{2,1,0:T(8,128)S(1)}, s32[2,48,128]{2,1,0:T(8,128)}, u32[]{:S(2)}) copy-start(s32[2,48,128]{2,1,0:T(8,128)} %solid_ref.5) | copy-start | bytes 147460
  17.1 6.2 %copy-start.2 = (f32[1,2,48,128]{3,2,1,0:T(8,128)S(1)}, f32[1,2,48,128]{3,2,1,0:T(8,128)}, u32[]{:S(2)}) copy-start(f32[1,2,48,128]{3,2,1,0:T(8,128)} %param.7) | copy-start | bytes 147460
  17.3 7.9 %collective-permute-start = (f32[8,128]{1,0:T(8,128)S(1)}, f32[8,128]{1,0:T(8,128)S(1)}, u32[]{:S(2)}, u32[]{:S(2)}) collective-permute-start(f32[8,128]{1,0:T(8,128)S(1)} %shard_map.94), channel_id=1, source_target_pairs={{1,0},{2,1},{3,2},{256,3},{129,128},{130,129},{131,130},{384,131},... | collective-permute-start | bytes 12296 | tf_op jit(solution)/shard_map/ppermute | solution.py:368
  22.6 0.7 copy-start.5
  22.6 0.7 copy-start.6
  23.3 0.7 copy-start.4
  25.2 19.3 %copy-start = (bf16[2048,128]{1,0:T(8,128)(2,1)S(1)}, bf16[2048,128]{1,0:T(8,128)(2,1)}, u32[]{:S(2)}) copy-start(bf16[2048,128]{1,0:T(8,128)(2,1)} %refs_5_.1) | copy-start | bytes 1572868
  25.8 18.7 %copy-start.3 = (bf16[64,64]{1,0:T(8,128)(2,1)S(1)}, bf16[64,64]{1,0:T(8,128)(2,1)}, u32[]{:S(2)}) copy-start(bf16[64,64]{1,0:T(8,128)(2,1)} %refs_4_.1) | copy-start | bytes 24580

commit v13 on v12

--- a/solution.py
+++ b/solution.py
@@ -195,9 +195,10 @@
     square = hidden * hidden
     tanh = jnp.tanh(hidden * (GELU_A + (GELU_A * GELU_B) * square))
     half = 0.5 + 0.5 * tanh
-    active = (hidden * half).astype(BF16)
-    rise = 0.5 * GELU_A + (1.5 * GELU_A * GELU_B) * square
-    slope = half + hidden * (1.0 - tanh * tanh) * rise
+    product = hidden * half
+    active = product.astype(BF16)
+    rise = 2.0 * GELU_A + (6.0 * GELU_A * GELU_B) * square
+    slope = half * (1.0 + (hidden - product) * rise)
     predicted = dot(proj, active, NN)
     wide_lines = lines.astype(F32)
     target = pltpu.roll(wide_lines, 5, 0) + neighbour_terms(wide_lines, rows)

time: 75.5 us -> 75.5 us (level)
  no operation moved by 1% of the time
where the time goes in v13:
time: 75.5 us; the launch traced here: 75.1 us
  blocking collectives  61.7 us (82%)
  Pallas kernels  6 us (8%)
  starting transfers between devices  5.29 us (7%)
  local copies, waits for them, and re-layouts  1.34 us (2%)
    all_to_all x1, blocking collectives, local(): lax.all_to_all(send, 'gx', split_axis=0, concat_axis=0, tiled=True)  18.6 us
    all_gather x1, blocking collectives, local(): fields = lax.all_gather(slot_field, 'grp', axis=0, tiled=True)  16.4 us
    all_to_all x1, blocking collectives, local(): lax.all_to_all(send, ('grp', 'gy'), split_axis=0, concat_axis=0, tiled=True)  13.4 us
    all_to_all x1, blocking collectives, local(): recv = lax.all_to_all(send, 'gx', split_axis=0, concat_axis=0, tiled=True)  13.3 us
    pallas_call x6, Pallas kernels, call(): pl.pallas_call(kernel, out_shape=out_shape, in_specs=[VMEM] * len(args),...  6 us
    ppermute x1, starting transfers between devices, local(): edge = lax.ppermute(edge, ('grp', 'gy'), pairs)  5.29 us
  transfers between devices with their start and end apart: 1, of which 0 were waited for; matrix products, arithmetic and copies ran while one was open for 0% of the time, Pallas kernels for 2%

profile of v13, /device:TPU:1, one launch (start us, length us, event | category | flops | bytes accessed | tf_op | source)
XLA Modules:
  0.0 75.1 jit_solution(2509542806655753383)
XLA Ops:
  0.6 0.0 copy-start.1
  0.6 16.4 %all_gather.3.fields_ref = f32[4,2,48,128]{3,2,1,0:T(8,128)S(1)} all-gather(f32[1,2,48,128]{3,2,1,0:T(8,128)} %param.7), channel_id=1, replica_groups=mesh['grp'=4,'gx'=32,'gy'=4] {'grp'}, dimensions={0}, use_global_device_ids=true | all-gather | bytes 245760 | tf_op jit(solution)/shard_map/all_gather | solution.py:362
  17.1 0.0 copy-done.1
  17.1 0.0 copy-start.2
  17.1 0.2 shard_map.94
  17.3 5.3 %collective-permute-start = (f32[8,128]{1,0:T(8,128)S(1)}, f32[8,128]{1,0:T(8,128)S(1)}, u32[]{:S(2)}, u32[]{:S(2)}) collective-permute-start(f32[8,128]{1,0:T(8,128)S(1)} %shard_map.94), channel_id=1, source_target_pairs={{1,0},{2,1},{3,2},{256,3},{129,128},{130,129},{131,130},{384,131},... | collective-permute-start | bytes 12296 | tf_op jit(solution)/shard_map/ppermute | solution.py:369
  22.6 0.0 copy-start.5
  22.6 0.0 copy-start.6
  22.6 0.6 copy-done.5
  23.2 0.0 copy-done.6
  23.3 0.0 copy-start.4
  23.3 0.0 copy-done.2
  23.3 0.6 copy-done.4
  23.9 1.2 %shard_map.95 = (bf16[128,4096]{1,0:T(8,128)(2,1)S(1)}, bf16[4096,128]{1,0:T(8,128)(2,1)S(1)}, f32[8,128]{1,0:T(8,128)S(1)}, bf16[256,1024]{1,0:T(8,128)(2,1)S(1)}) custom-call(s32[1,32]{1,0:T(1,128)S(1)} %bitcast.4, f32[2,48,128]{2,1,0:T(8,128)S(1)} %bitcast.3), custom_call_target="tpu_custom_call" | custom-call | tf_op jit(solution)/shard_map/pallas_call | solution.py:32
  25.2 0.0 collective-permute-done.edge_ref
  25.2 0.0 copy-start
  25.2 0.6 shard_map.96
  25.8 0.0 copy-start.3
  25.8 18.6 %all_to_all.15.refs_0_.lines_ref = bf16[32,16,128]{2,1,0:T(8,128)(2,1)S(1)} all-to-all(bf16[32,16,128]{2,1,0:T(8,128)(2,1)S(1)} %shard_map.96), channel_id=1, replica_groups=mesh['grp'=4,'gx'=32,'gy'=4] {'gx'}, dimensions={0} | all-to-all | bytes 262144 | tf_op jit(solution)/shard_map/all_to_all | solution.py:393
  44.4 0.0 copy-done
  44.4 0.0 copy-done.3
  44.4 2.6 %shard_map.97 = bf16[32,16,128]{2,1,0:T(8,128)(2,1)S(1)} custom-call(bf16[32,16,128]{2,1,0:T(8,128)(2,1)S(1)} %all_to_all.15.refs_0_.lines_ref, bf16[128,4096]{1,0:T(8,128)(2,1)S(1)} %get-tuple-element.22.refs_1_, bf16[4096,128]{1,0:T(8,128)(2,1)S(1)} %get-tuple-element.23.refs_2_, bf16[16,64]{1,0:T(8,128)(2,1)S(1)} %pad_maximum_fusion.refs_3_.small_ref, ...), custom_call_target="tpu_custom_call" | custom-call | tf_op jit(solution)/shard_map/pallas_call | solution.py:32
  47.0 13.3 %all_to_all.16.recv_ref = bf16[32,16,128]{2,1,0:T(8,128)(2,1)S(1)} all-to-all(bf16[32,16,128]{2,1,0:T(8,128)(2,1)S(1)} %shard_map.97), channel_id=1, replica_groups=mesh['grp'=4,'gx'=32,'gy'=4] {'gx'}, dimensions={0} | all-to-all | bytes 262144 | tf_op jit(solution)/shard_map/all_to_all | solution.py:405
  60.3 0.4 shard_map.98
  60.7 13.4 %all_to_all.17.recv_ref = f32[16,8,128]{2,1,0:T(8,128)S(1)} all-to-all(f32[16,8,128]{2,1,0:T(8,128)S(1)} %shard_map.98), channel_id=1, replica_groups=mesh['grp'=4,'gx'=32,'gy'=4] {'grp','gy'}, dimensions={0} | all-to-all | bytes 131072 | tf_op jit(solution)/shard_map/all_to_all | solution.py:413
  74.0 1.1 %shard_map.99 = (f32[4,128]{1,0:T(4,128)}, f32[64,64]{1,0:T(8,128)}, f32[3,2,48,128]{3,2,1,0:T(8,128)}) custom-call(f32[16,8,128]{2,1,0:T(8,128)S(1)} %all_to_all.17.recv_ref, bf16[16,64]{1,0:T(8,128)(2,1)S(1)} %pad_maximum_fusion.refs_3_.small_ref, f32[4,2,48,128]{3,2,1,0:T(8,128)S(1)} %all_gather.3.fields_ref, s32[2,48,128]{2,1,0:T(8,128)S(1)} %copy-done.1, ...), custom_call_target="tpu_custom_call" | custom-call | tf_op jit(solution)/shard_map/pallas_call | solution.py:32
  (2 shorter events, 0.0 us)
Async XLA Ops:
  0.6 16.5 %copy-start.1 = (s32[2,48,128]{2,1,0:T(8,128)S(1)}, s32[2,48,128]{2,1,0:T(8,128)}, u32[]{:S(2)}) copy-start(s32[2,48,128]{2,1,0:T(8,128)} %solid_ref.5) | copy-start | bytes 147460
  17.1 6.2 %copy-start.2 = (f32[1,2,48,128]{3,2,1,0:T(8,128)S(1)}, f32[1,2,48,128]{3,2,1,0:T(8,128)}, u32[]{:S(2)}) copy-start(f32[1,2,48,128]{3,2,1,0:T(8,128)} %param.7) | copy-start | bytes 147460
  17.3 7.9 %collective-permute-start = (f32[8,128]{1,0:T(8,128)S(1)}, f32[8,128]{1,0:T(8,128)S(1)}, u32[]{:S(2)}, u32[]{:S(2)}) collective-permute-start(f32[8,128]{1,0:T(8,128)S(1)} %shard_map.94), channel_id=1, source_target_pairs={{1,0},{2,1},{3,2},{256,3},{129,128},{130,129},{131,130},{384,131},... | collective-permute-start | bytes 12296 | tf_op jit(solution)/shard_map/ppermute | solution.py:369
  22.6 0.7 copy-start.5
  22.6 0.7 copy-start.6
  23.3 0.7 copy-start.4
  25.2 19.3 %copy-start = (bf16[2048,128]{1,0:T(8,128)(2,1)S(1)}, bf16[2048,128]{1,0:T(8,128)(2,1)}, u32[]{:S(2)}) copy-start(bf16[2048,128]{1,0:T(8,128)(2,1)} %refs_5_.1) | copy-start | bytes 1572868
  25.8 18.7 %copy-start.3 = (bf16[64,64]{1,0:T(8,128)(2,1)S(1)}, bf16[64,64]{1,0:T(8,128)(2,1)}, u32[]{:S(2)}) copy-start(bf16[64,64]{1,0:T(8,128)(2,1)} %refs_4_.1) | copy-start | bytes 24580
